TPU v7x, 128 devices: a whole 4x4x4 slice. The times are simulated.
128 devices in a mesh: wide: 64 (over x, y, z), narrow: 2 (over core).
Axes of the slice: x: 4, y: 4, z: 4, core: 2. Of those that a mesh axis runs over, the one named last changes fastest.
Arguments:
- user_emb: float32 [256, 512, 256], P('wide'), may hold values from -0.75 to 0.75
- item_emb: float32 [128, 512, 256], P('wide', 'narrow'), may hold values from -0.75 to 0.75
- pairs: int32 [64, 64, 3], P('wide'), may hold values from 0 to 255, as said below
- counts: int32 [64], P('wide'), may hold values from 57 to 64
- natural_exponent_param: float32 [1], replicated, may hold values from 1.5 to 2.5
- additive_shift_param: float32 [1], replicated, may hold values from -3 to -1
Outputs:
- user_grad: float32 [256, 512, 256], P('wide')
- item_grad: float32 [128, 512, 256], P('wide', 'narrow')
- objective_summary_vector: float32 [3], replicated
Inputs may be any that keep to these rules, and one draw needn't show every extreme that they name: `pairs`: row w lists slots (user block, item block, label): the user block lies in w * 4 to (w + 1) * 4 - 1; over the 64 slots of one row, item block // 2 takes every value 0 to 63 exactly once; label 1 is a positive pair, 0 a hard negative; slots at or past counts[w] are ignored.
All inputs are finite; a program needn't handle non-finite values.
Results may differ from a plain program's by a relative error of at most 0.0032.
Values may be sent and summed in bfloat16 or wider, within the bound.
No kernel may reach another device: no remote copies, remote signals or barrier semaphores. Data moves between devices by JAX's collectives and lax.ppermute only.
A program may use at most 128 MiB of HBM per device.

v0:
```python
import jax
import jax.numpy as jnp
from jax import lax
from jax.sharding import PartitionSpec as P

group_size = 8


def score_block_group(
    user_block_rows,
    item_block_rows,
    pair_labels,
    active_flag,
    sharpness_multiplier,
    present_shift,
    logistic_weight,
    diagonal_flag,
):
    similarity_dot = jnp.einsum(
        "gre,gce->grc", user_block_rows, item_block_rows, preferred_element_type=jnp.float32
    )
    couple_affinities = sharpness_multiplier * similarity_dot + present_shift
    target = jnp.where(
        (pair_labels == 1)[:, None, None] & diagonal_flag[None, :, :], 1.0, -1.0
    ).astype(jnp.float32)
    margin = -target * couple_affinities
    live_mask = active_flag[:, None, None]
    loss_sum = jnp.sum(jnp.where(live_mask, jax.nn.softplus(margin), 0.0))
    weight = jnp.where(live_mask, -target * jax.nn.sigmoid(margin), 0.0)
    scale_sum = jnp.sum(weight * similarity_dot)
    bias_sum = jnp.sum(weight)
    scaled = (weight * logistic_weight).astype(jnp.bfloat16)
    user_parts = jnp.einsum(
        "grc,gce->gre", scaled, item_block_rows, preferred_element_type=jnp.float32
    ).astype(jnp.bfloat16)
    item_parts = jnp.einsum(
        "grc,gre->gce", scaled, user_block_rows, preferred_element_type=jnp.float32
    ).astype(jnp.bfloat16)
    return (user_parts, item_parts, loss_sum, scale_sum, bias_sum)


def body(user_emb, item_emb, pairs, counts, natural_exponent_param, additive_shift_param):
    wide_count = lax.axis_size("wide")
    wide_index = lax.axis_index("wide")
    narrow_count = lax.axis_size("narrow")
    narrow_index = lax.axis_index("narrow")
    user_blocks, tile_height_value, width = user_emb.shape
    item_blocks, half_rows, unused_width = item_emb.shape
    slot_count = pairs.shape[1]
    own_pairs = pairs[0]
    live_count = counts[0]
    slot_ids = jnp.arange(slot_count)
    owner_ids = jnp.arange(wide_count)
    hitting = (own_pairs[None, :, 1] // item_blocks == owner_ids[:, None]) & (
        slot_ids < live_count
    )[None, :]
    request = jnp.stack(
        [
            jnp.any(hitting, axis=1).astype(jnp.int32),
            jnp.sum(jnp.where(hitting, own_pairs[None, :, 1] % item_blocks, 0), axis=1),
            jnp.sum(jnp.where(hitting, own_pairs[None, :, 2], 0), axis=1),
        ],
        axis=1,
    )
    answer = lax.all_to_all(request, "wide", split_axis=0, concat_axis=0, tiled=True)
    wanted = answer[:, 0] == 1
    wanted_block = answer[:, 1]
    items_low = item_emb.astype(jnp.bfloat16)
    users_low = user_emb.astype(jnp.bfloat16)
    sharpness_multiplier = jnp.exp(natural_exponent_param[0])
    present_shift = additive_shift_param[0]
    logistic_weight = sharpness_multiplier * tile_height_value ** (-0.5)
    row_ids = jnp.arange(tile_height_value)[:, None]
    col_ids = narrow_index * half_rows + jnp.arange(half_rows)[None, :]
    diagonal_flag = row_ids == col_ids
    group_ids = jnp.arange(group_size)
    block_ids = jnp.arange(item_blocks)
    user_ids = jnp.arange(user_blocks)
    zero = jnp.zeros((), jnp.float32)
    select = ((wanted_block[:, None] == block_ids[None, :]) & wanted[:, None]).astype(jnp.bfloat16)
    outgoing = jnp.einsum(
        "ri,ihe->rhe", select, items_low, preferred_element_type=jnp.float32
    ).astype(jnp.bfloat16)
    fetched = lax.all_to_all(outgoing, "wide", split_axis=0, concat_axis=0, tiled=True)

    def visit_group(group, state_now):
        user_acc, returned, objective_accum, multiplier_derivative_accum, shift_derivative_accum = (
            state_now
        )
        slots = group * group_size + group_ids
        embedding_rows = jnp.take(own_pairs, slots, axis=0)
        active_flag = slots < live_count
        local_user = jnp.clip(embedding_rows[:, 0] - wide_index * user_blocks, 0, user_blocks - 1)
        owner = embedding_rows[:, 1] // item_blocks
        user_block_rows = jnp.take(users_low, local_user, axis=0)
        item_block_rows = jnp.take(fetched, owner, axis=0)
        user_parts, item_parts, loss_sum, scale_sum, bias_sum = score_block_group(
            user_block_rows,
            item_block_rows,
            embedding_rows[:, 2],
            active_flag,
            sharpness_multiplier,
            present_shift,
            logistic_weight,
            diagonal_flag,
        )
        spread = ((local_user[:, None] == user_ids[None, :]) & active_flag[:, None]).astype(
            jnp.bfloat16
        )
        user_acc = user_acc + jnp.einsum(
            "gu,gre->ure", spread, user_parts, preferred_element_type=jnp.float32
        )
        returned = returned.at[owner].set(item_parts)
        return (
            user_acc,
            returned,
            objective_accum + loss_sum,
            multiplier_derivative_accum + scale_sum,
            shift_derivative_accum + bias_sum,
        )

    turns = (live_count + group_size - 1) // group_size
    initial = (
        jnp.zeros(user_emb.shape, jnp.float32),
        jnp.zeros(fetched.shape, jnp.bfloat16),
        zero,
        zero,
        zero,
    )
    user_acc, returned, objective_accum, multiplier_derivative_accum, shift_derivative_accum = (
        lax.fori_loop(0, turns, visit_group, initial)
    )
    returned_parts = lax.all_to_all(returned, "wide", split_axis=0, concat_axis=0, tiled=True)
    item_grad = jnp.einsum(
        "ri,rhe->ihe", select, returned_parts, preferred_element_type=jnp.float32
    )
    user_grad = lax.psum(user_acc, "narrow")
    collapsed_result = lax.psum(
        (
            objective_accum,
            multiplier_derivative_accum,
            shift_derivative_accum,
            live_count.astype(jnp.float32) / narrow_count,
        ),
        ("wide", "narrow"),
    )
    couple_normalizer = tile_height_value * tile_height_value * collapsed_result[3]
    objective_summary_vector = jnp.stack(
        [
            collapsed_result[0] / couple_normalizer,
            sharpness_multiplier * collapsed_result[1] / couple_normalizer,
            collapsed_result[2] / couple_normalizer,
        ]
    )
    return (user_grad, item_grad, objective_summary_vector)


def solution(mesh):
    placed = (
        P("wide", None, None),
        P("wide", "narrow", None),
        P("wide", None, None),
        P("wide"),
        P(),
        P(),
    )
    return jax.shard_map(
        body,
        mesh=mesh,
        in_specs=placed,
        out_specs=(P("wide", None, None), P("wide", "narrow", None), P()),
        check_vma=False,
    )
```

profile of v0, /device:TPU:0, one launch (start us, length us, event | category | flops | bytes accessed | tf_op | source)
XLA Modules:
  0.0 651.7 jit_solution(7807883971144680613)
XLA Ops:
  9.8 11.5 %all-to-all-start = ((s32[64,1,3]{2,1,0:T(1,128)}), s32[64,1,3]{2,1,0:T(1,128)S(1)}, u32[]{:S(2)}, u32[]{:S(2)}) async-start(s32[64,1,3]{2,1,0:T(1,128)} %copy.59), calls=%async_computation | async-start | bytes 65536 | tf_op jit(solution)/shard_map/all_to_all | solution.py:65
  21.3 1.1 convert_element_type.48
  22.4 8.4 %all-to-all-done = s32[64,1,3]{2,1,0:T(1,128)S(1)} async-done(((s32[64,1,3]{2,1,0:T(1,128)}), s32[64,1,3]{2,1,0:T(1,128)S(1)}, u32[]{:S(2)}, u32[]{:S(2)}) %all-to-all-start) | async-done | bytes 800 | tf_op jit(solution)/shard_map/all_to_all | solution.py:65
  31.0 5.6 convolution_convert_fusion.2
  36.7 11.4 %copy.61 = bf16[64,256,256]{2,1,0:T(8,128)(2,1)} copy(bf16[64,256,256]{2,0,1:T(8,128)(2,1)} %convolution_convert_fusion.2) | data formatting | bytes 16777216 | tf_op jit(solution)/shard_map/convert_element_type | solution.py:83
  48.0 5.9 all-to-all-start.1
  54.8 114.5 %all-to-all-done.1 = bf16[64,256,256]{2,1,0:T(8,128)(2,1)} async-done(((bf16[64,256,256]{2,1,0:T(8,128)(2,1)}), bf16[64,256,256]{2,1,0:T(8,128)(2,1)}, u32[]{:S(2)}, u32[]{:S(2)}) %all-to-all-start.1) | async-done | bytes 8388640 | tf_op jit(solution)/shard_map/all_to_all | solution.py:84
  169.3 1.6 broadcast_in_dim.117
  170.9 4.2 broadcast_in_dim.118
  175.1 268.9 %while.21 = (s32[]{:T(128)}, f32[4,512,256]{2,0,1:T(4,128)}, bf16[64,256,256]{2,1,0:T(8,128)(2,1)}, f32[]{:T(128)}, f32[]{:T(128)}, /*index=5*/f32[]{:T(128)}, s...) while((s32[]{:T(128)}, f32[4,512,256]{2,0,1:T(4,128)}, ...), condition=%wide.region_8.9_spmd.clone, body=%wide.region_3.8_spmd.clone.sunk | while | flops 1666190848 | bytes 71973368 | solution.py:131
  177.2 5.0 gather_fusion.1
  182.8 3.8 fusion.56
  186.7 7.6 %fusion.57 = (f32[]{:T(128)}, f32[]{:T(128)}, f32[]{:T(128)}, f32[8,512,256]{2,1,0:T(8,128)}) fusion(f32[8,512,256]{2,1,0:T(8,128)S(1)} %get-tuple-element.498, f32[]{:T(128)} %get-tuple-element.555, f32[]{:T(128)} %get-tuple-element.552, pred[512,256]{1,0:T(8,128)(4,1)S(1)} %iota_compare_fusion.5, pred[8]{0:T(512)(128)(4,1)S(1)} %get-tuple-element.493, ...), kind=kLoop, calls=%fused_computation.92.clone.1 | loop fusion | flops 26214396 | bytes 8650788 | tf_op jit(solution)/shard_map/while/body/reduce_sum | solution.py:31
  196.1 4.3 convolution_convert_fusion.6
  201.2 4.6 fusion.58
  205.9 2.9 scatter_fusion
  210.8 5.0 gather_fusion.1
  216.4 3.8 fusion.56
  220.3 7.6 %fusion.57 = (f32[]{:T(128)}, f32[]{:T(128)}, f32[]{:T(128)}, f32[8,512,256]{2,1,0:T(8,128)}) fusion(f32[8,512,256]{2,1,0:T(8,128)S(1)} %get-tuple-element.498, f32[]{:T(128)} %get-tuple-element.555, f32[]{:T(128)} %get-tuple-element.552, pred[512,256]{1,0:T(8,128)(4,1)S(1)} %iota_compare_fusion.5, pred[8]{0:T(512)(128)(4,1)S(1)} %get-tuple-element.493, ...), kind=kLoop, calls=%fused_computation.92.clone.1 | loop fusion | flops 26214396 | bytes 8650788 | tf_op jit(solution)/shard_map/while/body/reduce_sum | solution.py:31
  229.7 4.3 convolution_convert_fusion.6
  234.8 4.6 fusion.58
  239.4 2.9 scatter_fusion
  244.4 5.0 gather_fusion.1
  250.0 3.8 fusion.56
  253.9 7.6 %fusion.57 = (f32[]{:T(128)}, f32[]{:T(128)}, f32[]{:T(128)}, f32[8,512,256]{2,1,0:T(8,128)}) fusion(f32[8,512,256]{2,1,0:T(8,128)S(1)} %get-tuple-element.498, f32[]{:T(128)} %get-tuple-element.555, f32[]{:T(128)} %get-tuple-element.552, pred[512,256]{1,0:T(8,128)(4,1)S(1)} %iota_compare_fusion.5, pred[8]{0:T(512)(128)(4,1)S(1)} %get-tuple-element.493, ...), kind=kLoop, calls=%fused_computation.92.clone.1 | loop fusion | flops 26214396 | bytes 8650788 | tf_op jit(solution)/shard_map/while/body/reduce_sum | solution.py:31
  263.3 4.3 convolution_convert_fusion.6
  268.4 4.6 fusion.58
  273.1 2.9 scatter_fusion
  278.0 5.0 gather_fusion.1
  283.6 3.8 fusion.56
  287.5 7.6 %fusion.57 = (f32[]{:T(128)}, f32[]{:T(128)}, f32[]{:T(128)}, f32[8,512,256]{2,1,0:T(8,128)}) fusion(f32[8,512,256]{2,1,0:T(8,128)S(1)} %get-tuple-element.498, f32[]{:T(128)} %get-tuple-element.555, f32[]{:T(128)} %get-tuple-element.552, pred[512,256]{1,0:T(8,128)(4,1)S(1)} %iota_compare_fusion.5, pred[8]{0:T(512)(128)(4,1)S(1)} %get-tuple-element.493, ...), kind=kLoop, calls=%fused_computation.92.clone.1 | loop fusion | flops 26214396 | bytes 8650788 | tf_op jit(solution)/shard_map/while/body/reduce_sum | solution.py:31
  296.9 4.3 convolution_convert_fusion.6
  302.0 4.6 fusion.58
  306.7 2.9 scatter_fusion
  311.6 5.0 gather_fusion.1
  317.2 3.8 fusion.56
  321.1 7.6 %fusion.57 = (f32[]{:T(128)}, f32[]{:T(128)}, f32[]{:T(128)}, f32[8,512,256]{2,1,0:T(8,128)}) fusion(f32[8,512,256]{2,1,0:T(8,128)S(1)} %get-tuple-element.498, f32[]{:T(128)} %get-tuple-element.555, f32[]{:T(128)} %get-tuple-element.552, pred[512,256]{1,0:T(8,128)(4,1)S(1)} %iota_compare_fusion.5, pred[8]{0:T(512)(128)(4,1)S(1)} %get-tuple-element.493, ...), kind=kLoop, calls=%fused_computation.92.clone.1 | loop fusion | flops 26214396 | bytes 8650788 | tf_op jit(solution)/shard_map/while/body/reduce_sum | solution.py:31
  330.5 4.3 convolution_convert_fusion.6
  335.7 4.6 fusion.58
  340.3 2.9 scatter_fusion
  345.2 5.0 gather_fusion.1
  350.9 3.8 fusion.56
  354.7 7.6 %fusion.57 = (f32[]{:T(128)}, f32[]{:T(128)}, f32[]{:T(128)}, f32[8,512,256]{2,1,0:T(8,128)}) fusion(f32[8,512,256]{2,1,0:T(8,128)S(1)} %get-tuple-element.498, f32[]{:T(128)} %get-tuple-element.555, f32[]{:T(128)} %get-tuple-element.552, pred[512,256]{1,0:T(8,128)(4,1)S(1)} %iota_compare_fusion.5, pred[8]{0:T(512)(128)(4,1)S(1)} %get-tuple-element.493, ...), kind=kLoop, calls=%fused_computation.92.clone.1 | loop fusion | flops 26214396 | bytes 8650788 | tf_op jit(solution)/shard_map/while/body/reduce_sum | solution.py:31
  364.2 4.3 convolution_convert_fusion.6
  369.3 4.6 fusion.58
  373.9 2.9 scatter_fusion
  378.8 5.0 gather_fusion.1
  384.5 3.8 fusion.56
  388.3 7.6 %fusion.57 = (f32[]{:T(128)}, f32[]{:T(128)}, f32[]{:T(128)}, f32[8,512,256]{2,1,0:T(8,128)}) fusion(f32[8,512,256]{2,1,0:T(8,128)S(1)} %get-tuple-element.498, f32[]{:T(128)} %get-tuple-element.555, f32[]{:T(128)} %get-tuple-element.552, pred[512,256]{1,0:T(8,128)(4,1)S(1)} %iota_compare_fusion.5, pred[8]{0:T(512)(128)(4,1)S(1)} %get-tuple-element.493, ...), kind=kLoop, calls=%fused_computation.92.clone.1 | loop fusion | flops 26214396 | bytes 8650788 | tf_op jit(solution)/shard_map/while/body/reduce_sum | solution.py:31
  397.8 4.3 convolution_convert_fusion.6
  402.9 4.6 fusion.58
  407.5 2.9 scatter_fusion
  412.5 5.0 gather_fusion.1
  418.1 3.8 fusion.56
  422.0 7.6 %fusion.57 = (f32[]{:T(128)}, f32[]{:T(128)}, f32[]{:T(128)}, f32[8,512,256]{2,1,0:T(8,128)}) fusion(f32[8,512,256]{2,1,0:T(8,128)S(1)} %get-tuple-element.498, f32[]{:T(128)} %get-tuple-element.555, f32[]{:T(128)} %get-tuple-element.552, pred[512,256]{1,0:T(8,128)(4,1)S(1)} %iota_compare_fusion.5, pred[8]{0:T(512)(128)(4,1)S(1)} %get-tuple-element.493, ...), kind=kLoop, calls=%fused_computation.92.clone.1 | loop fusion | flops 26214396 | bytes 8650788 | tf_op jit(solution)/shard_map/while/body/reduce_sum | solution.py:31
  431.4 4.3 convolution_convert_fusion.6
  436.6 4.6 fusion.58
  441.2 2.9 scatter_fusion
  444.0 11.4 %all-to-all-start.2 = ((bf16[64,256,256]{2,1,0:T(8,128)(2,1)}), bf16[64,256,256]{2,1,0:T(8,128)(2,1)}, u32[]{:S(2)}, u32[]{:S(2)}) async-start(bf16[64,256,256]{2,1,0:T(8,128)(2,1)} %get-tuple-element.235), calls=%async_computation.2 | async-start | bytes 16777216 | tf_op jit(solution)/shard_map/all_to_all | solution.py:133
  455.5 3.3 copy.62
  458.8 170.9 %all-reduce = (f32[]{:T(128)}, f32[]{:T(128)}, f32[]{:T(128)}, f32[]{:T(128)}) all-reduce(f32[]{:T(128)} %get-tuple-element.238, f32[]{:T(128)S(6)} %div.52, f32[]{:T(128)} %get-tuple-element.237, f32[]{:T(128)} %get-tuple-element.236), channel_id=1, replica_groups=mesh['wide'=64,'narrow'=2] {'wide','narrow'}, use_global_device_ids=true, to_apply=%region_13.14 | all-reduce | flops 4 | bytes 32 | tf_op jit(solution)/shard_map/psum | solution.py:138
  633.0 8.0 %fusion.30 = f32[2,256,256]{2,0,1:T(2,128)S(1)} fusion(bf16[64,256,256]{2,1,0:T(8,128)(2,1)} %all-to-all-done.2, pred[64]{0:T(512)(128)(4,1)S(1)} %fusion.35, s32[64]{0:T(128)S(1)} %slice_reduce_fusion), kind=kOutput, calls=%fused_computation.61 | convolution fusion | flops 16777472 | bytes 8913216 | tf_op jit(solution)/shard_map/ri,rhe->ihe/dot_general | solution.py:134
  640.9 0.8 copy.64
  641.8 3.0 copy.104
  (180 shorter events, 30.9 us)
Async XLA Ops:
  9.8 21.0 %all-to-all-start = ((s32[64,1,3]{2,1,0:T(1,128)}), s32[64,1,3]{2,1,0:T(1,128)S(1)}, u32[]{:S(2)}, u32[]{:S(2)}) async-start(s32[64,1,3]{2,1,0:T(1,128)} %copy.59), calls=%async_computation | async-start | bytes 65536 | tf_op jit(solution)/shard_map/all_to_all | solution.py:65
  48.0 6.6 %copy-start.3 = (f32[4,512,256]{2,1,0:T(8,128)S(1)}, f32[4,512,256]{2,1,0:T(8,128)}, u32[]{:S(2)}) copy-start(f32[4,512,256]{2,1,0:T(8,128)} %param.8) | copy-start | bytes 6291460
  48.0 121.3 %all-to-all-start.1 = ((bf16[64,256,256]{2,1,0:T(8,128)(2,1)}), bf16[64,256,256]{2,1,0:T(8,128)(2,1)}, u32[]{:S(2)}, u32[]{:S(2)}) async-start(bf16[64,256,256]{2,1,0:T(8,128)(2,1)} %copy.61), calls=%async_computation.1 | async-start | bytes 16777216 | tf_op jit(solution)/shard_map/all_to_all | solution.py:84
  196.1 4.3 copy-start
  196.1 4.3 copy-start.1
  201.2 4.6 copy-start.2
  229.7 4.3 copy-start
  229.7 4.3 copy-start.1
  234.8 4.6 copy-start.2
  263.3 4.3 copy-start
  263.3 4.3 copy-start.1
  268.4 4.6 copy-start.2
  296.9 4.3 copy-start
  296.9 4.3 copy-start.1
  302.0 4.6 copy-start.2
  330.5 4.3 copy-start
  330.5 4.3 copy-start.1
  335.6 4.6 copy-start.2
  364.1 4.3 copy-start
  364.2 4.3 copy-start.1
  369.3 4.6 copy-start.2
  397.8 4.3 copy-start
  397.8 4.3 copy-start.1
  402.9 4.6 copy-start.2
  431.4 4.3 copy-start
  431.4 4.3 copy-start.1
  436.5 4.6 copy-start.2
  444.0 188.9 %all-to-all-start.2 = ((bf16[64,256,256]{2,1,0:T(8,128)(2,1)}), bf16[64,256,256]{2,1,0:T(8,128)(2,1)}, u32[]{:S(2)}, u32[]{:S(2)}) async-start(bf16[64,256,256]{2,1,0:T(8,128)(2,1)} %get-tuple-element.235), calls=%async_computation.2 | async-start | bytes 16777216 | tf_op jit(solution)/shard_map/all_to_all | solution.py:133
  455.5 186.3 %all-reduce.3.cloned.1.call-start = ((), (), s32[]{:S(2)}) async-start(), calls=%async_computation.3 | async-start | bytes 4194304 | tf_op jit(solution)/shard_map/psum | solution.py:137
Sparse Core Ops, SparseCore 0:
  458.9 27.9 all-reduce.2
where the time goes:
time: 654 us; the launch traced here: 652 us
  blocking collectives  171 us (26%)
  waiting for transfers between devices  123 us (19%)
  matrix products  122 us (19%)
  local copies, waits for them, and re-layouts  99.7 us (15%)
  other arithmetic  73.9 us (11%)
  starting transfers between devices  28.8 us (4%)
  between operations  18.2 us (3%)
  loops' own time  15.4 us (2%)
    psum x1, blocking collectives, body(): lax.psum((objective_accum, multiplier_derivative_accum, shift_derivative_...  171 us
    all_to_all x1, waiting for transfers between devices, body(): lax.all_to_all(outgoing, 'wide', split_axis=0, concat_axis=0, tiled=True)  115 us
    reduce_sum x8, other arithmetic, score_block_group(): bias_sum = jnp.sum(weight)  60.8 us
    gather x8, local copies, waits for them, and re-layouts, visit_group(): item_block_rows = jnp.take(fetched, owner, axis=0)  39.8 us
    dot_general x8, matrix products, visit_group(): jnp.einsum('gu,gre->ure', spread, user_parts, preferred_element_type=jnp....  36.9 us
    dot_general x8, matrix products, score_block_group(): jnp.einsum('grc,gre->gce', scaled, user_block_rows, preferred_element_typ...  34.4 us
    dot_general x8, matrix products, score_block_group(): jnp.einsum('gre,gce->grc', user_block_rows, item_block_rows, preferred_el...  30.6 us
    scatter x8, local copies, waits for them, and re-layouts, visit_group(): returned = returned.at[owner].set(item_parts)  23.1 us
  transfers between devices with their start and end apart: 4, of which 2 were waited for; matrix products, arithmetic and copies ran while one was open for 2% of the time, Pallas kernels for 0%

commit v1 on v0

v1 whole, which is shorter than its diff:
```python
import functools

import jax
import jax.numpy as jnp
from jax import lax
from jax.experimental import pallas as pl
from jax.experimental.pallas import tpu as pltpu
from jax.sharding import Mesh
from jax.sharding import PartitionSpec as P

LOG2E = 1.4426950408889634
RING = 4
NT = (((1,), (1,)), ((), ()))
NN = (((1,), (0,)), ((), ()))
TN = (((0,), (0,)), ((), ()))
WIDE = ("x", "y", "z")
BF = jnp.bfloat16
F32 = jnp.float32


def score_kernel(
    place, table, scalars, own_users, near_users, far_users, items_in,
    user_keep, user_give, item_keep, item_give, sums,
    users, items, uacc, iacc, ugive, igive, eye, jobs, in_sem, out_sem,
):
    my_x, my_y, my_z, core = place[0], place[1], place[2], place[3]
    blocks, height, width = own_users.shape
    half = height // 2
    mine = pl.multiple_of(core * half, half)
    other = pl.multiple_of((1 - core) * half, half)
    copies = [
        pltpu.make_async_copy(items_in, items, in_sem.at[0]),
        pltpu.make_async_copy(own_users, users.at[pl.ds(0, blocks)], in_sem.at[1]),
    ]
    for d in range(1, RING):
        rows = pl.ds(d * blocks, blocks)
        copies.append(pltpu.make_async_copy(
            near_users.at[pl.ds((d - 1) * blocks, blocks)],
            users.at[rows, pl.ds(mine, half), :], in_sem.at[2 * d]))
        copies.append(pltpu.make_async_copy(
            far_users.at[pl.ds((d - 1) * blocks, blocks)],
            users.at[rows, pl.ds(other, half), :], in_sem.at[2 * d + 1]))
    for c in copies:
        c.start()

    slots = 64

    def list_slot(i, count):
        d = i // slots
        slot = i % slots
        user, item, label = table[i * 3], table[i * 3 + 1], table[i * 3 + 2]
        owner = item // 2
        dx = (my_x - owner // 16) & 3
        dy = (my_y - (owner // 4) % 4) & 3
        first = jnp.where(core == 0, dy, dx)
        second = jnp.where(core == 0, dx, dy)
        jobs[count] = d * blocks + (user & (blocks - 1))
        jobs[count + 72] = (second * RING + first) * 2 + (item & 1)
        jobs[count + 144] = label
        live = (owner % 4 == my_z) & (slot < table[RING * slots * 3 + d])
        return count + live.astype(jnp.int32)

    count = lax.fori_loop(0, RING * slots, list_slot, jnp.int32(0), unroll=4)
    jobs[count] = 0
    jobs[count + 72] = 0
    jobs[count + 144] = 0

    uacc[...] = jnp.zeros_like(uacc)
    iacc[...] = jnp.zeros_like(iacc)
    row = lax.broadcasted_iota(jnp.int32, (128, 128), 0)
    col = lax.broadcasted_iota(jnp.int32, (128, 128), 1)
    eye[...] = (row == col).astype(F32)
    for c in copies:
        c.wait()

    slope, shift, gain = scalars[0], scalars[1], scalars[2]

    def tile(u, it, slope_j, shift_j, label_j):
        inner = lax.dot_general(u, it, NT, preferred_element_type=F32)
        x = inner * slope_j + shift_j
        e = jnp.exp2(-jnp.abs(x))
        t = 1.0 + e
        high = x >= 0.0
        num = jnp.where(high, 1.0, e)
        soft = jnp.maximum(x, 0.0)
        if label_j is not None:
            hit = eye[...] * label_j > 0.5
            nums, softs = [], []
            for q in range(2):
                r = slice(q * 128, (q + 1) * 128)
                xb, eb = x[r, r], e[r, r]
                nb = jnp.where(hit, jnp.where(high[r, r], -eb, -1.0), num[r, r])
                sb = soft[r, r] - jnp.where(hit, xb, 0.0)
                keep = slice((1 - q) * 128, (2 - q) * 128)
                nums.append(jnp.concatenate([nb, num[r, keep]] if q == 0 else [num[r, keep], nb], axis=1))
                softs.append(jnp.concatenate([sb, soft[r, keep]] if q == 0 else [soft[r, keep], sb], axis=1))
            num = jnp.concatenate(nums, axis=0)
            soft = jnp.concatenate(softs, axis=0)
        w = num * pl.reciprocal(t, approx=True)
        scaled = (w * gain).astype(BF)
        tt = t.reshape(8, 32, 256)
        ee = e.reshape(8, 32, 256)
        prod = ee[0]
        for m in range(1, 8):
            prod = prod * tt[m] + ee[m]
        pr = prod.reshape(4, 8, 256)
        p0 = pr[0] + pr[1] + pr[0] * pr[1]
        p1 = pr[2] + pr[3] + pr[2] * pr[3]
        p = p0 + p1 + p0 * p1
        logs = jnp.where(p < 1e-3, p * (1.0 - 0.5 * p), jnp.log(1.0 + p))
        soft_sum = soft.reshape(32, 8, 256).sum(0)
        w_sum = w.reshape(32, 8, 256).sum(0)
        return scaled, soft_sum, logs, w_sum

    def one_job(j, valid, carry):
        soft_acc, log_acc, w_acc = carry
        ui, ii = jobs[j], jobs[j + 72]
        label_j = jobs[j + 144].astype(F32)
        slope_j = jnp.where(valid, slope, 0.0)
        shift_j = jnp.where(valid, shift, -1e30)
        label_j = jnp.where(valid, label_j, 0.0)
        it = items[ii]
        um = users[ui, pl.ds(mine, half), :]
        uo = users[ui, pl.ds(other, half), :]
        sm, a0, l0, w0 = tile(um, it, slope_j, shift_j, label_j)
        so, a1, l1, w1 = tile(uo, it, slope_j, shift_j, None)
        uacc[ui, pl.ds(mine, half), :] += lax.dot_general(sm, it, NN, preferred_element_type=F32)
        uacc[ui, pl.ds(other, half), :] += lax.dot_general(so, it, NN, preferred_element_type=F32)
        iacc[ii] += (lax.dot_general(sm, um, TN, preferred_element_type=F32)
                     + lax.dot_general(so, uo, TN, preferred_element_type=F32))
        return soft_acc + (a0 + a1), log_acc + (l0 + l1), w_acc + (w0 + w1)

    def two_jobs(g, carry):
        carry = one_job(2 * g, True, carry)
        return one_job(2 * g + 1, 2 * g + 1 < count, carry)

    zero = jnp.zeros((8, 256), F32)
    soft_acc, log_acc, w_acc = lax.fori_loop(0, (count + 1) // 2, two_jobs, (zero, zero, zero))

    sends = RING * 2
    out = [
        pltpu.make_async_copy(uacc.at[:, pl.ds(mine, half), :], user_keep, out_sem.at[0]),
        pltpu.make_async_copy(iacc.at[pl.ds(0, sends)], item_keep, out_sem.at[1]),
    ]
    for c in out:
        c.start()

    def user_out(b, acc):
        given = uacc[b, pl.ds(other, half), :]
        ugive[b] = given.astype(BF)
        kept = uacc[b, pl.ds(mine, half), :]
        prod = (kept * users[b, pl.ds(mine, half), :].astype(F32)
                + given * users[b, pl.ds(other, half), :].astype(F32))
        return acc + prod.reshape(32, 8, 256).sum(0)

    scale_acc = lax.fori_loop(0, RING * blocks, user_out, zero)
    c = pltpu.make_async_copy(ugive, user_give, out_sem.at[2])
    c.start()
    out.append(c)

    def item_out(b, none):
        igive[b] = iacc[b + sends].astype(BF)
        return none

    lax.fori_loop(0, (RING - 1) * sends, item_out, 0)
    c = pltpu.make_async_copy(igive, item_give, out_sem.at[3])
    c.start()
    out.append(c)
    sums[0] = soft_acc * (1.0 / LOG2E) + log_acc
    sums[1] = scale_acc * scalars[3]
    sums[2] = w_acc
    for c in out:
        c.wait()


def score(place, table, scalars, own_users, near_users, far_users, items_in):
    blocks, height, width = own_users.shape
    half = height // 2
    n_users, n_items = RING * blocks, items_in.shape[0]
    smem = pl.BlockSpec(memory_space=pltpu.SMEM)
    any_ = pl.BlockSpec(memory_space=pl.ANY)
    return pl.pallas_call(
        score_kernel,
        in_specs=[smem, smem, smem, any_, any_, any_, any_],
        out_specs=[any_, any_, any_, any_, pl.BlockSpec(memory_space=pltpu.VMEM)],
        out_shape=[
            jax.ShapeDtypeStruct((n_users, half, width), F32),
            jax.ShapeDtypeStruct((n_users, half, width), BF),
            jax.ShapeDtypeStruct((2 * RING, half, width), F32),
            jax.ShapeDtypeStruct((n_items - 2 * RING, half, width), BF),
            jax.ShapeDtypeStruct((3, 8, width), F32),
        ],
        scratch_shapes=[
            pltpu.VMEM((n_users, height, width), BF),
            pltpu.VMEM((n_items, half, width), BF),
            pltpu.VMEM((n_users, height, width), F32),
            pltpu.VMEM((n_items, half, width), F32),
            pltpu.VMEM((n_users, half, width), BF),
            pltpu.VMEM((n_items - 2 * RING, half, width), BF),
            pltpu.VMEM((128, 128), F32),
            pltpu.SMEM((256,), jnp.int32),
            pltpu.SemaphoreType.DMA((8,)),
            pltpu.SemaphoreType.DMA((4,)),
        ],
        compiler_params=pltpu.CompilerParams(vmem_limit_bytes=56 * 2**20),
        cost_estimate=pl.CostEstimate(flops=13 * 10**9, bytes_accessed=20 * 2**20, transcendentals=2 * 10**7),
    )(place, table, scalars, own_users, near_users, far_users, items_in)


def device(x, y, z, core):
    return (((x % RING) * RING + y % RING) * RING + z % RING) * 2 + core


def every():
    return [(x, y, z, c) for x in range(RING) for y in range(RING) for z in range(RING) for c in range(2)]


AXES = ("x", "y", "z", "n")


def along_z(a, d):
    return lax.ppermute(a, AXES, [(device(x, y, z, c), device(x, y, z + d, c)) for x, y, z, c in every()])


def along_first(a, d):
    return lax.ppermute(a, AXES, [
        (device(x, y, z, c), device(x + (d if c else 0), y + (0 if c else d), z, c)) for x, y, z, c in every()])


def along_second(a, d):
    return lax.ppermute(a, AXES, [
        (device(x, y, z, c), device(x + (0 if c else d), y + (d if c else 0), z, c)) for x, y, z, c in every()])


def across(a):
    return lax.ppermute(a, AXES, [(device(x, y, z, c), device(x, y, z, 1 - c)) for x, y, z, c in every()])


def body(user_emb, item_emb, pairs, counts, natural_exponent_param, additive_shift_param):
    my_x, my_y, my_z = lax.axis_index("x"), lax.axis_index("y"), lax.axis_index("z")
    core = lax.axis_index("n")
    blocks, height, width = user_emb.shape
    half = height // 2
    sharpness = jnp.exp(natural_exponent_param[0])
    shift = additive_shift_param[0]
    root = height ** 0.5

    users_low = user_emb.astype(BF)
    my_half = lax.dynamic_slice_in_dim(user_emb, core * half, half, axis=1).astype(BF)
    slots = pairs.shape[1]
    flat = jnp.concatenate([pairs[0].reshape(-1), counts]).astype(F32)
    flat = jnp.pad(flat, (0, 16 * width - flat.shape[0])).astype(BF).reshape(16, width)
    packet = jnp.concatenate([my_half.reshape(blocks * half, width), flat], axis=0)
    items_low = item_emb.astype(BF)

    got = [along_z(packet, d) for d in (1, 2, 3)]
    line = jnp.concatenate([items_low] + [along_first(items_low, d) for d in (1, 2, 3)], axis=0)
    plane = jnp.concatenate([line] + [along_second(line, d) for d in (1, 2, 3)], axis=0)
    near = jnp.concatenate([g[: blocks * half].reshape(blocks, half, width) for g in got], axis=0)
    far = across(near)
    lists = [g[blocks * half:].reshape(-1)[: slots * 3 + 1].astype(jnp.int32) for g in [packet] + got]
    table = jnp.concatenate([v[: slots * 3] for v in lists] + [v[slots * 3:] for v in lists])
    place = jnp.stack([my_x, my_y, my_z, core]).astype(jnp.int32)
    scalars = jnp.stack([sharpness * LOG2E, shift * LOG2E, sharpness * height ** -0.5, jnp.float32(root)])

    user_keep, user_give, item_keep, item_give, sums = score(
        place, table, scalars, users_low, near, far, plane)

    user_got = across(user_give)
    summed = user_keep + user_got.astype(F32)
    back = [along_z(summed[d * blocks:(d + 1) * blocks].astype(BF), -d) for d in (1, 2, 3)]
    user_half = summed[:blocks] + back[0].astype(F32) + back[1].astype(F32) + back[2].astype(F32)
    user_rest = across(user_half)
    low = jnp.where(core == 0, user_half, user_rest)
    high = jnp.where(core == 0, user_rest, user_half)
    user_grad = jnp.concatenate([low, high], axis=1)

    n = 2 * RING
    back = [along_second(item_give[(d - 1) * n: d * n], -d) for d in (1, 2, 3)]
    item_line = item_keep + back[0].astype(F32) + back[1].astype(F32) + back[2].astype(F32)
    back = [along_first(item_line[2 * d: 2 * d + 2].astype(BF), -d) for d in (1, 2, 3)]
    item_grad = item_line[:2] + back[0].astype(F32) + back[1].astype(F32) + back[2].astype(F32)

    totals = jnp.concatenate([jnp.sum(sums, axis=(1, 2)), counts.astype(F32) * 0.5])
    totals = lax.psum(totals, AXES)
    objective = totals[:3] / (height * height * totals[3])
    return user_grad, item_grad, objective


def solution(mesh):
    grid = Mesh(mesh.devices.reshape(RING, RING, RING, 2), AXES)
    return jax.shard_map(
        body,
        mesh=grid,
        in_specs=(P(WIDE, None, None), P(WIDE, "n", None), P(WIDE, None, None), P(WIDE), P(), P()),
        out_specs=(P(WIDE, None, None), P(WIDE, "n", None), P()),
        check_vma=False,
    )
```

time: 654 us -> 242 us (0.37)
  matrix products: 122 us -> 0 us
  blocking collectives: 171 us -> 63.2 us
  waiting for transfers between devices: 123 us -> 46.1 us
  local copies, waits for them, and re-layouts: 99.7 us -> 24.6 us
  other arithmetic: 73.9 us -> 20.9 us
  Pallas kernels: 0 us -> 53 us
  loops' own time: 15.4 us -> 0 us
  between operations: 18.2 us -> 3.48 us
    all_to_all x3 -> x0, waiting for transfers between devices: 123 us -> none  [the longest x1 115 us: body(): lax.all_to_all(outgoing, 'wide', split_axis=0, concat_axis=0, tiled=True)]
    dot_general x34 -> x0, matrix products: 122 us -> none  [the longest x8 36.9 us: visit_group(): jnp.einsum('gu,gre->ure', spread, user_parts, preferred_element_type=jnp....]
    psum x1, blocking collectives: 171 us -> 63.2 us  [body(): totals = lax.psum(totals, AXES)]
    reduce_sum x9 -> x1, other arithmetic: 61 us -> 0.11 us  [body(): jnp.sum(sums, axis=(1, 2))]
    pallas_call x0 -> x1, Pallas kernels: none -> 53 us  [score(): pl.pallas_call(score_kernel, in_specs=[smem, smem, smem, any_, any_, any_...]
    gather x24 -> x0, local copies, waits for them, and re-layouts: 49.7 us -> none  [the longest x8 39.8 us: visit_group(): item_block_rows = jnp.take(fetched, owner, axis=0)]
    ppermute x0 -> x21, waiting for transfers between devices: none -> 46.1 us  [the longest x6 36.2 us: along_z(): lax.ppermute(a, AXES, [(device(x, y, z, c), device(x, y, z + d, c)) for x...]
    all_to_all x3 -> x0, starting transfers between devices: 28.8 us -> none  [the longest x1 11.5 us: body(): lax.all_to_all(request, 'wide', split_axis=0, concat_axis=0, tiled=True)]
  transfers between devices with their start and end apart: 4 -> 21, of which waited for: 2 -> 5; matrix products, arithmetic and copies ran while one was open for 2% -> 14% of each run, Pallas kernels for 0% -> 0%
where the time goes in v1:
time: 242 us; the launch traced here: 240 us
  blocking collectives  63.2 us (26%)
  Pallas kernels  53 us (22%)
  waiting for transfers between devices  46.1 us (19%)
  starting transfers between devices  28.4 us (12%)
  local copies, waits for them, and re-layouts  24.6 us (10%)
  other arithmetic  20.9 us (9%)
  between operations  3.48 us (1%)
    psum x1, blocking collectives, body(): totals = lax.psum(totals, AXES)  63.2 us
    pallas_call x1, Pallas kernels, score(): pl.pallas_call(score_kernel, in_specs=[smem, smem, smem, any_, any_, any_...  53 us
    ppermute x6, waiting for transfers between devices, along_z(): lax.ppermute(a, AXES, [(device(x, y, z, c), device(x, y, z + d, c)) for x...  36.2 us
    ppermute x6, starting transfers between devices, along_second(): lax.ppermute(a, AXES, [(device(x, y, z, c), device(x + (0 if c else d), y...  12.1 us
    unnamed x22, local copies, waits for them, and re-layouts  9.74 us
    ppermute x6, starting transfers between devices, along_first(): lax.ppermute(a, AXES, [(device(x, y, z, c), device(x + (d if c else 0), y...  8.66 us
    another operation x2, other arithmetic  7.91 us
    ppermute x6, starting transfers between devices, along_z(): lax.ppermute(a, AXES, [(device(x, y, z, c), device(x, y, z + d, c)) for x...  7.43 us
  transfers between devices with their start and end apart: 21, of which 5 were waited for; matrix products, arithmetic and copies ran while one was open for 14% of the time, Pallas kernels for 0%

profile of v1, /device:TPU:0, one launch (start us, length us, event | category | flops | bytes accessed | tf_op | source)
XLA Modules:
  0.0 239.6 jit_solution(688693022445464955)
XLA Ops:
  0.6 1.9 constant_dynamic-update-slice_fusion.6
  2.6 3.1 %collective-permute-start.6 = (bf16[2,256,256]{2,1,0:T(8,128)(2,1)S(1)}, bf16[2,256,256]{2,1,0:T(8,128)(2,1)S(1)}, u32[]{:S(2)}, u32[]{:S(2)}) collective-permute-start(bf16[2,256,256]{2,1,0:T(8,128)(2,1)S(1)} %get-tuple-element.18), channel_id=1, source_target_pairs={{0,24},{1,97},{2,26},{3,99},{4,28},{5,101},{6,30},{7,103},{8,0},{9... | collective-permute-start | bytes 786440 | tf_op jit(solution)/shard_map/ppermute | solution.py:226
  5.7 0.6 collective-permute-start.5
  6.3 1.0 collective-permute-start.4
  7.9 0.8 copy.9
  8.7 0.1 reshape_squeeze.3
  8.9 1.3 dynamic-slice_convert_fusion
  10.2 0.8 pad_maximum_fusion.3
  11.1 4.0 %collective-permute-start.2 = (bf16[1040,256]{1,0:T(8,128)(2,1)}, bf16[1040,256]{1,0:T(8,128)(2,1)}, u32[]{:S(2)}, u32[]{:S(2)}) collective-permute-start(bf16[1040,256]{1,0:T(8,128)(2,1)} %pad_maximum_fusion.3), channel_id=1, source_target_pairs={{0,6},{1,7},{2,0},{3,1},{4,2},{5,3},{6,4},{7,5},{8,14},{9,15},{10,... | collective-permute-start | bytes 1597448 | tf_op jit(solution)/shard_map/ppermute | solution.py:222
  16.4 0.6 pad_maximum_fusion.4.scalars
  17.1 1.3 collective-permute-start
  18.3 0.7 pad_add_fusion.place
  19.0 1.1 convert_element_type.72.own_users
  20.1 0.6 slice.110
  20.6 0.1 pad_maximum_fusion.2
  20.8 2.8 %collective-permute-start.9 = (bf16[8,256,256]{2,1,0:T(8,128)(2,1)S(1)}, bf16[8,256,256]{2,1,0:T(8,128)(2,1)}, u32[]{:S(2)}, u32[]{:S(2)}) collective-permute-start(bf16[8,256,256]{2,1,0:T(8,128)(2,1)S(1)} %pad_maximum_fusion.2), channel_id=1, source_target_pairs={{0,96},{1,25},{2,98},{3,27},{4,100},{5,29},{6,102},{7,31},{8,104},... | collective-permute-start | bytes 3145736 | tf_op jit(solution)/shard_map/ppermute | solution.py:231
  23.6 0.8 collective-permute-start.8
  24.4 0.7 constant_dynamic-update-slice_fusion.5
  25.1 0.7 constant_dynamic-update-slice_fusion.4
  25.9 0.7 constant_dynamic-update-slice_fusion.3
  26.6 10.6 %collective-permute-done.2 = bf16[1040,256]{1,0:T(8,128)(2,1)} collective-permute-done((bf16[1040,256]{1,0:T(8,128)(2,1)}, bf16[1040,256]{1,0:T(8,128)(2,1)}, u32[]{:S(2)}, u32[]{:S(2)}) %collective-permute-start.2) | collective-permute-done | bytes 532512 | tf_op jit(solution)/shard_map/ppermute | solution.py:222
  37.2 1.8 collective-permute-start.7
  39.0 1.1 slice.138
  40.1 1.1 slice.137
  41.2 0.2 pad_maximum_fusion.1.near_users
  41.4 0.1 collective-permute-start.3
  41.5 0.7 slice_bitcast_fusion
  42.2 0.7 slice_bitcast_fusion.1
  42.9 0.6 slice.113
  43.6 0.6 slice.112
  44.2 0.6 slice.111
  44.8 3.0 %concatenate.27.table = s32[772]{0:T(1024)} concatenate(s32[192]{0:T(256)S(1)} %bitcast.29, s32[192]{0:T(256)S(1)} %bitcast.32, s32[192]{0:T(256)S(1)} %bitcast.31, s32[192]{0:T(256)S(1)} %bitcast.30, s32[1]{0:T(128)} %slice.110, s32[1]{0:T(128)} %slice.111, s32[1]{0:T(128)} %slice.112, s32[1]{0:T(128)} %slice.113), dimensions={0} | concatenate | bytes 6176 | tf_op jit(solution)/shard_map/concatenate | solution.py:262
  47.8 5.5 %collective-permute-done.7 = bf16[8,256,256]{2,1,0:T(8,128)(2,1)} collective-permute-done((bf16[8,256,256]{2,1,0:T(8,128)(2,1)S(1)}, bf16[8,256,256]{2,1,0:T(8,128)(2,1)}, u32[]{:S(2)}, u32[]{:S(2)}) %collective-permute-start.7) | collective-permute-done | bytes 1048608 | tf_op jit(solution)/shard_map/ppermute | solution.py:231
  53.3 2.2 constant_dynamic-update-slice_fusion.2
  55.5 2.3 constant_dynamic-update-slice_fusion.1
  57.8 2.2 constant_dynamic-update-slice_fusion.items_in
  60.1 53.0 %shard_map.85 = (f32[16,256,256]{2,1,0:T(8,128)}, bf16[16,256,256]{2,1,0:T(8,128)(2,1)}, f32[8,256,256]{2,1,0:T(8,128)}, bf16[24,256,256]{2,1,0:T(8,128)(2,1)}, f32[3,8,256]{2,1,0:T(8,128)}) custom-call(s32[4]{0:T(128)} %pad_add_fusion.place, s32[772]{0:T(1024)} %concatenate.27.table, f32[4]{0:T(128)} %pad_maximum_fusion.4.scalars, ...), custom_call_target="tpu_custom_call" | custom-call | flops 12999999488 | bytes 20971520 | tf_op jit(solution)/shard_map/pallas_call | solution.py:182
  113.0 0.1 collective-permute-start.10
  113.1 4.4 %collective-permute-done.10 = bf16[16,256,256]{2,1,0:T(8,128)(2,1)S(1)} collective-permute-done((bf16[16,256,256]{2,1,0:T(8,128)(2,1)}, bf16[16,256,256]{2,1,0:T(8,128)(2,1)S(1)}, u32[]{:S(2)}, u32[]{:S(2)}) %collective-permute-start.10) | collective-permute-done | bytes 2097184 | tf_op jit(solution)/shard_map/ppermute | solution.py:236
  117.5 4.9 %fusion.6 = (bf16[16,256,256]{2,1,0:T(8,128)(2,1)S(1)}, f32[16,256,256]{2,1,0:T(8,128)}) fusion(f32[16,256,256]{2,1,0:T(8,128)} %get-tuple-element.8, bf16[16,256,256]{2,1,0:T(8,128)(2,1)S(1)} %collective-permute-done.10), kind=kLoop, calls=%fused_computation.35 | loop fusion | flops 3145728 | bytes 12582912 | tf_op jit(solution)/shard_map/convert.5
  122.4 0.9 fusion.10
  123.4 1.2 collective-permute-start.11
  124.6 1.2 fusion.9
  125.8 1.1 collective-permute-start.15
  126.9 2.0 collective-permute-start.17
  128.9 3.6 %collective-permute-start.16 = (bf16[8,256,256]{2,1,0:T(8,128)(2,1)S(1)}, bf16[8,256,256]{2,1,0:T(8,128)(2,1)}, u32[]{:S(2)}, u32[]{:S(2)}) collective-permute-start(bf16[8,256,256]{2,1,0:T(8,128)(2,1)S(1)} %get-tuple-element.23), channel_id=1, source_target_pairs={{0,64},{1,17},{2,66},{3,19},{4,68},{5,21},{6,70},{7,23},{8,72},{9,... | collective-permute-start | bytes 3145736 | tf_op jit(solution)/shard_map/ppermute | solution.py:231
  132.5 5.0 %collective-permute-done.11 = bf16[4,256,256]{2,1,0:T(8,128)(2,1)} collective-permute-done((bf16[4,256,256]{2,1,0:T(8,128)(2,1)S(1)}, bf16[4,256,256]{2,1,0:T(8,128)(2,1)}, u32[]{:S(2)}, u32[]{:S(2)}) %collective-permute-start.11) | collective-permute-done | bytes 524320 | tf_op jit(solution)/shard_map/ppermute | solution.py:222
  137.4 0.9 collective-permute-start.12
  138.4 0.1 reduce_sum.9
  138.5 20.6 %collective-permute-done.13 = bf16[4,256,256]{2,1,0:T(8,128)(2,1)} collective-permute-done((bf16[4,256,256]{2,1,0:T(8,128)(2,1)}, bf16[4,256,256]{2,1,0:T(8,128)(2,1)}, u32[]{:S(2)}, u32[]{:S(2)}) %collective-permute-start.13) | collective-permute-done | bytes 524320 | tf_op jit(solution)/shard_map/ppermute | solution.py:222
  159.1 0.8 copy-done.3
  159.9 1.9 fusion.1
  161.8 0.1 collective-permute-start.14
  161.9 3.0 %fusion.5 = (bf16[8,256,256]{2,1,0:T(8,128)(2,1)S(1)}, f32[8,256,256]{2,1,0:T(8,128)S(1)}) fusion(bf16[8,256,256]{2,1,0:T(8,128)(2,1)} %collective-permute-done.17, bf16[8,256,256]{2,1,0:T(8,128)(2,1)} %collective-permute-done.16, f32[8,256,256]{2,1,0:T(8,128)} %get-tuple-element.10, bf16[8,256,256]{2,1,0:T(8,128)(2,1)} %collective-permute-done.15), kind=kLoop, calls=%fused_computation.34 | loop fusion | flops 3670016 | bytes 8388608 | tf_op jit(solution)/shard_map/convert.2
  164.9 0.9 fusion.11
  165.8 1.3 collective-permute-start.18
  167.1 0.7 collective-permute-start.20
  167.8 1.9 collective-permute-start.19
  169.8 63.2 %psum.7 = f32[4]{0:T(128)S(1)} all-reduce(f32[4]{0:T(128)S(1)} %pad_maximum_fusion.5), channel_id=1, replica_groups=mesh['x'=4,'y'=4,'z'=4,'n'=2] {'x','y','z','n'}, use_global_device_ids=true, to_apply=%region_1.2 | all-reduce | flops 4 | bytes 32 | tf_op jit(solution)/shard_map/psum | solution.py:285
  233.0 0.6 slice.129
  234.2 0.5 slice_divide_fusion
  234.8 1.9 fusion.3
  236.7 1.4 broadcast_select_fusion.1
  238.1 1.5 pad_maximum_fusion
  (39 shorter events, 0.3 us)
Async XLA Ops:
  0.6 18.3 %copy-start = (f32[4,512,256]{2,1,0:T(8,128)S(1)}, f32[4,512,256]{2,1,0:T(8,128)}, u32[]{:S(2)}) copy-start(f32[4,512,256]{2,1,0:T(8,128)} %param.6) | copy-start | bytes 6291460
  2.6 14.5 %collective-permute-start.6 = (bf16[2,256,256]{2,1,0:T(8,128)(2,1)S(1)}, bf16[2,256,256]{2,1,0:T(8,128)(2,1)S(1)}, u32[]{:S(2)}, u32[]{:S(2)}) collective-permute-start(bf16[2,256,256]{2,1,0:T(8,128)(2,1)S(1)} %get-tuple-element.18), channel_id=1, source_target_pairs={{0,24},{1,97},{2,26},{3,99},{4,28},{5,101},{6,30},{7,103},{8,0},{9... | collective-permute-start | bytes 786440 | tf_op jit(solution)/shard_map/ppermute | solution.py:226
  5.7 15.0 %collective-permute-start.5 = (bf16[2,256,256]{2,1,0:T(8,128)(2,1)S(1)}, bf16[2,256,256]{2,1,0:T(8,128)(2,1)S(1)}, u32[]{:S(2)}, u32[]{:S(2)}) collective-permute-start(bf16[2,256,256]{2,1,0:T(8,128)(2,1)S(1)} %get-tuple-element.18), channel_id=1, source_target_pairs={{0,16},{1,65},{2,18},{3,67},{4,20},{5,69},{6,22},{7,71},{8,24},{9,... | collective-permute-start | bytes 786440 | tf_op jit(solution)/shard_map/ppermute | solution.py:226
  6.3 14.3 %collective-permute-start.4 = (bf16[2,256,256]{2,1,0:T(8,128)(2,1)S(1)}, bf16[2,256,256]{2,1,0:T(8,128)(2,1)S(1)}, u32[]{:S(2)}, u32[]{:S(2)}) collective-permute-start(bf16[2,256,256]{2,1,0:T(8,128)(2,1)S(1)} %get-tuple-element.18), channel_id=1, source_target_pairs={{0,8},{1,33},{2,10},{3,35},{4,12},{5,37},{6,14},{7,39},{8,16},{9,4... | collective-permute-start | bytes 786440 | tf_op jit(solution)/shard_map/ppermute | solution.py:226
  11.1 26.1 %collective-permute-start.2 = (bf16[1040,256]{1,0:T(8,128)(2,1)}, bf16[1040,256]{1,0:T(8,128)(2,1)}, u32[]{:S(2)}, u32[]{:S(2)}) collective-permute-start(bf16[1040,256]{1,0:T(8,128)(2,1)} %pad_maximum_fusion.3), channel_id=1, source_target_pairs={{0,6},{1,7},{2,0},{3,1},{4,2},{5,3},{6,4},{7,5},{8,14},{9,15},{10,... | collective-permute-start | bytes 1597448 | tf_op jit(solution)/shard_map/ppermute | solution.py:222
  15.1 25.0 %collective-permute-start.1 = (bf16[1040,256]{1,0:T(8,128)(2,1)}, bf16[1040,256]{1,0:T(8,128)(2,1)}, u32[]{:S(2)}, u32[]{:S(2)}) collective-permute-start(bf16[1040,256]{1,0:T(8,128)(2,1)} %pad_maximum_fusion.3), channel_id=1, source_target_pairs={{0,4},{1,5},{2,6},{3,7},{4,0},{5,1},{6,2},{7,3},{8,12},{9,13},{10,... | collective-permute-start | bytes 1597448 | tf_op jit(solution)/shard_map/ppermute | solution.py:222
  17.1 24.1 %collective-permute-start = (bf16[1040,256]{1,0:T(8,128)(2,1)}, bf16[1040,256]{1,0:T(8,128)(2,1)S(1)}, u32[]{:S(2)}, u32[]{:S(2)}) collective-permute-start(bf16[1040,256]{1,0:T(8,128)(2,1)} %pad_maximum_fusion.3), channel_id=1, source_target_pairs={{0,2},{1,3},{2,4},{3,5},{4,6},{5,7},{6,0},{7,1},{8,10},{9,11},{10,... | collective-permute-start | bytes 1597448 | tf_op jit(solution)/shard_map/ppermute | solution.py:222
  20.8 37.0 %collective-permute-start.9 = (bf16[8,256,256]{2,1,0:T(8,128)(2,1)S(1)}, bf16[8,256,256]{2,1,0:T(8,128)(2,1)}, u32[]{:S(2)}, u32[]{:S(2)}) collective-permute-start(bf16[8,256,256]{2,1,0:T(8,128)(2,1)S(1)} %pad_maximum_fusion.2), channel_id=1, source_target_pairs={{0,96},{1,25},{2,98},{3,27},{4,100},{5,29},{6,102},{7,31},{8,104},... | collective-permute-start | bytes 3145736 | tf_op jit(solution)/shard_map/ppermute | solution.py:231
  23.6 31.9 %collective-permute-start.8 = (bf16[8,256,256]{2,1,0:T(8,128)(2,1)S(1)}, bf16[8,256,256]{2,1,0:T(8,128)(2,1)}, u32[]{:S(2)}, u32[]{:S(2)}) collective-permute-start(bf16[8,256,256]{2,1,0:T(8,128)(2,1)S(1)} %pad_maximum_fusion.2), channel_id=1, source_target_pairs={{0,64},{1,17},{2,66},{3,19},{4,68},{5,21},{6,70},{7,23},{8,72},{9,... | collective-permute-start | bytes 3145736 | tf_op jit(solution)/shard_map/ppermute | solution.py:231
  37.2 16.1 %collective-permute-start.7 = (bf16[8,256,256]{2,1,0:T(8,128)(2,1)S(1)}, bf16[8,256,256]{2,1,0:T(8,128)(2,1)}, u32[]{:S(2)}, u32[]{:S(2)}) collective-permute-start(bf16[8,256,256]{2,1,0:T(8,128)(2,1)S(1)} %pad_maximum_fusion.2), channel_id=1, source_target_pairs={{0,32},{1,9},{2,34},{3,11},{4,36},{5,13},{6,38},{7,15},{8,40},{9,1... | collective-permute-start | bytes 3145736 | tf_op jit(solution)/shard_map/ppermute | solution.py:231
  41.4 16.4 %copy-start.2 = (bf16[12,256,256]{2,1,0:T(8,128)(2,1)}, bf16[12,256,256]{2,1,0:T(8,128)(2,1)S(1)}, u32[]{:S(2)}) copy-start(bf16[12,256,256]{2,1,0:T(8,128)(2,1)S(1)} %pad_maximum_fusion.1.near_users) | copy-start | bytes 4718596
  41.4 18.7 %collective-permute-start.3 = (bf16[12,256,256]{2,1,0:T(8,128)(2,1)S(1)}, bf16[12,256,256]{2,1,0:T(8,128)(2,1)}, u32[]{:S(2)}, u32[]{:S(2)}) collective-permute-start(bf16[12,256,256]{2,1,0:T(8,128)(2,1)S(1)} %pad_maximum_fusion.1.near_users), channel_id=1, source_target_pairs={{0,1},{1,0},{2,3},{3,2},{4,5},{5,4},{6,7},{7,6},{8,9},{9,8},{10,11... | collective-permute-start | bytes 4718600 | tf_op jit(solution)/shard_map/ppermute | solution.py:236
  113.0 4.5 %collective-permute-start.10 = (bf16[16,256,256]{2,1,0:T(8,128)(2,1)}, bf16[16,256,256]{2,1,0:T(8,128)(2,1)S(1)}, u32[]{:S(2)}, u32[]{:S(2)}) collective-permute-start(bf16[16,256,256]{2,1,0:T(8,128)(2,1)} %get-tuple-element.9), channel_id=1, source_target_pairs={{0,1},{1,0},{2,3},{3,2},{4,5},{5,4},{6,7},{7,6},{8,9},{9,8},{10,11... | collective-permute-start | bytes 6291464 | tf_op jit(solution)/shard_map/ppermute | solution.py:236
  122.4 2.1 copy-start.1
  123.4 14.1 %collective-permute-start.11 = (bf16[4,256,256]{2,1,0:T(8,128)(2,1)S(1)}, bf16[4,256,256]{2,1,0:T(8,128)(2,1)}, u32[]{:S(2)}, u32[]{:S(2)}) collective-permute-start(bf16[4,256,256]{2,1,0:T(8,128)(2,1)S(1)} %get-tuple-element.26), channel_id=1, source_target_pairs={{0,6},{1,7},{2,0},{3,1},{4,2},{5,3},{6,4},{7,5},{8,14},{9,15},{10,... | collective-permute-start | bytes 1572872 | tf_op jit(solution)/shard_map/ppermute | solution.py:222
  124.6 13.8 %copy-start.4 = (f32[3,8,256]{2,1,0:T(8,128)S(1)}, f32[3,8,256]{2,1,0:T(8,128)}, u32[]{:S(2)}) copy-start(f32[3,8,256]{2,1,0:T(8,128)} %get-tuple-element.12) | copy-start | bytes 73732
  125.8 36.1 %collective-permute-start.15 = (bf16[8,256,256]{2,1,0:T(8,128)(2,1)}, bf16[8,256,256]{2,1,0:T(8,128)(2,1)}, u32[]{:S(2)}, u32[]{:S(2)}) collective-permute-start(bf16[8,256,256]{2,1,0:T(8,128)(2,1)} %get-tuple-element.21), channel_id=1, source_target_pairs={{0,96},{1,25},{2,98},{3,27},{4,100},{5,29},{6,102},{7,31},{8,104},... | collective-permute-start | bytes 3145736 | tf_op jit(solution)/shard_map/ppermute | solution.py:231
  126.9 35.0 %collective-permute-start.17 = (bf16[8,256,256]{2,1,0:T(8,128)(2,1)S(1)}, bf16[8,256,256]{2,1,0:T(8,128)(2,1)}, u32[]{:S(2)}, u32[]{:S(2)}) collective-permute-start(bf16[8,256,256]{2,1,0:T(8,128)(2,1)S(1)} %get-tuple-element.22), channel_id=1, source_target_pairs={{0,32},{1,9},{2,34},{3,11},{4,36},{5,13},{6,38},{7,15},{8,40},{9,1... | collective-permute-start | bytes 3145736 | tf_op jit(solution)/shard_map/ppermute | solution.py:231
  128.9 33.0 %collective-permute-start.16 = (bf16[8,256,256]{2,1,0:T(8,128)(2,1)S(1)}, bf16[8,256,256]{2,1,0:T(8,128)(2,1)}, u32[]{:S(2)}, u32[]{:S(2)}) collective-permute-start(bf16[8,256,256]{2,1,0:T(8,128)(2,1)S(1)} %get-tuple-element.23), channel_id=1, source_target_pairs={{0,64},{1,17},{2,66},{3,19},{4,68},{5,21},{6,70},{7,23},{8,72},{9,... | collective-permute-start | bytes 3145736 | tf_op jit(solution)/shard_map/ppermute | solution.py:231
  132.5 26.6 %collective-permute-start.13 = (bf16[4,256,256]{2,1,0:T(8,128)(2,1)}, bf16[4,256,256]{2,1,0:T(8,128)(2,1)}, u32[]{:S(2)}, u32[]{:S(2)}) collective-permute-start(bf16[4,256,256]{2,1,0:T(8,128)(2,1)} %get-tuple-element.27), channel_id=1, source_target_pairs={{0,2},{1,3},{2,4},{3,5},{4,6},{5,7},{6,0},{7,1},{8,10},{9,11},{10,... | collective-permute-start | bytes 1572872 | tf_op jit(solution)/shard_map/ppermute | solution.py:222
  137.4 21.7 %collective-permute-start.12 = (bf16[4,256,256]{2,1,0:T(8,128)(2,1)S(1)}, bf16[4,256,256]{2,1,0:T(8,128)(2,1)S(1)}, u32[]{:S(2)}, u32[]{:S(2)}) collective-permute-start(bf16[4,256,256]{2,1,0:T(8,128)(2,1)S(1)} %get-tuple-element.28), channel_id=1, source_target_pairs={{0,4},{1,5},{2,6},{3,7},{4,0},{5,1},{6,2},{7,3},{8,12},{9,13},{10,... | collective-permute-start | bytes 1572872 | tf_op jit(solution)/shard_map/ppermute | solution.py:222
  159.1 0.8 copy-start.3
  161.8 74.9 %collective-permute-start.14 = (f32[4,256,256]{2,1,0:T(8,128)S(1)}, f32[4,256,256]{2,1,0:T(8,128)}, u32[]{:S(2)}, u32[]{:S(2)}) collective-permute-start(f32[4,256,256]{2,1,0:T(8,128)S(1)} %fusion.1), channel_id=1, source_target_pairs={{0,1},{1,0},{2,3},{3,2},{4,5},{5,4},{6,7},{7,6},{8,9},{9,8},{10,11... | collective-permute-start | bytes 3145736 | tf_op jit(solution)/shard_map/ppermute | solution.py:236
  165.8 69.0 %collective-permute-start.18 = (bf16[2,256,256]{2,1,0:T(8,128)(2,1)}, bf16[2,256,256]{2,1,0:T(8,128)(2,1)S(1)}, u32[]{:S(2)}, u32[]{:S(2)}) collective-permute-start(bf16[2,256,256]{2,1,0:T(8,128)(2,1)} %get-tuple-element.29), channel_id=1, source_target_pairs={{0,24},{1,97},{2,26},{3,99},{4,28},{5,101},{6,30},{7,103},{8,0},{9... | collective-permute-start | bytes 786440 | tf_op jit(solution)/shard_map/ppermute | solution.py:226
  167.1 67.7 %collective-permute-start.20 = (bf16[2,256,256]{2,1,0:T(8,128)(2,1)}, bf16[2,256,256]{2,1,0:T(8,128)(2,1)}, u32[]{:S(2)}, u32[]{:S(2)}) collective-permute-start(bf16[2,256,256]{2,1,0:T(8,128)(2,1)} %get-tuple-element.30), channel_id=1, source_target_pairs={{0,8},{1,33},{2,10},{3,35},{4,12},{5,37},{6,14},{7,39},{8,16},{9,4... | collective-permute-start | bytes 786440 | tf_op jit(solution)/shard_map/ppermute | solution.py:226
  167.8 66.9 %collective-permute-start.19 = (bf16[2,256,256]{2,1,0:T(8,128)(2,1)}, bf16[2,256,256]{2,1,0:T(8,128)(2,1)}, u32[]{:S(2)}, u32[]{:S(2)}) collective-permute-start(bf16[2,256,256]{2,1,0:T(8,128)(2,1)} %get-tuple-element.31), channel_id=1, source_target_pairs={{0,16},{1,65},{2,18},{3,67},{4,20},{5,69},{6,22},{7,71},{8,24},{9,... | collective-permute-start | bytes 786440 | tf_op jit(solution)/shard_map/ppermute | solution.py:226

commit v2 on v1

v2 whole, which is shorter than its diff:
```python
import functools

import jax
import jax.numpy as jnp
from jax import lax
from jax.experimental import pallas as pl
from jax.experimental.pallas import tpu as pltpu
from jax.sharding import Mesh
from jax.sharding import PartitionSpec as P

LOG2E = 1.4426950408889634
RING = 4
NT = (((1,), (1,)), ((), ()))
NN = (((1,), (0,)), ((), ()))
TN = (((0,), (0,)), ((), ()))
WIDE = ("x", "y", "z")
BF = jnp.bfloat16
F32 = jnp.float32


def score_kernel(
    place, scalars, own, ring_a, ring_b, ring_c, over_a, over_b, over_c, line, second_1, second_2, second_3,
    keep_2, keep_late, keep_early, own_out, give_2, give_early, give_late,
    item_keep, item_give_1, item_give_2, item_give_3, sums,
    users, items, uacc, iacc, ugive, igive, eye, jobs, rows_low, rows_int, table, in_sem, out_sem, table_sem,
):
    my_x, my_y, my_z, core = place[0], place[1], place[2], place[3]
    blocks, half, width = keep_2.shape
    mine = pl.multiple_of(core * half, half)
    other = pl.multiple_of((1 - core) * half, half)
    near = jnp.where(core == 0, 1, RING - 1)
    far = RING - near
    body_rows = blocks * half
    lists = []
    for k, (packet, first, d) in enumerate(
            [(own, 2 * body_rows, 0), (ring_a, body_rows, near), (over_a, body_rows, far), (ring_c, body_rows, 2)]):
        to = rows_low.at[pl.ds(pl.multiple_of(d * 16, 16), 16), :]
        lists.append(pltpu.make_async_copy(packet.at[pl.ds(first, 16), :], to, table_sem.at[k]))
    for c in lists:
        c.start()
    copies = []
    n = line.shape[0]
    for k, piece in enumerate([line, second_1, second_2, second_3]):
        copies.append(pltpu.make_async_copy(piece, items.at[pl.ds(k * n, n)], in_sem.at[k]))
    moves = [(own, 0, 0, 0), (own, body_rows, 0, half), (ring_a, 0, near, mine), (ring_b, 0, near, other),
             (over_a, 0, far, other), (over_b, 0, far, mine), (ring_c, 0, 2, mine), (over_c, 0, 2, other)]
    for k, (packet, first, d, at) in enumerate(moves):
        for b in range(blocks):
            copies.append(pltpu.make_async_copy(
                packet.at[pl.ds(first + b * half, half), :],
                users.at[d * blocks + b, pl.ds(at, half), :], in_sem.at[4 + k * blocks + b]))
    for c in copies:
        c.start()

    for c in lists:
        c.wait()
    rows_int[...] = rows_low[...].astype(F32).astype(jnp.int32)
    to_smem = pltpu.make_async_copy(rows_int, table, table_sem.at[4])
    to_smem.start()
    uacc[...] = jnp.zeros_like(uacc)
    iacc[...] = jnp.zeros_like(iacc)
    row = lax.broadcasted_iota(jnp.int32, (128, 128), 0)
    col = lax.broadcasted_iota(jnp.int32, (128, 128), 1)
    eye[...] = (row == col).astype(F32)
    to_smem.wait()
    count = jnp.int32(0)
    for d in range(RING):
        live_slots = table[16 * d + 3, 0]

        def list_slot(slot, count, d=d, live_slots=live_slots):
            user, item, label = table[16 * d, slot], table[16 * d + 1, slot], table[16 * d + 2, slot]
            dx = (my_x - (item >> 5)) & 3
            dy = (my_y - (item >> 3)) & 3
            first = jnp.where(core == 0, dy, dx)
            second = jnp.where(core == 0, dx, dy)
            jobs[count] = d * blocks + (user & (blocks - 1))
            jobs[count + 72] = (second * RING + first) * 2 + (item & 1)
            jobs[count + 144] = label
            live = (((item >> 1) & 3) == my_z) & (slot < live_slots)
            return count + live.astype(jnp.int32)

        count = lax.fori_loop(0, 64, list_slot, count, unroll=4)
    jobs[count] = 0
    jobs[count + 72] = 0
    jobs[count + 144] = 0
    for c in copies:
        c.wait()

    slope, shift, gain = scalars[0], scalars[1], scalars[2]

    def tile(u, it, slope_j, shift_j, label_j):
        inner = lax.dot_general(u, it, NT, preferred_element_type=F32)
        x = inner * slope_j + shift_j
        e = jnp.exp2(-jnp.abs(x))
        t = 1.0 + e
        high = x >= 0.0
        num = jnp.where(high, 1.0, e)
        soft = jnp.maximum(x, 0.0)
        if label_j is not None:
            hit = eye[...] * label_j > 0.5
            nums, softs = [], []
            for q in range(2):
                r = slice(q * 128, (q + 1) * 128)
                xb, eb = x[r, r], e[r, r]
                nb = jnp.where(hit, jnp.where(high[r, r], -eb, -1.0), num[r, r])
                sb = soft[r, r] - jnp.where(hit, xb, 0.0)
                keep = slice((1 - q) * 128, (2 - q) * 128)
                nums.append(jnp.concatenate([nb, num[r, keep]] if q == 0 else [num[r, keep], nb], axis=1))
                softs.append(jnp.concatenate([sb, soft[r, keep]] if q == 0 else [soft[r, keep], sb], axis=1))
            num = jnp.concatenate(nums, axis=0)
            soft = jnp.concatenate(softs, axis=0)
        w = num * pl.reciprocal(t, approx=True)
        scaled = (w * gain).astype(BF)
        tt = t.reshape(8, 32, 256)
        ee = e.reshape(8, 32, 256)
        prod = ee[0]
        for m in range(1, 8):
            prod = prod * tt[m] + ee[m]
        pr = prod.reshape(4, 8, 256)
        p0 = pr[0] + pr[1] + pr[0] * pr[1]
        p1 = pr[2] + pr[3] + pr[2] * pr[3]
        p = p0 + p1 + p0 * p1
        logs = jnp.where(p < 1e-3, p * (1.0 - 0.5 * p), jnp.log(1.0 + p))
        soft_sum = soft.reshape(32, 8, 256).sum(0)
        w_sum = w.reshape(32, 8, 256).sum(0)
        return scaled, soft_sum, logs, w_sum

    def one_job(j, valid, carry):
        soft_acc, log_acc, w_acc = carry
        ui, ii = jobs[j], jobs[j + 72]
        label_j = jobs[j + 144].astype(F32)
        slope_j = jnp.where(valid, slope, 0.0)
        shift_j = jnp.where(valid, shift, -1e30)
        label_j = jnp.where(valid, label_j, 0.0)
        it = items[ii]
        um = users[ui, pl.ds(mine, half), :]
        uo = users[ui, pl.ds(other, half), :]
        sm, a0, l0, w0 = tile(um, it, slope_j, shift_j, label_j)
        so, a1, l1, w1 = tile(uo, it, slope_j, shift_j, None)
        uacc[ui, pl.ds(mine, half), :] += lax.dot_general(sm, it, NN, preferred_element_type=F32)
        uacc[ui, pl.ds(other, half), :] += lax.dot_general(so, it, NN, preferred_element_type=F32)
        iacc[ii] += (lax.dot_general(sm, um, TN, preferred_element_type=F32)
                     + lax.dot_general(so, uo, TN, preferred_element_type=F32))
        return soft_acc + (a0 + a1), log_acc + (l0 + l1), w_acc + (w0 + w1)

    def two_jobs(g, carry):
        carry = one_job(2 * g, True, carry)
        return one_job(2 * g + 1, 2 * g + 1 < count, carry)

    zero = jnp.zeros((8, 256), F32)
    soft_acc, log_acc, w_acc = lax.fori_loop(0, (count + 1) // 2, two_jobs, (zero, zero, zero))

    serve = far
    give = near
    out = []

    def send(src, dst):
        c = pltpu.make_async_copy(src, dst, out_sem.at[len(out)])
        c.start()
        out.append(c)

    def rows_of(d, at):
        return uacc.at[pl.ds(d * blocks, blocks), pl.ds(at, half), :]

    def lower(d, at, slot):
        def one(b, none):
            ugive[slot * blocks + b] = uacc[d * blocks + b, pl.ds(at, half), :].astype(BF)
            return none
        lax.fori_loop(0, blocks, one, 0)

    lower(2, other, 0)
    send(ugive.at[pl.ds(0, blocks)], give_2)
    lower(give, mine, 1)
    send(ugive.at[pl.ds(blocks, blocks)], give_early)
    lower(give, other, 2)
    send(ugive.at[pl.ds(2 * blocks, blocks)], give_late)
    send(rows_of(2, mine), keep_2)
    send(rows_of(serve, other), keep_early)
    send(rows_of(serve, mine), keep_late)
    send(uacc.at[pl.ds(0, blocks)], own_out)
    for k, dst in enumerate([item_give_1, item_give_2, item_give_3]):
        def item_out(b, none, k=k):
            igive[k * n + b] = iacc[(k + 1) * n + b].astype(BF)
            return none
        lax.fori_loop(0, n, item_out, 0)
        send(igive.at[pl.ds(k * n, n)], dst)
    send(iacc.at[pl.ds(0, n)], item_keep)

    def scale_sum(b, acc):
        prod = uacc[b] * users[b].astype(F32)
        return acc + prod.reshape(64, 8, 256).sum(0)

    scale_acc = lax.fori_loop(0, RING * blocks, scale_sum, zero)
    total = [soft_acc * (1.0 / LOG2E) + log_acc, scale_acc * scalars[3], w_acc]
    lane = lax.broadcasted_iota(jnp.int32, (8, 128), 1)
    packed = jnp.zeros((8, 128), F32)
    for k in range(3):
        packed = jnp.where(lane == k, jnp.sum(total[k]), packed)
    packed = jnp.where(lane == 3, 0.5 * table[3, 0].astype(F32), packed)
    sums[...] = packed
    for c in out:
        c.wait()


def score(place, scalars, pieces):
    n, half, width = pieces[7].shape
    blocks = 4
    height = 2 * half
    n_users, n_items = RING * blocks, RING * n
    smem = pl.BlockSpec(memory_space=pltpu.SMEM)
    any_ = pl.BlockSpec(memory_space=pl.ANY)
    part = (blocks, half, width)
    return pl.pallas_call(
        score_kernel,
        in_specs=[smem, smem] + [any_] * 11,
        out_specs=[any_] * 11 + [pl.BlockSpec(memory_space=pltpu.VMEM)],
        out_shape=[jax.ShapeDtypeStruct(part, F32)] * 3 + [jax.ShapeDtypeStruct((blocks, height, width), F32)]
        + [jax.ShapeDtypeStruct(part, BF)] * 3
        + [jax.ShapeDtypeStruct((n, half, width), F32)] + [jax.ShapeDtypeStruct((n, half, width), BF)] * 3
        + [jax.ShapeDtypeStruct((8, 128), F32)],
        scratch_shapes=[
            pltpu.VMEM((n_users, height, width), BF),
            pltpu.VMEM((n_items, half, width), BF),
            pltpu.VMEM((n_users, height, width), F32),
            pltpu.VMEM((n_items, half, width), F32),
            pltpu.VMEM((3 * blocks, half, width), BF),
            pltpu.VMEM((n_items - n, half, width), BF),
            pltpu.VMEM((128, 128), F32),
            pltpu.SMEM((256,), jnp.int32),
            pltpu.VMEM((64, width), BF),
            pltpu.VMEM((64, width), jnp.int32),
            pltpu.SMEM((64, width), jnp.int32),
            pltpu.SemaphoreType.DMA((40,)),
            pltpu.SemaphoreType.DMA((16,)),
            pltpu.SemaphoreType.DMA((5,)),
        ],
        compiler_params=pltpu.CompilerParams(vmem_limit_bytes=56 * 2**20),
        cost_estimate=pl.CostEstimate(flops=13 * 10**9, bytes_accessed=20 * 2**20, transcendentals=2 * 10**7),
    )(place, scalars, *pieces)


def device(x, y, z, core):
    return (((x % RING) * RING + y % RING) * RING + z % RING) * 2 + core


def every():
    return [(x, y, z, c) for x in range(RING) for y in range(RING) for z in range(RING) for c in range(2)]


AXES = ("x", "y", "z", "n")


def along_z(a):
    return lax.ppermute(a, AXES, [
        (device(x, y, z, c), device(x, y, z + (-1 if c else 1), c)) for x, y, z, c in every()])


def swap(a, bit):
    return lax.ppermute(a, AXES, [(i, i ^ bit) for i in range(128)])


def along_first(a, d):
    return lax.ppermute(a, AXES, [
        (device(x, y, z, c), device(x + (d if c else 0), y + (0 if c else d), z, c)) for x, y, z, c in every()])


def along_second(a, d):
    return lax.ppermute(a, AXES, [
        (device(x, y, z, c), device(x + (0 if c else d), y + (d if c else 0), z, c)) for x, y, z, c in every()])


def across(a):
    return lax.ppermute(a, AXES, [(device(x, y, z, c), device(x, y, z, 1 - c)) for x, y, z, c in every()])


def body(user_emb, item_emb, pairs, counts, natural_exponent_param, additive_shift_param):
    my_x, my_y, my_z = lax.axis_index("x"), lax.axis_index("y"), lax.axis_index("z")
    core = lax.axis_index("n")
    blocks, height, width = user_emb.shape
    half = height // 2
    sharpness = jnp.exp(natural_exponent_param[0])
    shift = additive_shift_param[0]
    place = jnp.stack([my_x, my_y, my_z, core]).astype(jnp.int32)
    scalars = jnp.stack([sharpness * LOG2E, shift * LOG2E, sharpness * height ** -0.5, jnp.float32(height ** 0.5)])

    slots = pairs.shape[1]
    rows = jnp.concatenate([pairs[0].T, jnp.broadcast_to(counts[:, None], (1, slots))], axis=0)
    rows = jnp.pad(rows.astype(F32), ((0, 12), (0, width - slots))).astype(BF)
    lower = [user_emb[:, :half].astype(BF).reshape(blocks * half, width),
             user_emb[:, half:].astype(BF).reshape(blocks * half, width)]
    own = jnp.concatenate(lower + [rows], axis=0)
    items_low = item_emb.astype(BF)
    halves = user_emb.reshape(blocks, 2, half, width)
    mine = lax.dynamic_index_in_dim(halves, core, 1, keepdims=False).astype(BF).reshape(blocks * half, width)
    other = lax.dynamic_index_in_dim(halves, 1 - core, 1, keepdims=False).astype(BF).reshape(blocks * half, width)

    ring_a = along_z(jnp.concatenate([mine, rows], axis=0))
    ring_b = along_z(other)
    ring_c = along_z(ring_a)
    over_a, over_b, over_c = across(ring_a), across(ring_b), across(ring_c)
    line = jnp.concatenate([items_low] + [along_first(items_low, d) for d in (1, 2, 3)], axis=0)
    second = [along_second(line, d) for d in (1, 2, 3)]

    (keep_2, keep_late, keep_early, own_part, give_2, give_early, give_late,
     item_keep, item_give_1, item_give_2, item_give_3, sums) = score(
        place, scalars, [own, ring_a, ring_b, ring_c, over_a, over_b, over_c, line] + second)

    for bit in (1, 2, 4, 8, 16, 32, 64):
        sums = sums + swap(sums, bit)
    totals = sums[0]
    objective = totals[:3] / (height * height * totals[3])

    back = [along_second(g, -d) for d, g in ((1, item_give_1), (2, item_give_2), (3, item_give_3))]
    item_line = item_keep + back[0].astype(F32) + back[1].astype(F32) + back[2].astype(F32)
    back = [along_first(item_line[2 * d: 2 * d + 2].astype(BF), -d) for d in (1, 2, 3)]
    item_grad = item_line[:2] + back[0].astype(F32) + back[1].astype(F32) + back[2].astype(F32)

    relay = along_z((keep_2 + across(give_2).astype(F32)).astype(BF))
    early = along_z((keep_early + across(give_early).astype(F32)).astype(BF))
    late = along_z((keep_late + across(give_late).astype(F32) + relay.astype(F32)).astype(BF))
    own_sum = own_part + across(own_part)
    early_over, late_over = across(early), across(late)
    first_core = core == 0
    low_a, low_b = jnp.where(first_core, late, late_over), jnp.where(first_core, early_over, early)
    high_a, high_b = jnp.where(first_core, early, early_over), jnp.where(first_core, late_over, late)
    user_grad = own_sum + jnp.concatenate(
        [low_a.astype(F32) + low_b.astype(F32), high_a.astype(F32) + high_b.astype(F32)], axis=1)
    return user_grad, item_grad, objective


def solution(mesh):
    grid = Mesh(mesh.devices.reshape(RING, RING, RING, 2), AXES)
    return jax.shard_map(
        body,
        mesh=grid,
        in_specs=(P(WIDE, None, None), P(WIDE, "n", None), P(WIDE, None, None), P(WIDE), P(), P()),
        out_specs=(P(WIDE, None, None), P(WIDE, "n", None), P()),
        check_vma=False,
    )
```

time: 242 us -> 188 us (0.78)
  blocking collectives: 63.2 us -> 0 us
  waiting for transfers between devices: 46.1 us -> 77 us
  local copies, waits for them, and re-layouts: 24.6 us -> 4.69 us
  other arithmetic: 20.9 us -> 13.7 us
  starting transfers between devices: 28.4 us -> 34.3 us
    psum x1 -> x0, blocking collectives: 63.2 us -> none  [body(): totals = lax.psum(totals, AXES)]
    ppermute x6, waiting for transfers between devices: 5.5 us -> 30.3 us  [along_second(): lax.ppermute(a, AXES, [(device(x, y, z, c), device(x + (0 if c else d), y...]
    unnamed x22 -> x17, local copies, waits for them, and re-layouts: 9.74 us -> 1.52 us
    another operation x2 -> x3, other arithmetic: 7.91 us -> 0.58 us
    ppermute x6 -> x13, starting transfers between devices: 7.43 us -> 14.1 us  [the longest x7 8.71 us: swap(): return lax.ppermute(a, AXES, [(i, i ^ bit) for i in range(128)])]
    slice x9 -> x1, local copies, waits for them, and re-layouts: 6.65 us -> 0.07 us  [body(): user_emb[:, :half].astype(BF).reshape(blocks * half, width)]
    ppermute x6, waiting for transfers between devices: 0.02 us -> 6.51 us  [along_first(): lax.ppermute(a, AXES, [(device(x, y, z, c), device(x + (d if c else 0), y...]
    concatenate x2 -> x0, local copies, waits for them, and re-layouts: 5.3 us -> none  [the longest x1 3.05 us: body(): jnp.concatenate([v[:slots * 3] for v in lists] + [v[slots * 3:] for v in...]
  transfers between devices with their start and end apart: 21 -> 34, of which waited for: 5 -> 16; matrix products, arithmetic and copies ran while one was open for 14% -> 6% of each run, Pallas kernels for 0% -> 0%
where the time goes in v2:
time: 188 us; the launch traced here: 187 us
  waiting for transfers between devices  77 us (41%)
  Pallas kernels  53.9 us (29%)
  starting transfers between devices  34.3 us (18%)
  other arithmetic  13.7 us (7%)
  local copies, waits for them, and re-layouts  4.69 us (2%)
  between operations  3.52 us (2%)
    pallas_call x1, Pallas kernels, score(): pl.pallas_call(score_kernel, in_specs=[smem, smem] + [any_] * 11, out_spe...  53.9 us
    ppermute x6, waiting for transfers between devices, along_second(): lax.ppermute(a, AXES, [(device(x, y, z, c), device(x + (0 if c else d), y...  30.3 us
    ppermute x6, waiting for transfers between devices, along_z(): lax.ppermute(a, AXES, [(device(x, y, z, c), device(x, y, z + (-1 if c els...  21.4 us
    ppermute x7, waiting for transfers between devices, swap(): return lax.ppermute(a, AXES, [(i, i ^ bit) for i in range(128)])  18.8 us
    ppermute x6, starting transfers between devices, along_second(): lax.ppermute(a, AXES, [(device(x, y, z, c), device(x + (0 if c else d), y...  9.25 us
    ppermute x7, starting transfers between devices, swap(): return lax.ppermute(a, AXES, [(i, i ^ bit) for i in range(128)])  8.71 us
    ppermute x6, starting transfers between devices, along_first(): lax.ppermute(a, AXES, [(device(x, y, z, c), device(x + (d if c else 0), y...  7.77 us
    ppermute x6, waiting for transfers between devices, along_first(): lax.ppermute(a, AXES, [(device(x, y, z, c), device(x + (d if c else 0), y...  6.51 us
  transfers between devices with their start and end apart: 34, of which 16 were waited for; matrix products, arithmetic and copies ran while one was open for 6% of the time, Pallas kernels for 0%

profile of v2, /device:TPU:0, one launch (start us, length us, event | category | flops | bytes accessed | tf_op | source)
XLA Modules:
  0.0 187.2 jit_solution(14808455348416410359)
XLA Ops:
  1.3 0.7 copy.15
  2.1 1.7 bitcast_convert_fusion
  3.7 0.0 copy-start
  3.8 2.1 %collective-permute-start = (bf16[1040,256]{1,0:T(8,128)(2,1)S(1)}, bf16[1040,256]{1,0:T(8,128)(2,1)}, u32[]{:S(2)}, u32[]{:S(2)}) collective-permute-start(bf16[1040,256]{1,0:T(8,128)(2,1)S(1)} %pad_maximum_fusion.2), channel_id=1, source_target_pairs={{0,2},{1,7},{2,4},{3,1},{4,6},{5,3},{6,0},{7,5},{8,10},{9,15},{10,... | collective-permute-start | bytes 1597448 | tf_op jit(solution)/shard_map/ppermute | solution.py:254
  5.8 1.9 %collective-permute-start.1 = (bf16[1024,256]{1,0:T(8,128)(2,1)S(1)}, bf16[1024,256]{1,0:T(8,128)(2,1)}, u32[]{:S(2)}, u32[]{:S(2)}) collective-permute-start(bf16[1024,256]{1,0:T(8,128)(2,1)S(1)} %bitcast.27), channel_id=1, source_target_pairs={{0,2},{1,7},{2,4},{3,1},{4,6},{5,3},{6,0},{7,5},{8,10},{9,15},{10,... | collective-permute-start | bytes 1572872 | tf_op jit(solution)/shard_map/ppermute | solution.py:254
  7.8 3.1 %collective-permute-start.8 = (bf16[2,256,256]{2,1,0:T(8,128)(2,1)S(1)}, bf16[2,256,256]{2,1,0:T(8,128)(2,1)S(1)}, u32[]{:S(2)}, u32[]{:S(2)}) collective-permute-start(bf16[2,256,256]{2,1,0:T(8,128)(2,1)S(1)} %convert_element_type.84), channel_id=1, source_target_pairs={{0,24},{1,97},{2,26},{3,99},{4,28},{5,101},{6,30},{7,103},{8,0},{9... | collective-permute-start | bytes 786440 | tf_op jit(solution)/shard_map/ppermute | solution.py:263
  10.9 0.6 collective-permute-start.7
  11.5 1.0 collective-permute-start.6
  12.5 8.5 %collective-permute-done.1.ring_b = bf16[1024,256]{1,0:T(8,128)(2,1)} collective-permute-done((bf16[1024,256]{1,0:T(8,128)(2,1)S(1)}, bf16[1024,256]{1,0:T(8,128)(2,1)}, u32[]{:S(2)}, u32[]{:S(2)}) %collective-permute-start.1) | collective-permute-done | bytes 524320 | tf_op jit(solution)/shard_map/ppermute | solution.py:254
  21.0 0.6 collective-permute-done.6
  21.6 1.1 pad_maximum_fusion.1.line
  22.7 2.8 %collective-permute-start.11 = (bf16[8,256,256]{2,1,0:T(8,128)(2,1)}, bf16[8,256,256]{2,1,0:T(8,128)(2,1)}, u32[]{:S(2)}, u32[]{:S(2)}) collective-permute-start(bf16[8,256,256]{2,1,0:T(8,128)(2,1)} %pad_maximum_fusion.1.line), channel_id=1, source_target_pairs={{0,96},{1,25},{2,98},{3,27},{4,100},{5,29},{6,102},{7,31},{8,104},... | collective-permute-start | bytes 3145736 | tf_op jit(solution)/shard_map/ppermute | solution.py:268
  25.4 0.8 collective-permute-start.10
  26.2 0.9 collective-permute-start.9
  27.1 0.1 convert.13
  27.2 0.1 fusion.4
  27.3 1.0 collective-permute-start.3
  28.4 3.4 %collective-permute-done.2.ring_c = bf16[1040,256]{1,0:T(8,128)(2,1)} collective-permute-done((bf16[1040,256]{1,0:T(8,128)(2,1)}, bf16[1040,256]{1,0:T(8,128)(2,1)}, u32[]{:S(2)}, u32[]{:S(2)}) %collective-permute-start.2) | collective-permute-done | bytes 532512 | tf_op jit(solution)/shard_map/ppermute | solution.py:254
  31.7 0.7 pad_add_fusion.place
  33.7 0.6 pad_maximum_fusion.3.scalars
  34.3 1.0 pad_maximum_fusion.own
  35.4 14.0 %collective-permute-done.11.second_3 = bf16[8,256,256]{2,1,0:T(8,128)(2,1)} collective-permute-done((bf16[8,256,256]{2,1,0:T(8,128)(2,1)}, bf16[8,256,256]{2,1,0:T(8,128)(2,1)}, u32[]{:S(2)}, u32[]{:S(2)}) %collective-permute-start.11) | collective-permute-done | bytes 1048608 | tf_op jit(solution)/shard_map/ppermute | solution.py:268
  49.3 3.9 %collective-permute-done.9.second_1 = bf16[8,256,256]{2,1,0:T(8,128)(2,1)} collective-permute-done((bf16[8,256,256]{2,1,0:T(8,128)(2,1)}, bf16[8,256,256]{2,1,0:T(8,128)(2,1)}, u32[]{:S(2)}, u32[]{:S(2)}) %collective-permute-start.9) | collective-permute-done | bytes 1048608 | tf_op jit(solution)/shard_map/ppermute | solution.py:268
  53.3 0.8 copy-done.7
  54.1 53.9 %shard_map.85 = (f32[4,256,256]{2,1,0:T(8,128)}, f32[4,256,256]{2,1,0:T(8,128)}, f32[4,256,256]{2,1,0:T(8,128)}, f32[4,512,256]{2,1,0:T(8,128)}, bf16[4,256,256]...) custom-call(s32[4]{0:T(128)} %pad_add_fusion.place, ...), custom_call_target="tpu_custom_call" | custom-call | flops 12999999488 | bytes 20971520 | tf_op jit(solution)/shard_map/pallas_call | solution.py:213
  108.0 0.5 collective-permute-start.14
  108.6 0.1 collective-permute-start.13
  108.7 0.4 collective-permute-start.18
  109.1 2.8 %collective-permute-start.21 = (bf16[8,256,256]{2,1,0:T(8,128)(2,1)}, bf16[8,256,256]{2,1,0:T(8,128)(2,1)S(1)}, u32[]{:S(2)}, u32[]{:S(2)}) collective-permute-start(bf16[8,256,256]{2,1,0:T(8,128)(2,1)} %get-tuple-element.23), channel_id=1, source_target_pairs={{0,96},{1,25},{2,98},{3,27},{4,100},{5,29},{6,102},{7,31},{8,104},... | collective-permute-start | bytes 3145736 | tf_op jit(solution)/shard_map/ppermute | solution.py:268
  111.9 2.0 %collective-permute-start.22 = (bf16[8,256,256]{2,1,0:T(8,128)(2,1)}, bf16[8,256,256]{2,1,0:T(8,128)(2,1)S(1)}, u32[]{:S(2)}, u32[]{:S(2)}) collective-permute-start(bf16[8,256,256]{2,1,0:T(8,128)(2,1)} %get-tuple-element.24), channel_id=1, source_target_pairs={{0,64},{1,17},{2,66},{3,19},{4,68},{5,21},{6,70},{7,23},{8,72},{9,... | collective-permute-start | bytes 3145736 | tf_op jit(solution)/shard_map/ppermute | solution.py:268
  113.9 1.4 add_convert_fusion.2
  115.4 0.1 collective-permute-start.15
  115.5 0.6 collective-permute-start.12
  116.1 0.1 add_convert_fusion
  116.2 9.6 %collective-permute-done.15 = bf16[4,256,256]{2,1,0:T(8,128)(2,1)S(1)} collective-permute-done((bf16[4,256,256]{2,1,0:T(8,128)(2,1)S(1)}, bf16[4,256,256]{2,1,0:T(8,128)(2,1)S(1)}, u32[]{:S(2)}, u32[]{:S(2)}) %collective-permute-start.15) | collective-permute-done | bytes 524320 | tf_op jit(solution)/shard_map/ppermute | solution.py:254
  125.8 0.2 add_convert_fusion.1
  126.0 9.8 %collective-permute-done.21 = bf16[8,256,256]{2,1,0:T(8,128)(2,1)S(1)} collective-permute-done((bf16[8,256,256]{2,1,0:T(8,128)(2,1)}, bf16[8,256,256]{2,1,0:T(8,128)(2,1)S(1)}, u32[]{:S(2)}, u32[]{:S(2)}) %collective-permute-start.21) | collective-permute-done | bytes 1048608 | tf_op jit(solution)/shard_map/ppermute | solution.py:268
  135.8 1.2 collective-permute-start.16
  137.0 2.6 %collective-permute-done.23 = bf16[8,256,256]{2,1,0:T(8,128)(2,1)S(1)} collective-permute-done((bf16[8,256,256]{2,1,0:T(8,128)(2,1)}, bf16[8,256,256]{2,1,0:T(8,128)(2,1)S(1)}, u32[]{:S(2)}, u32[]{:S(2)}) %collective-permute-start.23) | collective-permute-done | bytes 1048608 | tf_op jit(solution)/shard_map/ppermute | solution.py:268
  139.6 0.5 fusion.2
  140.1 0.9 fusion.3
  140.9 0.6 collective-permute-start.24
  141.5 1.2 collective-permute-done.27
  142.7 1.8 collective-permute-start.28
  144.4 1.9 collective-permute-done.28
  146.3 3.4 %collective-permute-start.29 = (f32[8,128]{1,0:T(8,128)S(1)}, f32[8,128]{1,0:T(8,128)S(1)}, u32[]{:S(2)}, u32[]{:S(2)}) collective-permute-start(f32[8,128]{1,0:T(8,128)S(1)} %add.92), channel_id=1, source_target_pairs={{0,4},{1,5},{2,6},{3,7},{4,0},{5,1},{6,2},{7,3},{8,12},{9,13},{10,... | collective-permute-start | bytes 12296 | tf_op jit(solution)/shard_map/ppermute | solution.py:259
  149.7 1.7 collective-permute-done.29
  151.4 1.4 collective-permute-start.30
  152.9 2.2 %collective-permute-done.30 = f32[8,128]{1,0:T(8,128)S(1)} collective-permute-done((f32[8,128]{1,0:T(8,128)S(1)}, f32[8,128]{1,0:T(8,128)S(1)}, u32[]{:S(2)}, u32[]{:S(2)}) %collective-permute-start.30) | collective-permute-done | bytes 4128 | tf_op jit(solution)/shard_map/ppermute | solution.py:259
  155.0 0.6 collective-permute-start.31
  155.7 4.5 %collective-permute-done.31 = f32[8,128]{1,0:T(8,128)S(1)} collective-permute-done((f32[8,128]{1,0:T(8,128)S(1)}, f32[8,128]{1,0:T(8,128)S(1)}, u32[]{:S(2)}, u32[]{:S(2)}) %collective-permute-start.31) | collective-permute-done | bytes 4128 | tf_op jit(solution)/shard_map/ppermute | solution.py:259
  160.1 0.0 collective-permute-start.32
  160.1 3.6 %collective-permute-done.32 = f32[8,128]{1,0:T(8,128)S(1)} collective-permute-done((f32[8,128]{1,0:T(8,128)S(1)}, f32[8,128]{1,0:T(8,128)S(1)}, u32[]{:S(2)}, u32[]{:S(2)}) %collective-permute-start.32) | collective-permute-done | bytes 4128 | tf_op jit(solution)/shard_map/ppermute | solution.py:259
  163.8 1.4 collective-permute-start.33
  165.2 3.9 %collective-permute-done.33 = f32[8,128]{1,0:T(8,128)S(1)} collective-permute-done((f32[8,128]{1,0:T(8,128)S(1)}, f32[8,128]{1,0:T(8,128)S(1)}, u32[]{:S(2)}, u32[]{:S(2)}) %collective-permute-start.33) | collective-permute-done | bytes 4128 | tf_op jit(solution)/shard_map/ppermute | solution.py:259
  169.1 1.4 collective-permute-start.26
  170.5 1.1 collective-permute-start.25
  171.6 0.5 collective-permute-start.17
  172.1 0.6 slice.41
  173.3 0.5 divide_bitcast_fusion
  173.9 5.9 %collective-permute-done.26 = bf16[2,256,256]{2,1,0:T(8,128)(2,1)} collective-permute-done((bf16[2,256,256]{2,1,0:T(8,128)(2,1)}, bf16[2,256,256]{2,1,0:T(8,128)(2,1)}, u32[]{:S(2)}, u32[]{:S(2)}) %collective-permute-start.26) | collective-permute-done | bytes 262176 | tf_op jit(solution)/shard_map/ppermute | solution.py:263
  179.8 1.9 %fusion.1 = f32[2,256,256]{2,1,0:T(8,128)} fusion(f32[8,256,256]{2,1,0:T(8,128)S(1)} %get-tuple-element.28, bf16[2,256,256]{2,1,0:T(8,128)(2,1)} %collective-permute-done.26, bf16[2,256,256]{2,1,0:T(8,128)(2,1)} %collective-permute-done.25, bf16[2,256,256]{2,1,0:T(8,128)(2,1)S(1)} %collective-permute-done.24), kind=kLoop, calls=%fused_computation.14 | loop fusion | flops 786432 | bytes 1835008 | tf_op jit(solution)/shard_map/add | solution.py:316
  181.7 1.5 convert_add_fusion.2
  183.3 4.0 %maximum_add_fusion = f32[4,512,256]{2,1,0:T(8,128)} fusion(f32[4,256,256]{2,1,0:T(8,128)S(1)} %get-tuple-element.30, f32[4,256,256]{2,1,0:T(8,128)S(1)} %get-tuple-element.29, f32[4,512,256]{2,1,0:T(8,128)} %get-tuple-element.15, f32[4,512,256]{2,1,0:T(8,128)} %collective-permute-done.12), kind=kLoop, calls=%fused_computation | loop fusion | flops 1572864 | bytes 8388608 | tf_op jit(solution)/shard_map/add | solution.py:326
  (50 shorter events, 0.2 us)
Async XLA Ops:
  0.6 7.1 %copy-start.4 = (f32[2,256,256]{2,1,0:T(8,128)S(1)}, f32[2,256,256]{2,1,0:T(8,128)}, u32[]{:S(2)}) copy-start(f32[2,256,256]{2,1,0:T(8,128)} %param.7) | copy-start | bytes 1572868
  3.7 23.4 %copy-start = (f32[4,512,256]{2,1,0:T(8,128)S(1)}, f32[4,512,256]{2,1,0:T(8,128)}, u32[]{:S(2)}) copy-start(f32[4,512,256]{2,1,0:T(8,128)} %param.6) | copy-start | bytes 6291460
  3.8 17.2 %collective-permute-start = (bf16[1040,256]{1,0:T(8,128)(2,1)S(1)}, bf16[1040,256]{1,0:T(8,128)(2,1)}, u32[]{:S(2)}, u32[]{:S(2)}) collective-permute-start(bf16[1040,256]{1,0:T(8,128)(2,1)S(1)} %pad_maximum_fusion.2), channel_id=1, source_target_pairs={{0,2},{1,7},{2,4},{3,1},{4,6},{5,3},{6,0},{7,5},{8,10},{9,15},{10,... | collective-permute-start | bytes 1597448 | tf_op jit(solution)/shard_map/ppermute | solution.py:254
  5.8 15.1 %collective-permute-start.1 = (bf16[1024,256]{1,0:T(8,128)(2,1)S(1)}, bf16[1024,256]{1,0:T(8,128)(2,1)}, u32[]{:S(2)}, u32[]{:S(2)}) collective-permute-start(bf16[1024,256]{1,0:T(8,128)(2,1)S(1)} %bitcast.27), channel_id=1, source_target_pairs={{0,2},{1,7},{2,4},{3,1},{4,6},{5,3},{6,0},{7,5},{8,10},{9,15},{10,... | collective-permute-start | bytes 1572872 | tf_op jit(solution)/shard_map/ppermute | solution.py:254
  7.8 13.2 %collective-permute-start.8 = (bf16[2,256,256]{2,1,0:T(8,128)(2,1)S(1)}, bf16[2,256,256]{2,1,0:T(8,128)(2,1)S(1)}, u32[]{:S(2)}, u32[]{:S(2)}) collective-permute-start(bf16[2,256,256]{2,1,0:T(8,128)(2,1)S(1)} %convert_element_type.84), channel_id=1, source_target_pairs={{0,24},{1,97},{2,26},{3,99},{4,28},{5,101},{6,30},{7,103},{8,0},{9... | collective-permute-start | bytes 786440 | tf_op jit(solution)/shard_map/ppermute | solution.py:263
  10.9 10.1 %collective-permute-start.7 = (bf16[2,256,256]{2,1,0:T(8,128)(2,1)S(1)}, bf16[2,256,256]{2,1,0:T(8,128)(2,1)S(1)}, u32[]{:S(2)}, u32[]{:S(2)}) collective-permute-start(bf16[2,256,256]{2,1,0:T(8,128)(2,1)S(1)} %convert_element_type.84), channel_id=1, source_target_pairs={{0,16},{1,65},{2,18},{3,67},{4,20},{5,69},{6,22},{7,71},{8,24},{9,... | collective-permute-start | bytes 786440 | tf_op jit(solution)/shard_map/ppermute | solution.py:263
  11.5 10.1 %collective-permute-start.6 = (bf16[2,256,256]{2,1,0:T(8,128)(2,1)S(1)}, bf16[2,256,256]{2,1,0:T(8,128)(2,1)S(1)}, u32[]{:S(2)}, u32[]{:S(2)}) collective-permute-start(bf16[2,256,256]{2,1,0:T(8,128)(2,1)S(1)} %convert_element_type.84), channel_id=1, source_target_pairs={{0,8},{1,33},{2,10},{3,35},{4,12},{5,37},{6,14},{7,39},{8,16},{9,4... | collective-permute-start | bytes 786440 | tf_op jit(solution)/shard_map/ppermute | solution.py:263
  20.9 6.4 %collective-permute-start.4 = (bf16[1024,256]{1,0:T(8,128)(2,1)}, bf16[1024,256]{1,0:T(8,128)(2,1)}, u32[]{:S(2)}, u32[]{:S(2)}) collective-permute-start(bf16[1024,256]{1,0:T(8,128)(2,1)} %collective-permute-done.1.ring_b), channel_id=1, source_target_pairs={{0,1},{1,0},{2,3},{3,2},{4,5},{5,4},{6,7},{7,6},{8,9},{9,8},{10,11... | collective-permute-start | bytes 1572872 | tf_op jit(solution)/shard_map/ppermute | solution.py:273
  20.9 10.8 %collective-permute-start.2 = (bf16[1040,256]{1,0:T(8,128)(2,1)}, bf16[1040,256]{1,0:T(8,128)(2,1)}, u32[]{:S(2)}, u32[]{:S(2)}) collective-permute-start(bf16[1040,256]{1,0:T(8,128)(2,1)} %collective-permute-done.ring_a), channel_id=1, source_target_pairs={{0,2},{1,7},{2,4},{3,1},{4,6},{5,3},{6,0},{7,5},{8,10},{9,15},{10,... | collective-permute-start | bytes 1597448 | tf_op jit(solution)/shard_map/ppermute | solution.py:254
  22.7 26.7 %collective-permute-start.11 = (bf16[8,256,256]{2,1,0:T(8,128)(2,1)}, bf16[8,256,256]{2,1,0:T(8,128)(2,1)}, u32[]{:S(2)}, u32[]{:S(2)}) collective-permute-start(bf16[8,256,256]{2,1,0:T(8,128)(2,1)} %pad_maximum_fusion.1.line), channel_id=1, source_target_pairs={{0,96},{1,25},{2,98},{3,27},{4,100},{5,29},{6,102},{7,31},{8,104},... | collective-permute-start | bytes 3145736 | tf_op jit(solution)/shard_map/ppermute | solution.py:268
  25.4 23.9 %collective-permute-start.10 = (bf16[8,256,256]{2,1,0:T(8,128)(2,1)}, bf16[8,256,256]{2,1,0:T(8,128)(2,1)}, u32[]{:S(2)}, u32[]{:S(2)}) collective-permute-start(bf16[8,256,256]{2,1,0:T(8,128)(2,1)} %pad_maximum_fusion.1.line), channel_id=1, source_target_pairs={{0,64},{1,17},{2,66},{3,19},{4,68},{5,21},{6,70},{7,23},{8,72},{9,... | collective-permute-start | bytes 3145736 | tf_op jit(solution)/shard_map/ppermute | solution.py:268
  26.2 27.1 %collective-permute-start.9 = (bf16[8,256,256]{2,1,0:T(8,128)(2,1)}, bf16[8,256,256]{2,1,0:T(8,128)(2,1)}, u32[]{:S(2)}, u32[]{:S(2)}) collective-permute-start(bf16[8,256,256]{2,1,0:T(8,128)(2,1)} %pad_maximum_fusion.1.line), channel_id=1, source_target_pairs={{0,32},{1,9},{2,34},{3,11},{4,36},{5,13},{6,38},{7,15},{8,40},{9,1... | collective-permute-start | bytes 3145736 | tf_op jit(solution)/shard_map/ppermute | solution.py:268
  27.3 8.1 %collective-permute-start.3 = (bf16[1040,256]{1,0:T(8,128)(2,1)}, bf16[1040,256]{1,0:T(8,128)(2,1)S(1)}, u32[]{:S(2)}, u32[]{:S(2)}) collective-permute-start(bf16[1040,256]{1,0:T(8,128)(2,1)} %collective-permute-done.ring_a), channel_id=1, source_target_pairs={{0,1},{1,0},{2,3},{3,2},{4,5},{5,4},{6,7},{7,6},{8,9},{9,8},{10,11... | collective-permute-start | bytes 1597448 | tf_op jit(solution)/shard_map/ppermute | solution.py:273
  31.7 21.5 %collective-permute-start.5 = (bf16[1040,256]{1,0:T(8,128)(2,1)}, bf16[1040,256]{1,0:T(8,128)(2,1)S(1)}, u32[]{:S(2)}, u32[]{:S(2)}) collective-permute-start(bf16[1040,256]{1,0:T(8,128)(2,1)} %collective-permute-done.2.ring_c), channel_id=1, source_target_pairs={{0,1},{1,0},{2,3},{3,2},{4,5},{5,4},{6,7},{7,6},{8,9},{9,8},{10,11... | collective-permute-start | bytes 1597448 | tf_op jit(solution)/shard_map/ppermute | solution.py:273
  35.4 17.9 %copy-start.6 = (bf16[1040,256]{1,0:T(8,128)(2,1)}, bf16[1040,256]{1,0:T(8,128)(2,1)S(1)}, u32[]{:S(2)}) copy-start(bf16[1040,256]{1,0:T(8,128)(2,1)S(1)} %collective-permute-done.3.over_a) | copy-start | bytes 1597444
  53.3 0.8 copy-start.7
  108.0 8.1 %copy-start.3 = (f32[4,256,256]{2,1,0:T(8,128)S(1)}, f32[4,256,256]{2,1,0:T(8,128)}, u32[]{:S(2)}) copy-start(f32[4,256,256]{2,1,0:T(8,128)} %get-tuple-element.20) | copy-start | bytes 3145732
  108.0 5.9 %collective-permute-start.14 = (bf16[4,256,256]{2,1,0:T(8,128)(2,1)}, bf16[4,256,256]{2,1,0:T(8,128)(2,1)S(1)}, u32[]{:S(2)}, u32[]{:S(2)}) collective-permute-start(bf16[4,256,256]{2,1,0:T(8,128)(2,1)} %get-tuple-element.19), channel_id=1, source_target_pairs={{0,1},{1,0},{2,3},{3,2},{4,5},{5,4},{6,7},{7,6},{8,9},{9,8},{10,11... | collective-permute-start | bytes 1572872 | tf_op jit(solution)/shard_map/ppermute | solution.py:273
  108.6 6.8 %collective-permute-start.13 = (bf16[4,256,256]{2,1,0:T(8,128)(2,1)}, bf16[4,256,256]{2,1,0:T(8,128)(2,1)S(1)}, u32[]{:S(2)}, u32[]{:S(2)}) collective-permute-start(bf16[4,256,256]{2,1,0:T(8,128)(2,1)} %get-tuple-element.17), channel_id=1, source_target_pairs={{0,1},{1,0},{2,3},{3,2},{4,5},{5,4},{6,7},{7,6},{8,9},{9,8},{10,11... | collective-permute-start | bytes 1572872 | tf_op jit(solution)/shard_map/ppermute | solution.py:273
  108.7 6.8 %collective-permute-start.18 = (bf16[4,256,256]{2,1,0:T(8,128)(2,1)}, bf16[4,256,256]{2,1,0:T(8,128)(2,1)S(1)}, u32[]{:S(2)}, u32[]{:S(2)}) collective-permute-start(bf16[4,256,256]{2,1,0:T(8,128)(2,1)} %get-tuple-element.21), channel_id=1, source_target_pairs={{0,1},{1,0},{2,3},{3,2},{4,5},{5,4},{6,7},{7,6},{8,9},{9,8},{10,11... | collective-permute-start | bytes 1572872 | tf_op jit(solution)/shard_map/ppermute | solution.py:273
  109.1 26.7 %collective-permute-start.21 = (bf16[8,256,256]{2,1,0:T(8,128)(2,1)}, bf16[8,256,256]{2,1,0:T(8,128)(2,1)S(1)}, u32[]{:S(2)}, u32[]{:S(2)}) collective-permute-start(bf16[8,256,256]{2,1,0:T(8,128)(2,1)} %get-tuple-element.23), channel_id=1, source_target_pairs={{0,96},{1,25},{2,98},{3,27},{4,100},{5,29},{6,102},{7,31},{8,104},... | collective-permute-start | bytes 3145736 | tf_op jit(solution)/shard_map/ppermute | solution.py:268
  111.9 25.2 %collective-permute-start.22 = (bf16[8,256,256]{2,1,0:T(8,128)(2,1)}, bf16[8,256,256]{2,1,0:T(8,128)(2,1)S(1)}, u32[]{:S(2)}, u32[]{:S(2)}) collective-permute-start(bf16[8,256,256]{2,1,0:T(8,128)(2,1)} %get-tuple-element.24), channel_id=1, source_target_pairs={{0,64},{1,17},{2,66},{3,19},{4,68},{5,21},{6,70},{7,23},{8,72},{9,... | collective-permute-start | bytes 3145736 | tf_op jit(solution)/shard_map/ppermute | solution.py:268
  113.9 25.7 %collective-permute-start.23 = (bf16[8,256,256]{2,1,0:T(8,128)(2,1)}, bf16[8,256,256]{2,1,0:T(8,128)(2,1)S(1)}, u32[]{:S(2)}, u32[]{:S(2)}) collective-permute-start(bf16[8,256,256]{2,1,0:T(8,128)(2,1)} %get-tuple-element.25), channel_id=1, source_target_pairs={{0,32},{1,9},{2,34},{3,11},{4,36},{5,13},{6,38},{7,15},{8,40},{9,1... | collective-permute-start | bytes 3145736 | tf_op jit(solution)/shard_map/ppermute | solution.py:268
  113.9 11.9 %copy-start.2 = (f32[4,256,256]{2,1,0:T(8,128)S(1)}, f32[4,256,256]{2,1,0:T(8,128)}, u32[]{:S(2)}) copy-start(f32[4,256,256]{2,1,0:T(8,128)} %get-tuple-element.16) | copy-start | bytes 3145732
  115.4 10.5 %collective-permute-start.15 = (bf16[4,256,256]{2,1,0:T(8,128)(2,1)S(1)}, bf16[4,256,256]{2,1,0:T(8,128)(2,1)S(1)}, u32[]{:S(2)}, u32[]{:S(2)}) collective-permute-start(bf16[4,256,256]{2,1,0:T(8,128)(2,1)S(1)} %add_convert_fusion.2), channel_id=1, source_target_pairs={{0,2},{1,7},{2,4},{3,1},{4,6},{5,3},{6,0},{7,5},{8,10},{9,15},{10,... | collective-permute-start | bytes 1572872 | tf_op jit(solution)/shard_map/ppermute | solution.py:254
  115.5 67.8 %collective-permute-start.12 = (f32[4,512,256]{2,1,0:T(8,128)}, f32[4,512,256]{2,1,0:T(8,128)}, u32[]{:S(2)}, u32[]{:S(2)}) collective-permute-start(f32[4,512,256]{2,1,0:T(8,128)} %get-tuple-element.15), channel_id=1, source_target_pairs={{0,1},{1,0},{2,3},{3,2},{4,5},{5,4},{6,7},{7,6},{8,9},{9,8},{10,11... | collective-permute-start | bytes 6291464 | tf_op jit(solution)/shard_map/ppermute | solution.py:273
  116.1 23.5 %copy-start.1 = (f32[8,256,256]{2,1,0:T(8,128)S(1)}, f32[8,256,256]{2,1,0:T(8,128)}, u32[]{:S(2)}) copy-start(f32[8,256,256]{2,1,0:T(8,128)} %get-tuple-element.22) | copy-start | bytes 6291460
  125.8 44.7 %collective-permute-start.19 = (bf16[4,256,256]{2,1,0:T(8,128)(2,1)S(1)}, bf16[4,256,256]{2,1,0:T(8,128)(2,1)S(1)}, u32[]{:S(2)}, u32[]{:S(2)}) collective-permute-start(bf16[4,256,256]{2,1,0:T(8,128)(2,1)S(1)} %add_convert_fusion), channel_id=1, source_target_pairs={{0,2},{1,7},{2,4},{3,1},{4,6},{5,3},{6,0},{7,5},{8,10},{9,15},{10,... | collective-permute-start | bytes 1572872 | tf_op jit(solution)/shard_map/ppermute | solution.py:254
  135.8 35.8 %collective-permute-start.16 = (bf16[4,256,256]{2,1,0:T(8,128)(2,1)S(1)}, bf16[4,256,256]{2,1,0:T(8,128)(2,1)S(1)}, u32[]{:S(2)}, u32[]{:S(2)}) collective-permute-start(bf16[4,256,256]{2,1,0:T(8,128)(2,1)S(1)} %add_convert_fusion.1), channel_id=1, source_target_pairs={{0,2},{1,7},{2,4},{3,1},{4,6},{5,3},{6,0},{7,5},{8,10},{9,15},{10,... | collective-permute-start | bytes 1572872 | tf_op jit(solution)/shard_map/ppermute | solution.py:254
  139.6 1.9 %copy-start.5 = (f32[8,128]{1,0:T(8,128)S(1)}, f32[8,128]{1,0:T(8,128)}, u32[]{:S(2)}) copy-start(f32[8,128]{1,0:T(8,128)} %get-tuple-element.26) | copy-start | bytes 12292
  140.9 30.7 %collective-permute-start.24 = (bf16[2,256,256]{2,1,0:T(8,128)(2,1)S(1)}, bf16[2,256,256]{2,1,0:T(8,128)(2,1)S(1)}, u32[]{:S(2)}, u32[]{:S(2)}) collective-permute-start(bf16[2,256,256]{2,1,0:T(8,128)(2,1)S(1)} %get-tuple-element.33), channel_id=1, source_target_pairs={{0,24},{1,97},{2,26},{3,99},{4,28},{5,101},{6,30},{7,103},{8,0},{9... | collective-permute-start | bytes 786440 | tf_op jit(solution)/shard_map/ppermute | solution.py:263
  141.5 1.2 collective-permute-start.27
  142.7 3.6 %collective-permute-start.28 = (f32[8,128]{1,0:T(8,128)S(1)}, f32[8,128]{1,0:T(8,128)S(1)}, u32[]{:S(2)}, u32[]{:S(2)}) collective-permute-start(f32[8,128]{1,0:T(8,128)S(1)} %add.91), channel_id=1, source_target_pairs={{0,2},{1,3},{2,0},{3,1},{4,6},{5,7},{6,4},{7,5},{8,10},{9,11},{10,... | collective-permute-start | bytes 12296 | tf_op jit(solution)/shard_map/ppermute | solution.py:259
  146.3 5.1 %collective-permute-start.29 = (f32[8,128]{1,0:T(8,128)S(1)}, f32[8,128]{1,0:T(8,128)S(1)}, u32[]{:S(2)}, u32[]{:S(2)}) collective-permute-start(f32[8,128]{1,0:T(8,128)S(1)} %add.92), channel_id=1, source_target_pairs={{0,4},{1,5},{2,6},{3,7},{4,0},{5,1},{6,2},{7,3},{8,12},{9,13},{10,... | collective-permute-start | bytes 12296 | tf_op jit(solution)/shard_map/ppermute | solution.py:259
  151.4 3.6 %collective-permute-start.30 = (f32[8,128]{1,0:T(8,128)S(1)}, f32[8,128]{1,0:T(8,128)S(1)}, u32[]{:S(2)}, u32[]{:S(2)}) collective-permute-start(f32[8,128]{1,0:T(8,128)S(1)} %add.93), channel_id=1, source_target_pairs={{0,8},{1,9},{2,10},{3,11},{4,12},{5,13},{6,14},{7,15},{8,0},{9,1},... | collective-permute-start | bytes 12296 | tf_op jit(solution)/shard_map/ppermute | solution.py:259
  155.0 5.1 %collective-permute-start.31 = (f32[8,128]{1,0:T(8,128)S(1)}, f32[8,128]{1,0:T(8,128)S(1)}, u32[]{:S(2)}, u32[]{:S(2)}) collective-permute-start(f32[8,128]{1,0:T(8,128)S(1)} %add.94), channel_id=1, source_target_pairs={{0,16},{1,17},{2,18},{3,19},{4,20},{5,21},{6,22},{7,23},{8,24},{9,... | collective-permute-start | bytes 12296 | tf_op jit(solution)/shard_map/ppermute | solution.py:259
  160.1 3.6 %collective-permute-start.32 = (f32[8,128]{1,0:T(8,128)S(1)}, f32[8,128]{1,0:T(8,128)S(1)}, u32[]{:S(2)}, u32[]{:S(2)}) collective-permute-start(f32[8,128]{1,0:T(8,128)S(1)} %add.95), channel_id=1, source_target_pairs={{0,32},{1,33},{2,34},{3,35},{4,36},{5,37},{6,38},{7,39},{8,40},{9,... | collective-permute-start | bytes 12296 | tf_op jit(solution)/shard_map/ppermute | solution.py:259
  163.8 5.3 %collective-permute-start.33 = (f32[8,128]{1,0:T(8,128)S(1)}, f32[8,128]{1,0:T(8,128)S(1)}, u32[]{:S(2)}, u32[]{:S(2)}) collective-permute-start(f32[8,128]{1,0:T(8,128)S(1)} %add.96), channel_id=1, source_target_pairs={{0,64},{1,65},{2,66},{3,67},{4,68},{5,69},{6,70},{7,71},{8,72},{9,... | collective-permute-start | bytes 12296 | tf_op jit(solution)/shard_map/ppermute | solution.py:259
  169.1 10.7 %collective-permute-start.26 = (bf16[2,256,256]{2,1,0:T(8,128)(2,1)}, bf16[2,256,256]{2,1,0:T(8,128)(2,1)}, u32[]{:S(2)}, u32[]{:S(2)}) collective-permute-start(bf16[2,256,256]{2,1,0:T(8,128)(2,1)} %get-tuple-element.34), channel_id=1, source_target_pairs={{0,8},{1,33},{2,10},{3,35},{4,12},{5,37},{6,14},{7,39},{8,16},{9,4... | collective-permute-start | bytes 786440 | tf_op jit(solution)/shard_map/ppermute | solution.py:263
  170.5 9.3 %collective-permute-start.25 = (bf16[2,256,256]{2,1,0:T(8,128)(2,1)}, bf16[2,256,256]{2,1,0:T(8,128)(2,1)}, u32[]{:S(2)}, u32[]{:S(2)}) collective-permute-start(bf16[2,256,256]{2,1,0:T(8,128)(2,1)} %get-tuple-element.35), channel_id=1, source_target_pairs={{0,16},{1,65},{2,18},{3,67},{4,20},{5,69},{6,22},{7,71},{8,24},{9,... | collective-permute-start | bytes 786440 | tf_op jit(solution)/shard_map/ppermute | solution.py:263
  171.6 10.1 %collective-permute-start.20 = (bf16[4,256,256]{2,1,0:T(8,128)(2,1)S(1)}, bf16[4,256,256]{2,1,0:T(8,128)(2,1)}, u32[]{:S(2)}, u32[]{:S(2)}) collective-permute-start(bf16[4,256,256]{2,1,0:T(8,128)(2,1)S(1)} %collective-permute-done.19), channel_id=1, source_target_pairs={{0,1},{1,0},{2,3},{3,2},{4,5},{5,4},{6,7},{7,6},{8,9},{9,8},{10,11... | collective-permute-start | bytes 1572872 | tf_op jit(solution)/shard_map/ppermute | solution.py:273
  171.6 10.1 %collective-permute-start.17 = (bf16[4,256,256]{2,1,0:T(8,128)(2,1)S(1)}, bf16[4,256,256]{2,1,0:T(8,128)(2,1)}, u32[]{:S(2)}, u32[]{:S(2)}) collective-permute-start(bf16[4,256,256]{2,1,0:T(8,128)(2,1)S(1)} %collective-permute-done.16), channel_id=1, source_target_pairs={{0,1},{1,0},{2,3},{3,2},{4,5},{5,4},{6,7},{7,6},{8,9},{9,8},{10,11... | collective-permute-start | bytes 1572872 | tf_op jit(solution)/shard_map/ppermute | solution.py:273

commit v3 on v2

v3 whole, which is shorter than its diff:
```python
import functools

import jax
import jax.numpy as jnp
from jax import lax
from jax.experimental import pallas as pl
from jax.experimental.pallas import tpu as pltpu
from jax.sharding import Mesh
from jax.sharding import PartitionSpec as P

LOG2E = 1.4426950408889634
RING = 4
NT = (((1,), (1,)), ((), ()))
NN = (((1,), (0,)), ((), ()))
TN = (((0,), (0,)), ((), ()))
WIDE = ("x", "y", "z")
BF = jnp.bfloat16
F32 = jnp.float32


def plan_kernel(place, own, ring, ring_2, over, *rest):
    jobs, rows_low, sem = rest[-3:]
    my_x, my_y, my_z, core = place[0], place[1], place[2], place[3]
    near = jnp.where(core == 0, 1, RING - 1)
    copies = []
    for k, (packet, d) in enumerate([(own, 0), (ring, near), (over, RING - near), (ring_2, 2)]):
        to = rows_low.at[pl.ds(pl.multiple_of(d * 16, 16), 16), :]
        copies.append(pltpu.make_async_copy(packet.at[pl.ds(packet.shape[0] - 16, 16), :], to, sem.at[k]))
    for c in copies:
        c.start()
    for c in copies:
        c.wait()
    width = rows_low.shape[1]
    owner_id = lax.broadcasted_iota(jnp.int32, (16, width), 0)
    slot = lax.broadcasted_iota(jnp.int32, (16, width), 1)
    lane = lax.broadcasted_iota(jnp.int32, (16, 128), 1)
    for d in range(RING):
        rows = rows_low[16 * d: 16 * d + 16, :].astype(F32)
        user, item, label = (jnp.broadcast_to(rows[k: k + 1], (16, width)) for k in range(3))
        live_slots = jnp.broadcast_to(rows[3:4, :1], (16, width))
        item = item.astype(jnp.int32)
        mine = (((item >> 1) & 3) == my_z) & ((item >> 3) == owner_id) & (slot.astype(F32) < live_slots)
        dx = (my_x - (item >> 5)) & 3
        dy = (my_y - ((item >> 3) & 3)) & 3
        at = jnp.where(core == 0, dx * 4 + dy, dy * 4 + dx) * 2 + (item & 1)
        block = d * 4 + (user.astype(jnp.int32) & 3)
        out = jnp.zeros((16, 128), F32)
        for k, v in enumerate([block.astype(F32), at.astype(F32), label, jnp.ones_like(label)]):
            out = jnp.where(lane == k, jnp.sum(jnp.where(mine, v, 0.0), axis=1, keepdims=True), out)
        if d == 0:
            out = jnp.where(lane == 4, live_slots[:, :128], out)
        jobs[16 * d: 16 * d + 16, :] = out.astype(jnp.int32)


def plan(place, own, ring, ring_2, over, *before):
    hbm = pl.BlockSpec(memory_space=pl.ANY)
    width = own.shape[1]
    return pl.pallas_call(
        plan_kernel,
        in_specs=[pl.BlockSpec(memory_space=pltpu.SMEM)] + [hbm] * (4 + len(before)),
        out_specs=pl.BlockSpec(memory_space=pltpu.VMEM),
        out_shape=jax.ShapeDtypeStruct((64, 128), jnp.int32),
        scratch_shapes=[pltpu.VMEM((64, width), BF), pltpu.SemaphoreType.DMA((4,))],
        compiler_params=pltpu.CompilerParams(vmem_limit_bytes=2**20),
        cost_estimate=pl.CostEstimate(flops=10**6, bytes_accessed=2**20, transcendentals=0),
    )(place, own, ring, ring_2, over, *before)


def score_kernel(
    place, jobs, scalars, own, ring, ring_2, over, line_a, line_b, up_a, up_b, down_a, down_b, up_2, down_2,
    keep_2, keep_late, keep_early, give,
    item_keep, item_up, item_down, item_up_low, item_down_low, item_relay_up, item_relay_down, sums,
    users, items, uacc, iacc, ugive, igive, eye, in_sem, out_sem,
):
    core = place[3]
    blocks, half, width = keep_2.shape
    mine = pl.multiple_of(core * half, half)
    other = pl.multiple_of((1 - core) * half, half)
    near = jnp.where(core == 0, 1, RING - 1)
    far = RING - near
    body_rows = blocks * half
    copies = []
    h = line_a.shape[0]
    n = 2 * h
    for k, (piece, at) in enumerate([
            (line_a, 0), (line_b, h), (up_a, n), (up_b, n + h), (down_b, 3 * n), (down_a, 3 * n + h),
            (up_2, 2 * n), (down_2, 2 * n + h)]):
        copies.append(pltpu.make_async_copy(piece, items.at[pl.ds(at, piece.shape[0])], in_sem.at[k]))
    moves = [(own, 0, 0, 0), (own, body_rows, 0, half), (ring, 0, near, 0), (ring, body_rows, near, half),
             (over, body_rows + 16, far, 0), (over, 2 * body_rows + 16, far, half), (ring_2, 0, 2, mine),
             (over, 0, 2, other)]
    for k, (packet, first, d, at) in enumerate(moves):
        for b in range(blocks):
            copies.append(pltpu.make_async_copy(
                packet.at[pl.ds(first + b * half, half), :],
                users.at[d * blocks + b, pl.ds(at, half), :], in_sem.at[8 + k * blocks + b]))
    for c in copies:
        c.start()

    uacc[...] = jnp.zeros_like(uacc)
    iacc[...] = jnp.zeros_like(iacc)
    row = lax.broadcasted_iota(jnp.int32, (128, 128), 0)
    col = lax.broadcasted_iota(jnp.int32, (128, 128), 1)
    eye[...] = (row == col).astype(F32)
    for c in copies:
        c.wait()

    slope, shift, gain = scalars[0], scalars[1], scalars[2]

    def tile(u, it, slope_j, shift_j, label_j):
        inner = lax.dot_general(u, it, NT, preferred_element_type=F32)
        y = inner * slope_j + shift_j
        w = pl.reciprocal(1.0 + jnp.exp2(y), approx=True)
        less = 1.0 - w
        near_one = jnp.maximum(w, less)
        low = jnp.minimum(y, 0.0)
        if label_j is not None:
            hit = eye[...] * label_j > 0.5
            ws, lows = [], []
            for q in range(2):
                r = slice(q * 128, (q + 1) * 128)
                keep = slice((1 - q) * 128, (2 - q) * 128)
                wb = jnp.where(hit, -less[r, r], w[r, r])
                lb = jnp.minimum(jnp.where(hit, -y[r, r], y[r, r]), 0.0)
                ws.append(jnp.concatenate([wb, w[r, keep]] if q == 0 else [w[r, keep], wb], axis=1))
                lows.append(jnp.concatenate([lb, low[r, keep]] if q == 0 else [low[r, keep], lb], axis=1))
            w = jnp.concatenate(ws, axis=0)
            low = jnp.concatenate(lows, axis=0)
        scaled = (w * gain).astype(BF)
        nn = near_one.reshape(32, 8, 256)
        logs = jnp.log2(functools.reduce(lambda p, m: p * nn[m], range(1, 32), nn[0]))
        soft_sum = low.reshape(32, 8, 256).sum(0)
        w_sum = w.reshape(32, 8, 256).sum(0)
        return scaled, soft_sum, logs, w_sum

    def one_job(j, carry):
        soft_acc, log_acc, w_acc = carry
        ui, ii, live = jobs[j, 0], jobs[j, 1], jobs[j, 3] == 1
        label_j = jobs[j, 2].astype(F32)
        slope_j = jnp.where(live, slope, 0.0)
        shift_j = jnp.where(live, shift, 1e30)
        it = items[ii]
        um = users[ui, pl.ds(mine, half), :]
        uo = users[ui, pl.ds(other, half), :]
        sm, a0, l0, w0 = tile(um, it, slope_j, shift_j, label_j)
        so, a1, l1, w1 = tile(uo, it, slope_j, shift_j, None)
        uacc[ui, pl.ds(mine, half), :] += lax.dot_general(sm, it, NN, preferred_element_type=F32)
        uacc[ui, pl.ds(other, half), :] += lax.dot_general(so, it, NN, preferred_element_type=F32)
        iacc[ii] += (lax.dot_general(sm, um, TN, preferred_element_type=F32)
                     + lax.dot_general(so, uo, TN, preferred_element_type=F32))
        return soft_acc + (a0 + a1), log_acc + (l0 + l1), w_acc + (w0 + w1)

    turn = 4

    def some_jobs(g, carry):
        for k in range(turn):
            carry = one_job(turn * g + k, carry)
        return carry

    zero = jnp.zeros((8, 256), F32)
    soft_acc, log_acc, w_acc = lax.fori_loop(0, jobs.shape[0] // turn, some_jobs, (zero, zero, zero))

    out = []

    def send(src, dst):
        c = pltpu.make_async_copy(src, dst, out_sem.at[len(out)])
        c.start()
        out.append(c)

    def rows_of(d, at):
        return uacc.at[pl.ds(d * blocks, blocks), pl.ds(at, half), :]

    def lower(d, at, slot):
        def one(b, none):
            ugive[slot * blocks + b] = uacc[d * blocks + b, pl.ds(at, half), :].astype(BF)
            return none
        lax.fori_loop(0, blocks, one, 0)

    def item_lower(first, count, at, dst):
        def one(b, none):
            igive[at + b] = iacc[first + b].astype(BF)
            return none
        lax.fori_loop(0, count, one, 0)
        send(igive.at[pl.ds(at, count)], dst)

    item_lower(2 * n, h, 0, item_relay_down)
    item_lower(2 * n + h, h, h, item_relay_up)
    lower(2, other, 0)
    lower(near, mine, 1)
    lower(near, other, 2)

    def own_lower(b, none):
        for k in range(2):
            ugive[3 * blocks + 2 * b + k] = uacc[b, k * half: (k + 1) * half, :].astype(BF)
        return none

    lax.fori_loop(0, blocks, own_lower, 0)
    send(ugive, give)
    send(iacc.at[pl.ds(n, h)], item_down)
    send(iacc.at[pl.ds(3 * n + h, h)], item_up)
    item_lower(n + h, h, 2 * h, item_down_low)
    item_lower(3 * n, h, 3 * h, item_up_low)
    send(iacc.at[pl.ds(0, n)], item_keep)
    send(rows_of(2, mine), keep_2)
    send(rows_of(far, other), keep_early)
    send(rows_of(far, mine), keep_late)

    def scale_sum(b, acc):
        prod = uacc[b] * users[b].astype(F32)
        return acc + prod.reshape(64, 8, 256).sum(0)

    scale_acc = lax.fori_loop(0, RING * blocks, scale_sum, zero)
    total = [(soft_acc + log_acc) * (-1.0 / LOG2E), scale_acc * scalars[3], w_acc]
    lane = lax.broadcasted_iota(jnp.int32, (8, 256), 1)
    packed = jnp.zeros((8, 256), F32)
    for k in range(3):
        packed = jnp.where(lane == k, jnp.sum(total[k]), packed)
    packed = jnp.where(lane == 3, 0.5 * jobs[0, 4].astype(F32), packed)
    sums[...] = packed
    for c in out:
        c.wait()


def score(place, jobs, scalars, pieces):
    n, half, width = pieces[4].shape
    n = 2 * n
    blocks = 4
    height = 2 * half
    n_users, n_items = RING * blocks, RING * n
    smem = pl.BlockSpec(memory_space=pltpu.SMEM)
    any_ = pl.BlockSpec(memory_space=pl.ANY)
    part = (blocks, half, width)
    return pl.pallas_call(
        score_kernel,
        in_specs=[smem, smem, smem] + [any_] * len(pieces),
        out_specs=[any_] * 11 + [pl.BlockSpec(memory_space=pltpu.VMEM)],
        out_shape=[jax.ShapeDtypeStruct(part, F32)] * 3 + [jax.ShapeDtypeStruct((5 * blocks, half, width), BF)]
        + [jax.ShapeDtypeStruct((n, half, width), F32)] + [jax.ShapeDtypeStruct((n // 2, half, width), F32)] * 2
        + [jax.ShapeDtypeStruct((n // 2, half, width), BF)] * 4
        + [jax.ShapeDtypeStruct((8, width), F32)],
        scratch_shapes=[
            pltpu.VMEM((n_users, height, width), BF),
            pltpu.VMEM((n_items, half, width), BF),
            pltpu.VMEM((n_users, height, width), F32),
            pltpu.VMEM((n_items, half, width), F32),
            pltpu.VMEM((5 * blocks, half, width), BF),
            pltpu.VMEM((2 * n, half, width), BF),
            pltpu.VMEM((128, 128), F32),
            pltpu.SemaphoreType.DMA((48,)),
            pltpu.SemaphoreType.DMA((16,)),
        ],
        compiler_params=pltpu.CompilerParams(vmem_limit_bytes=36 * 2**20),
        cost_estimate=pl.CostEstimate(flops=13 * 10**9, bytes_accessed=20 * 2**20, transcendentals=2 * 10**7),
    )(place, jobs, scalars, *pieces)


def finish_kernel(place, give, given, early, late, early_over, late_over, out):
    first = place[3] == 0
    half = early.shape[1]
    for k, (ours, theirs) in enumerate([((late, early_over), (late_over, early)), ((early, late_over), (early_over, late))]):
        a = jnp.where(first, ours[0][0].astype(F32), theirs[0][0].astype(F32))
        b = jnp.where(first, ours[1][0].astype(F32), theirs[1][0].astype(F32))
        own = give[k].astype(F32) + given[k].astype(F32)
        out[0, k * half: (k + 1) * half, :] = own + (a + b)


def finish(place, give, given, early, late, early_over, late_over):
    blocks, half, width = early.shape
    own = pl.BlockSpec((2, half, width), lambda b: (3 * blocks // 2 + b, 0, 0))
    part = pl.BlockSpec((1, half, width), lambda b: (b, 0, 0))
    return pl.pallas_call(
        finish_kernel,
        grid=(blocks,),
        in_specs=[pl.BlockSpec(memory_space=pltpu.SMEM), own, own, part, part, part, part],
        out_specs=pl.BlockSpec((1, 2 * half, width), lambda b: (b, 0, 0)),
        out_shape=jax.ShapeDtypeStruct((blocks, 2 * half, width), F32),
        compiler_params=pltpu.CompilerParams(vmem_limit_bytes=8 * 2**20),
        cost_estimate=pl.CostEstimate(flops=2 * 10**6, bytes_accessed=6 * 2**20, transcendentals=0),
    )(place, give, given, early, late, early_over, late_over)


def device(x, y, z, core):
    return (((x % RING) * RING + y % RING) * RING + z % RING) * 2 + core


def every():
    return [(x, y, z, c) for x in range(RING) for y in range(RING) for z in range(RING) for c in range(2)]


AXES = ("x", "y", "z", "n")


def named(f):
    def call(a, *rest, name):
        with jax.named_scope(name):
            return f(a, *rest)
    return call


@named
def along_z(a):
    return lax.ppermute(a, AXES, [
        (device(x, y, z, c), device(x, y, z + (-1 if c else 1), c)) for x, y, z, c in every()])


@named
def swap(a, bit):
    return lax.ppermute(a, AXES, [(i, i ^ bit) for i in range(128)])


@named
def along_first(a, d):
    return lax.ppermute(a, AXES, [
        (device(x, y, z, c), device(x + (d if c else 0), y + (0 if c else d), z, c)) for x, y, z, c in every()])


@named
def along_second(a, d):
    return lax.ppermute(a, AXES, [
        (device(x, y, z, c), device(x + (0 if c else d), y + (d if c else 0), z, c)) for x, y, z, c in every()])


@named
def across(a):
    return lax.ppermute(a, AXES, [(device(x, y, z, c), device(x, y, z, 1 - c)) for x, y, z, c in every()])


def body(user_emb, item_emb, pairs, counts, natural_exponent_param, additive_shift_param):
    my_x, my_y, my_z = lax.axis_index("x"), lax.axis_index("y"), lax.axis_index("z")
    core = lax.axis_index("n")
    blocks, height, width = user_emb.shape
    half = height // 2
    sharpness = jnp.exp(natural_exponent_param[0])
    shift = additive_shift_param[0]
    place = jnp.stack([my_x, my_y, my_z, core]).astype(jnp.int32)
    scalars = jnp.stack([-sharpness * LOG2E, -shift * LOG2E, sharpness * height ** -0.5, jnp.float32(height ** 0.5)])

    slots = pairs.shape[1]
    rows = jnp.concatenate([pairs[0].T, jnp.broadcast_to(counts[:, None], (1, slots))], axis=0)
    rows = jnp.pad(rows.astype(F32), ((0, 12), (0, width - slots))).astype(BF)
    lower = [user_emb[:, :half].astype(BF).reshape(blocks * half, width),
             user_emb[:, half:].astype(BF).reshape(blocks * half, width)]
    own = jnp.concatenate(lower + [rows], axis=0)
    items_low = item_emb.astype(BF)

    line = [items_low] + [along_first(items_low, d, name="items_line") for d in (1, 2, 3)]
    line_a, line_b = jnp.concatenate(line[:2], axis=0), jnp.concatenate(line[2:], axis=0)
    h = line_a.shape[0]
    up_a, down_a = along_second(line_a, 1, name="items_up_a"), along_second(line_b, -1, name="items_down_a")
    up_b, down_b = along_second(line_b, 1, name="items_up_b"), along_second(line_a, -1, name="items_down_b")
    up_2, down_2 = along_second(up_a, 1, name="items_up_2"), along_second(down_a, -1, name="items_down_2")
    ring = along_z(own, name="users_ring")
    n_rows = blocks * half
    mine = lax.dynamic_slice_in_dim(ring, core * n_rows, n_rows, axis=0)
    ring_2 = along_z(jnp.concatenate([mine, ring[2 * n_rows:]], axis=0), name="users_ring_2")
    lists = ring_2[n_rows:] + (up_a[0, :16] + down_a[0, :16] + up_b[0, :16] + down_b[0, :16]) * 0
    over = across(jnp.concatenate([ring_2[:n_rows], lists, ring], axis=0), name="users_over")

    jobs = plan(place, own, ring, ring_2, over, up_b, down_b)
    (keep_2, keep_late, keep_early, give,
     item_keep, item_up, item_down, item_up_low, item_down_low, item_relay_up, item_relay_down, sums) = score(
        place, jobs, scalars, [own, ring, ring_2, over, line_a, line_b, up_a, up_b, down_a, down_b, up_2, down_2])

    given = across(give, name="give")

    steps = []
    for k in range(7):
        if k == 3:
            sums = sums + given[0, :8].astype(F32) * 0.0
        sums = sums + swap(sums, 1 << k, name="totals_" + str(k))
        steps.append(sums)
    objective = sums[0, :3] / (height * height * sums[0, 3])

    def after(step, a):
        return (a.reshape(-1, 8, width) + steps[step - 1] * 0.0).reshape(a.shape)

    from_up = along_second(item_relay_down, -1, name="item_relay_down")
    from_down = along_second(item_relay_up, 1, name="item_relay_up")
    item_down = jnp.concatenate([after(3, item_down + from_up.astype(F32)).astype(BF), item_down_low])
    item_up = jnp.concatenate([item_up_low, after(3, item_up + from_down.astype(F32)).astype(BF)])
    item_down = along_second(item_down, -1, name="item_down")
    item_up = along_second(item_up, 1, name="item_up")
    item_line = after(5, item_keep + item_down.astype(F32) + item_up.astype(F32))
    back = [along_first(item_line[2 * d: 2 * d + 2].astype(BF), -d, name="item_back") for d in (1, 2, 3)]
    item_grad = item_line[:2] + back[0].astype(F32) + back[1].astype(F32) + back[2].astype(F32)

    relay = along_z((keep_2 + given[:blocks].astype(F32)).astype(BF), name="user_relay")
    early = along_z((keep_early + given[blocks:2 * blocks].astype(F32)).astype(BF), name="user_early")
    late = along_z((keep_late + early[0, :1].astype(F32) * 0.0 + given[2 * blocks:3 * blocks].astype(F32) + relay.astype(F32)).astype(BF), name="user_late")
    early_over, late_over = across(early, name="early_over"), across(late, name="late_over")
    user_grad = finish(place, give, given, early, late, early_over, late_over)
    return user_grad, item_grad, objective


def solution(mesh):
    grid = Mesh(mesh.devices.reshape(RING, RING, RING, 2), AXES)
    return jax.shard_map(
        body,
        mesh=grid,
        in_specs=(P(WIDE, None, None), P(WIDE, "n", None), P(WIDE, None, None), P(WIDE), P(), P()),
        out_specs=(P(WIDE, None, None), P(WIDE, "n", None), P()),
        check_vma=False,
    )
```

time: 188 us -> 141 us (0.75)
  waiting for transfers between devices: 77 us -> 35 us
  starting transfers between devices: 34.3 us -> 45.7 us
  Pallas kernels: 53.9 us -> 43.8 us
  other arithmetic: 13.7 us -> 7.21 us
    ppermute x6 -> x10, waiting for transfers between devices: 30.3 us -> 5.27 us  [along_second(): lax.ppermute(a, AXES, [(device(x, y, z, c), device(x + (0 if c else d), y...]
    pallas_call x1 -> x3, Pallas kernels: 53.9 us -> 43.8 us  [the longest x1 39.6 us: score(): pl.pallas_call(score_kernel, in_specs=[smem, smem, smem] + [any_] * len(p...]
    ppermute x6 -> x5, waiting for transfers between devices: 21.4 us -> 13.2 us  [along_z(): lax.ppermute(a, AXES, [(device(x, y, z, c), device(x, y, z + (-1 if c els...]
    ppermute x6 -> x10, starting transfers between devices: 9.25 us -> 16.1 us  [along_second(): lax.ppermute(a, AXES, [(device(x, y, z, c), device(x + (0 if c else d), y...]
    ppermute x7, waiting for transfers between devices: 18.8 us -> 13.7 us  [swap(): return lax.ppermute(a, AXES, [(i, i ^ bit) for i in range(128)])]
    add x9 -> x8, other arithmetic: 5.51 us -> 1.19 us  [the longest x1 0.72 us: body(): ring_2[n_rows:]]
    ppermute x6, waiting for transfers between devices: 6.51 us -> 2.92 us  [along_first(): lax.ppermute(a, AXES, [(device(x, y, z, c), device(x + (d if c else 0), y...]
    ppermute x6, starting transfers between devices: 7.77 us -> 11.3 us  [along_first(): lax.ppermute(a, AXES, [(device(x, y, z, c), device(x + (d if c else 0), y...]
  transfers between devices with their start and end apart: 34 -> 32, of which waited for: 16 -> 15; matrix products, arithmetic and copies ran while one was open for 6% -> 3% of each run, Pallas kernels for 0% -> 1%
where the time goes in v3:
time: 141 us; the launch traced here: 140 us
  starting transfers between devices  45.7 us (32%)
  Pallas kernels  43.8 us (31%)
  waiting for transfers between devices  35 us (25%)
  other arithmetic  7.21 us (5%)
  local copies, waits for them, and re-layouts  4.42 us (3%)
  between operations  3.59 us (3%)
    pallas_call x1, Pallas kernels, score(): pl.pallas_call(score_kernel, in_specs=[smem, smem, smem] + [any_] * len(p...  39.6 us
    ppermute x10, starting transfers between devices, along_second(): lax.ppermute(a, AXES, [(device(x, y, z, c), device(x + (0 if c else d), y...  16.1 us
    ppermute x7, waiting for transfers between devices, swap(): return lax.ppermute(a, AXES, [(i, i ^ bit) for i in range(128)])  13.7 us
    ppermute x5, waiting for transfers between devices, along_z(): lax.ppermute(a, AXES, [(device(x, y, z, c), device(x, y, z + (-1 if c els...  13.2 us
    ppermute x6, starting transfers between devices, along_first(): lax.ppermute(a, AXES, [(device(x, y, z, c), device(x + (d if c else 0), y...  11.3 us
    ppermute x7, starting transfers between devices, swap(): return lax.ppermute(a, AXES, [(i, i ^ bit) for i in range(128)])  11.1 us
    ppermute x5, starting transfers between devices, along_z(): lax.ppermute(a, AXES, [(device(x, y, z, c), device(x, y, z + (-1 if c els...  6.29 us
    ppermute x10, waiting for transfers between devices, along_second(): lax.ppermute(a, AXES, [(device(x, y, z, c), device(x + (0 if c else d), y...  5.27 us
  transfers between devices with their start and end apart: 32, of which 15 were waited for; matrix products, arithmetic and copies ran while one was open for 3% of the time, Pallas kernels for 1%

profile of v3, /device:TPU:0, one launch (start us, length us, event | category | flops | bytes accessed | tf_op | source)
XLA Modules:
  0.0 139.7 jit_solution(4359300523108317187)
XLA Ops:
  1.3 0.7 copy.11
  2.0 1.7 %convert.13 = bf16[4,512,256]{2,1,0:T(8,128)(2,1)S(1)} convert(f32[4,512,256]{2,1,0:T(8,128)} %param.6) | non-fusion elementwise | flops 524288 | bytes 3145728 | tf_op jit(solution)/shard_map/convert.6
  3.8 2.1 %collective-permute-start = (bf16[2064,256]{1,0:T(8,128)(2,1)S(1)}, bf16[2064,256]{1,0:T(8,128)(2,1)S(1)}, u32[]{:S(2)}, u32[]{:S(2)}) collective-permute-start(bf16[2064,256]{1,0:T(8,128)(2,1)S(1)} %fusion.1.own), channel_id=1, source_target_pairs={{0,2},{1,7},{2,4},{3,1},{4,6},{5,3},{6,0},{7,5},{8,10},{9,15},{10,... | collective-permute-start | bytes 3170312 | tf_op jit(solution)/shard_map/users_ring/ppermute | solution.py:302
  5.9 1.6 %collective-permute-start.2 = (bf16[2,256,256]{2,1,0:T(8,128)(2,1)S(1)}, bf16[2,256,256]{2,1,0:T(8,128)(2,1)S(1)}, u32[]{:S(2)}, u32[]{:S(2)}) collective-permute-start(bf16[2,256,256]{2,1,0:T(8,128)(2,1)S(1)} %convert_element_type.82), channel_id=1, source_target_pairs={{0,8},{1,33},{2,10},{3,35},{4,12},{5,37},{6,14},{7,39},{8,16},{9,4... | collective-permute-start | bytes 786440 | tf_op jit(solution)/shard_map/items_line/ppermute | solution.py:313
  7.6 2.9 %collective-permute-start.4 = (bf16[2,256,256]{2,1,0:T(8,128)(2,1)S(1)}, bf16[2,256,256]{2,1,0:T(8,128)(2,1)S(1)}, u32[]{:S(2)}, u32[]{:S(2)}) collective-permute-start(bf16[2,256,256]{2,1,0:T(8,128)(2,1)S(1)} %convert_element_type.82), channel_id=1, source_target_pairs={{0,16},{1,65},{2,18},{3,67},{4,20},{5,69},{6,22},{7,71},{8,24},{9,... | collective-permute-start | bytes 786440 | tf_op jit(solution)/shard_map/items_line/ppermute | solution.py:313
  10.5 1.3 collective-permute-start.5
  11.8 1.8 %collective-permute-done.2 = bf16[2,256,256]{2,1,0:T(8,128)(2,1)S(1)} collective-permute-done((bf16[2,256,256]{2,1,0:T(8,128)(2,1)S(1)}, bf16[2,256,256]{2,1,0:T(8,128)(2,1)S(1)}, u32[]{:S(2)}, u32[]{:S(2)}) %collective-permute-start.2) | collective-permute-done | bytes 262176 | tf_op jit(solution)/shard_map/items_line/ppermute | solution.py:313
  13.7 2.8 %collective-permute-start.8 = (bf16[4,256,256]{2,1,0:T(8,128)(2,1)S(1)}, bf16[4,256,256]{2,1,0:T(8,128)(2,1)S(1)}, u32[]{:S(2)}, u32[]{:S(2)}) collective-permute-start(bf16[4,256,256]{2,1,0:T(8,128)(2,1)S(1)} %pad_maximum_fusion.4.line_a), channel_id=1, source_target_pairs={{0,96},{1,25},{2,98},{3,27},{4,100},{5,29},{6,102},{7,31},{8,104},... | collective-permute-start | bytes 1572872 | tf_op jit(solution)/shard_map/items_down_b/ppermute | solution.py:319
  16.5 1.2 collective-permute-done.4
  17.7 3.2 %collective-permute-done.ring = bf16[2064,256]{1,0:T(8,128)(2,1)S(1)} collective-permute-done((bf16[2064,256]{1,0:T(8,128)(2,1)S(1)}, bf16[2064,256]{1,0:T(8,128)(2,1)S(1)}, u32[]{:S(2)}, u32[]{:S(2)}) %collective-permute-start) | collective-permute-done | bytes 1056800 | tf_op jit(solution)/shard_map/users_ring/ppermute | solution.py:302
  21.1 1.0 constant_dynamic-update-slice_fusion.line_b
  22.1 1.9 %collective-permute-start.7 = (bf16[4,256,256]{2,1,0:T(8,128)(2,1)S(1)}, bf16[4,256,256]{2,1,0:T(8,128)(2,1)S(1)}, u32[]{:S(2)}, u32[]{:S(2)}) collective-permute-start(bf16[4,256,256]{2,1,0:T(8,128)(2,1)S(1)} %constant_dynamic-update-slice_fusion.line_b), channel_id=1, source_target_pairs={{0,32},{1,9},{2,34},{3,11},{4,36},{5,13},{6,38},{7,15},{8,40},{9,1... | collective-permute-start | bytes 1572872 | tf_op jit(solution)/shard_map/items_up_b/ppermute | solution.py:319
  24.0 1.4 collective-permute-start.6
  25.4 6.2 %collective-permute-done.1.ring_2 = bf16[1040,256]{1,0:T(8,128)(2,1)S(1)} collective-permute-done((bf16[1040,256]{1,0:T(8,128)(2,1)S(1)}, bf16[1040,256]{1,0:T(8,128)(2,1)S(1)}, u32[]{:S(2)}, u32[]{:S(2)}) %collective-permute-start.1) | collective-permute-done | bytes 532512 | tf_op jit(solution)/shard_map/users_ring_2/ppermute | solution.py:302
  31.6 0.9 collective-permute-done.7.rest_0_.up_b
  32.5 0.8 collective-permute-done.6.down_a
  33.3 0.7 fusion.8
  34.0 0.8 copy-done.1
  34.8 1.2 pad_maximum_fusion
  36.1 0.3 collective-permute-start.9
  36.3 1.3 collective-permute-start.10
  37.7 1.9 %collective-permute-start.11 = (bf16[4,256,256]{2,1,0:T(8,128)(2,1)}, bf16[4,256,256]{2,1,0:T(8,128)(2,1)}, u32[]{:S(2)}, u32[]{:S(2)}) collective-permute-start(bf16[4,256,256]{2,1,0:T(8,128)(2,1)} %collective-permute-done.6.down_a), channel_id=1, source_target_pairs={{0,96},{1,25},{2,98},{3,27},{4,100},{5,29},{6,102},{7,31},{8,104},... | collective-permute-start | bytes 1572872 | tf_op jit(solution)/shard_map/items_down_2/ppermute | solution.py:319
  40.9 0.1 pad_add_fusion.place
  41.0 0.1 pad_maximum_fusion.5.scalars
  41.1 1.0 copy-done.2
  42.1 1.5 %shard_map.85.jobs = s32[64,128]{1,0:T(8,128)S(1)} custom-call(s32[4]{0:T(128)S(1)} %pad_add_fusion.place, bf16[2064,256]{1,0:T(8,128)(2,1)S(1)} %fusion.1.own, bf16[2064,256]{1,0:T(8,128)(2,1)S(1)} %collective-permute-done.ring, bf16[1040,256]{1,0:T(8,128)(2,1)S(1)} %collective-permute-done.1.ring_2, bf16[3104,256]{1,0:T(8,128)(2,1)} %collective-permute-done.9.over, ...), custom_call_target="tpu_custom_call" | custom-call | flops 1000000 | bytes 1048576 | tf_op jit(solution)/shard_map/pallas_call | solution.py:58
  43.6 3.5 %collective-permute-done.10.up_2 = bf16[4,256,256]{2,1,0:T(8,128)(2,1)} collective-permute-done((bf16[4,256,256]{2,1,0:T(8,128)(2,1)}, bf16[4,256,256]{2,1,0:T(8,128)(2,1)}, u32[]{:S(2)}, u32[]{:S(2)}) %collective-permute-start.10) | collective-permute-done | bytes 524320 | tf_op jit(solution)/shard_map/items_up_2/ppermute | solution.py:319
  47.1 0.1 collective-permute-done.11.down_2
  47.2 39.6 %shard_map.86 = (f32[4,256,256]{2,1,0:T(8,128)S(1)}, f32[4,256,256]{2,1,0:T(8,128)S(1)}, f32[4,256,256]{2,1,0:T(8,128)S(1)}, bf16[20,256,256]{2,1,0:T(8,128)(2,1...) custom-call(s32[4]{0:T(128)S(1)} %pad_add_fusion.place, ...), custom_call_target="tpu_custom_call" | custom-call | flops 12999999488 | bytes 20971520 | tf_op jit(solution)/shard_map/pallas_call | solution.py:233
  86.8 0.1 collective-permute-start.12
  86.9 3.2 %collective-permute-start.18 = (bf16[4,256,256]{2,1,0:T(8,128)(2,1)S(1)}, bf16[4,256,256]{2,1,0:T(8,128)(2,1)S(1)}, u32[]{:S(2)}, u32[]{:S(2)}) collective-permute-start(bf16[4,256,256]{2,1,0:T(8,128)(2,1)S(1)} %get-tuple-element.21), channel_id=1, source_target_pairs={{0,96},{1,25},{2,98},{3,27},{4,100},{5,29},{6,102},{7,31},{8,104},... | collective-permute-start | bytes 1572872 | tf_op jit(solution)/shard_map/item_relay_down/ppermute | solution.py:319
  90.1 1.7 %collective-permute-done.19 = f32[8,256]{1,0:T(8,128)S(1)} collective-permute-done((f32[8,256]{1,0:T(8,128)S(1)}, f32[8,256]{1,0:T(8,128)S(1)}, u32[]{:S(2)}, u32[]{:S(2)}) %collective-permute-start.19) | collective-permute-done | bytes 8224 | tf_op jit(solution)/shard_map/totals_0/ppermute | solution.py:308
  91.8 2.0 %collective-permute-start.20 = (f32[8,256]{1,0:T(8,128)S(1)}, f32[8,256]{1,0:T(8,128)S(1)}, u32[]{:S(2)}, u32[]{:S(2)}) collective-permute-start(f32[8,256]{1,0:T(8,128)S(1)} %add.128), channel_id=1, source_target_pairs={{0,2},{1,3},{2,0},{3,1},{4,6},{5,7},{6,4},{7,5},{8,10},{9,11},{10,... | collective-permute-start | bytes 24584 | tf_op jit(solution)/shard_map/totals_1/ppermute | solution.py:308
  93.7 1.7 %collective-permute-done.20 = f32[8,256]{1,0:T(8,128)S(1)} collective-permute-done((f32[8,256]{1,0:T(8,128)S(1)}, f32[8,256]{1,0:T(8,128)S(1)}, u32[]{:S(2)}, u32[]{:S(2)}) %collective-permute-start.20) | collective-permute-done | bytes 8224 | tf_op jit(solution)/shard_map/totals_1/ppermute | solution.py:308
  95.4 3.3 %collective-permute-start.21 = (f32[8,256]{1,0:T(8,128)S(1)}, f32[8,256]{1,0:T(8,128)S(1)}, u32[]{:S(2)}, u32[]{:S(2)}) collective-permute-start(f32[8,256]{1,0:T(8,128)S(1)} %add.129), channel_id=1, source_target_pairs={{0,4},{1,5},{2,6},{3,7},{4,0},{5,1},{6,2},{7,3},{8,12},{9,13},{10,... | collective-permute-start | bytes 24584 | tf_op jit(solution)/shard_map/totals_2/ppermute | solution.py:308
  98.7 1.8 %collective-permute-done.21 = f32[8,256]{1,0:T(8,128)S(1)} collective-permute-done((f32[8,256]{1,0:T(8,128)S(1)}, f32[8,256]{1,0:T(8,128)S(1)}, u32[]{:S(2)}, u32[]{:S(2)}) %collective-permute-start.21) | collective-permute-done | bytes 8224 | tf_op jit(solution)/shard_map/totals_2/ppermute | solution.py:308
  100.7 0.3 fusion.2
  101.0 0.1 pad_maximum_fusion.2
  101.1 1.5 %collective-permute-start.24 = (bf16[8,256,256]{2,1,0:T(8,128)(2,1)S(1)}, bf16[8,256,256]{2,1,0:T(8,128)(2,1)S(1)}, u32[]{:S(2)}, u32[]{:S(2)}) collective-permute-start(bf16[8,256,256]{2,1,0:T(8,128)(2,1)S(1)} %pad_maximum_fusion.2), channel_id=1, source_target_pairs={{0,32},{1,9},{2,34},{3,11},{4,36},{5,13},{6,38},{7,15},{8,40},{9,1... | collective-permute-start | bytes 3145736 | tf_op jit(solution)/shard_map/item_up/ppermute | solution.py:319
  102.6 0.1 pad_maximum_fusion.1
  102.7 2.0 %collective-permute-start.22 = (bf16[8,256,256]{2,1,0:T(8,128)(2,1)S(1)}, bf16[8,256,256]{2,1,0:T(8,128)(2,1)S(1)}, u32[]{:S(2)}, u32[]{:S(2)}) collective-permute-start(bf16[8,256,256]{2,1,0:T(8,128)(2,1)S(1)} %pad_maximum_fusion.1), channel_id=1, source_target_pairs={{0,96},{1,25},{2,98},{3,27},{4,100},{5,29},{6,102},{7,31},{8,104},... | collective-permute-start | bytes 3145736 | tf_op jit(solution)/shard_map/item_down/ppermute | solution.py:319
  104.8 0.4 add_convert_fusion.1
  105.1 2.0 %collective-permute-start.13 = (bf16[4,256,256]{2,1,0:T(8,128)(2,1)S(1)}, bf16[4,256,256]{2,1,0:T(8,128)(2,1)S(1)}, u32[]{:S(2)}, u32[]{:S(2)}) collective-permute-start(bf16[4,256,256]{2,1,0:T(8,128)(2,1)S(1)} %get-tuple-element.32), channel_id=1, source_target_pairs={{0,2},{1,7},{2,4},{3,1},{4,6},{5,3},{6,0},{7,5},{8,10},{9,15},{10,... | collective-permute-start | bytes 1572872 | tf_op jit(solution)/shard_map/user_early/ppermute | solution.py:302
  107.1 1.3 collective-permute-start.14
  108.5 1.2 collective-permute-start.25
  109.7 2.6 %collective-permute-done.25 = f32[8,256]{1,0:T(8,128)S(1)} collective-permute-done((f32[8,256]{1,0:T(8,128)S(1)}, f32[8,256]{1,0:T(8,128)S(1)}, u32[]{:S(2)}, u32[]{:S(2)}) %collective-permute-start.25) | collective-permute-done | bytes 8224 | tf_op jit(solution)/shard_map/totals_3/ppermute | solution.py:308
  112.3 3.3 %collective-permute-start.26 = (f32[8,256]{1,0:T(8,128)S(1)}, f32[8,256]{1,0:T(8,128)S(1)}, u32[]{:S(2)}, u32[]{:S(2)}) collective-permute-start(f32[8,256]{1,0:T(8,128)S(1)} %add.139), channel_id=1, source_target_pairs={{0,16},{1,17},{2,18},{3,19},{4,20},{5,21},{6,22},{7,23},{8,24},{9,... | collective-permute-start | bytes 24584 | tf_op jit(solution)/shard_map/totals_4/ppermute | solution.py:308
  115.5 1.9 %collective-permute-done.26 = f32[8,256]{1,0:T(8,128)S(1)} collective-permute-done((f32[8,256]{1,0:T(8,128)S(1)}, f32[8,256]{1,0:T(8,128)S(1)}, u32[]{:S(2)}, u32[]{:S(2)}) %collective-permute-start.26) | collective-permute-done | bytes 8224 | tf_op jit(solution)/shard_map/totals_4/ppermute | solution.py:308
  117.4 3.8 %collective-permute-done.14 = bf16[4,256,256]{2,1,0:T(8,128)(2,1)S(1)} collective-permute-done((bf16[4,256,256]{2,1,0:T(8,128)(2,1)S(1)}, bf16[4,256,256]{2,1,0:T(8,128)(2,1)S(1)}, u32[]{:S(2)}, u32[]{:S(2)}) %collective-permute-start.14) | collective-permute-done | bytes 524320 | tf_op jit(solution)/shard_map/user_relay/ppermute | solution.py:302
  121.2 0.2 add_convert_fusion
  121.4 0.8 collective-permute-start.15
  122.3 0.4 convert_add_fusion
  122.7 0.2 fusion.11
  123.0 1.0 collective-permute-start.29
  124.0 2.3 %collective-permute-start.27 = (bf16[2,256,256]{2,1,0:T(8,128)(2,1)S(1)}, bf16[2,256,256]{2,1,0:T(8,128)(2,1)S(1)}, u32[]{:S(2)}, u32[]{:S(2)}) collective-permute-start(bf16[2,256,256]{2,1,0:T(8,128)(2,1)S(1)} %bitcast.48), channel_id=1, source_target_pairs={{0,24},{1,97},{2,26},{3,99},{4,28},{5,101},{6,30},{7,103},{8,0},{9... | collective-permute-start | bytes 786440 | tf_op jit(solution)/shard_map/item_back/ppermute | solution.py:313
  126.3 2.1 %collective-permute-start.28 = (bf16[2,256,256]{2,1,0:T(8,128)(2,1)S(1)}, bf16[2,256,256]{2,1,0:T(8,128)(2,1)S(1)}, u32[]{:S(2)}, u32[]{:S(2)}) collective-permute-start(bf16[2,256,256]{2,1,0:T(8,128)(2,1)S(1)} %bitcast.47), channel_id=1, source_target_pairs={{0,16},{1,65},{2,18},{3,67},{4,20},{5,69},{6,22},{7,71},{8,24},{9,... | collective-permute-start | bytes 786440 | tf_op jit(solution)/shard_map/item_back/ppermute | solution.py:313
  128.4 1.3 collective-permute-start.31
  129.7 4.0 %collective-permute-done.31 = f32[8,256]{1,0:T(8,128)S(1)} collective-permute-done((f32[8,256]{1,0:T(8,128)S(1)}, f32[8,256]{1,0:T(8,128)S(1)}, u32[]{:S(2)}, u32[]{:S(2)}) %collective-permute-start.31) | collective-permute-done | bytes 8224 | tf_op jit(solution)/shard_map/totals_6/ppermute | solution.py:308
  133.7 0.1 collective-permute-start.16
  133.8 0.4 collective-permute-start.17
  134.2 0.6 slice.111
  135.5 0.5 fusion.10
  136.0 0.9 fusion.5
  137.0 2.8 %shard_map.87 = f32[4,512,256]{2,1,0:T(8,128)} custom-call(s32[4]{0:T(128)S(1)} %pad_add_fusion.place, bf16[20,256,256]{2,1,0:T(8,128)(2,1)S(1)} %copy-done, bf16[20,256,256]{2,1,0:T(8,128)(2,1)S(1)} %collective-permute-done.12.given, bf16[4,256,256]{2,1,0:T(8,128)(2,1)S(1)} %collective-permute-done.13.early, ...), custom_call_target="tpu_custom_call" | custom-call | flops 2000000 | bytes 6291456 | tf_op jit(solution)/shard_map/pallas_call | solution.py:271
  (59 shorter events, 0.7 us)
Async XLA Ops:
  3.7 2.3 %copy-start.8 = (f32[2,256,256]{2,1,0:T(8,128)S(1)}, f32[2,256,256]{2,1,0:T(8,128)}, u32[]{:S(2)}) copy-start(f32[2,256,256]{2,1,0:T(8,128)} %param.7) | copy-start | bytes 1572868
  3.8 17.1 %collective-permute-start = (bf16[2064,256]{1,0:T(8,128)(2,1)S(1)}, bf16[2064,256]{1,0:T(8,128)(2,1)S(1)}, u32[]{:S(2)}, u32[]{:S(2)}) collective-permute-start(bf16[2064,256]{1,0:T(8,128)(2,1)S(1)} %fusion.1.own), channel_id=1, source_target_pairs={{0,2},{1,7},{2,4},{3,1},{4,6},{5,3},{6,0},{7,5},{8,10},{9,15},{10,... | collective-permute-start | bytes 3170312 | tf_op jit(solution)/shard_map/users_ring/ppermute | solution.py:302
  5.9 7.7 %collective-permute-start.2 = (bf16[2,256,256]{2,1,0:T(8,128)(2,1)S(1)}, bf16[2,256,256]{2,1,0:T(8,128)(2,1)S(1)}, u32[]{:S(2)}, u32[]{:S(2)}) collective-permute-start(bf16[2,256,256]{2,1,0:T(8,128)(2,1)S(1)} %convert_element_type.82), channel_id=1, source_target_pairs={{0,8},{1,33},{2,10},{3,35},{4,12},{5,37},{6,14},{7,39},{8,16},{9,4... | collective-permute-start | bytes 786440 | tf_op jit(solution)/shard_map/items_line/ppermute | solution.py:313
  7.6 10.1 %collective-permute-start.4 = (bf16[2,256,256]{2,1,0:T(8,128)(2,1)S(1)}, bf16[2,256,256]{2,1,0:T(8,128)(2,1)S(1)}, u32[]{:S(2)}, u32[]{:S(2)}) collective-permute-start(bf16[2,256,256]{2,1,0:T(8,128)(2,1)S(1)} %convert_element_type.82), channel_id=1, source_target_pairs={{0,16},{1,65},{2,18},{3,67},{4,20},{5,69},{6,22},{7,71},{8,24},{9,... | collective-permute-start | bytes 786440 | tf_op jit(solution)/shard_map/items_line/ppermute | solution.py:313
  10.5 10.6 %collective-permute-start.5 = (bf16[2,256,256]{2,1,0:T(8,128)(2,1)S(1)}, bf16[2,256,256]{2,1,0:T(8,128)(2,1)}, u32[]{:S(2)}, u32[]{:S(2)}) collective-permute-start(bf16[2,256,256]{2,1,0:T(8,128)(2,1)S(1)} %convert_element_type.82), channel_id=1, source_target_pairs={{0,24},{1,97},{2,26},{3,99},{4,28},{5,101},{6,30},{7,103},{8,0},{9... | collective-permute-start | bytes 786440 | tf_op jit(solution)/shard_map/items_line/ppermute | solution.py:313
  13.6 17.9 %copy-start.4 = (bf16[4,256,256]{2,1,0:T(8,128)(2,1)}, bf16[4,256,256]{2,1,0:T(8,128)(2,1)S(1)}, u32[]{:S(2)}) copy-start(bf16[4,256,256]{2,1,0:T(8,128)(2,1)S(1)} %pad_maximum_fusion.4.line_a) | copy-start | bytes 1572868
  13.7 17.9 %collective-permute-start.8 = (bf16[4,256,256]{2,1,0:T(8,128)(2,1)S(1)}, bf16[4,256,256]{2,1,0:T(8,128)(2,1)S(1)}, u32[]{:S(2)}, u32[]{:S(2)}) collective-permute-start(bf16[4,256,256]{2,1,0:T(8,128)(2,1)S(1)} %pad_maximum_fusion.4.line_a), channel_id=1, source_target_pairs={{0,96},{1,25},{2,98},{3,27},{4,100},{5,29},{6,102},{7,31},{8,104},... | collective-permute-start | bytes 1572872 | tf_op jit(solution)/shard_map/items_down_b/ppermute | solution.py:319
  16.5 15.1 %collective-permute-start.3 = (bf16[4,256,256]{2,1,0:T(8,128)(2,1)S(1)}, bf16[4,256,256]{2,1,0:T(8,128)(2,1)}, u32[]{:S(2)}, u32[]{:S(2)}) collective-permute-start(bf16[4,256,256]{2,1,0:T(8,128)(2,1)S(1)} %pad_maximum_fusion.4.line_a), channel_id=1, source_target_pairs={{0,32},{1,9},{2,34},{3,11},{4,36},{5,13},{6,38},{7,15},{8,40},{9,1... | collective-permute-start | bytes 1572872 | tf_op jit(solution)/shard_map/items_up_a/ppermute | solution.py:319
  21.0 10.5 %collective-permute-start.1 = (bf16[1040,256]{1,0:T(8,128)(2,1)S(1)}, bf16[1040,256]{1,0:T(8,128)(2,1)S(1)}, u32[]{:S(2)}, u32[]{:S(2)}) collective-permute-start(bf16[1040,256]{1,0:T(8,128)(2,1)S(1)} %pad_maximum_fusion.3), channel_id=1, source_target_pairs={{0,2},{1,7},{2,4},{3,1},{4,6},{5,3},{6,0},{7,5},{8,10},{9,15},{10,... | collective-permute-start | bytes 1597448 | tf_op jit(solution)/shard_map/users_ring_2/ppermute | solution.py:302
  22.1 10.5 %copy-start.6 = (bf16[4,256,256]{2,1,0:T(8,128)(2,1)}, bf16[4,256,256]{2,1,0:T(8,128)(2,1)S(1)}, u32[]{:S(2)}) copy-start(bf16[4,256,256]{2,1,0:T(8,128)(2,1)S(1)} %constant_dynamic-update-slice_fusion.line_b) | copy-start | bytes 1572868
  22.1 10.5 %collective-permute-start.7 = (bf16[4,256,256]{2,1,0:T(8,128)(2,1)S(1)}, bf16[4,256,256]{2,1,0:T(8,128)(2,1)S(1)}, u32[]{:S(2)}, u32[]{:S(2)}) collective-permute-start(bf16[4,256,256]{2,1,0:T(8,128)(2,1)S(1)} %constant_dynamic-update-slice_fusion.line_b), channel_id=1, source_target_pairs={{0,32},{1,9},{2,34},{3,11},{4,36},{5,13},{6,38},{7,15},{8,40},{9,1... | collective-permute-start | bytes 1572872 | tf_op jit(solution)/shard_map/items_up_b/ppermute | solution.py:319
  24.0 9.3 %collective-permute-start.6 = (bf16[4,256,256]{2,1,0:T(8,128)(2,1)S(1)}, bf16[4,256,256]{2,1,0:T(8,128)(2,1)}, u32[]{:S(2)}, u32[]{:S(2)}) collective-permute-start(bf16[4,256,256]{2,1,0:T(8,128)(2,1)S(1)} %constant_dynamic-update-slice_fusion.line_b), channel_id=1, source_target_pairs={{0,96},{1,25},{2,98},{3,27},{4,100},{5,29},{6,102},{7,31},{8,104},... | collective-permute-start | bytes 1572872 | tf_op jit(solution)/shard_map/items_down_a/ppermute | solution.py:319
  34.0 0.8 copy-start.1
  36.1 5.0 %collective-permute-start.9 = (bf16[3104,256]{1,0:T(8,128)(2,1)}, bf16[3104,256]{1,0:T(8,128)(2,1)}, u32[]{:S(2)}, u32[]{:S(2)}) collective-permute-start(bf16[3104,256]{1,0:T(8,128)(2,1)} %pad_maximum_fusion), channel_id=1, source_target_pairs={{0,1},{1,0},{2,3},{3,2},{4,5},{5,4},{6,7},{7,6},{8,9},{9,8},{10,11... | collective-permute-start | bytes 4767752 | tf_op jit(solution)/shard_map/users_over/ppermute | solution.py:325
  36.3 10.7 %collective-permute-start.10 = (bf16[4,256,256]{2,1,0:T(8,128)(2,1)}, bf16[4,256,256]{2,1,0:T(8,128)(2,1)}, u32[]{:S(2)}, u32[]{:S(2)}) collective-permute-start(bf16[4,256,256]{2,1,0:T(8,128)(2,1)} %collective-permute-done.3.up_a), channel_id=1, source_target_pairs={{0,32},{1,9},{2,34},{3,11},{4,36},{5,13},{6,38},{7,15},{8,40},{9,1... | collective-permute-start | bytes 1572872 | tf_op jit(solution)/shard_map/items_up_2/ppermute | solution.py:319
  37.7 9.5 %collective-permute-start.11 = (bf16[4,256,256]{2,1,0:T(8,128)(2,1)}, bf16[4,256,256]{2,1,0:T(8,128)(2,1)}, u32[]{:S(2)}, u32[]{:S(2)}) collective-permute-start(bf16[4,256,256]{2,1,0:T(8,128)(2,1)} %collective-permute-done.6.down_a), channel_id=1, source_target_pairs={{0,96},{1,25},{2,98},{3,27},{4,100},{5,29},{6,102},{7,31},{8,104},... | collective-permute-start | bytes 1572872 | tf_op jit(solution)/shard_map/items_down_2/ppermute | solution.py:319
  41.1 1.0 copy-start.2
  42.1 5.0 %copy-start.3 = (bf16[4,256,256]{2,1,0:T(8,128)(2,1)S(1)}, bf16[4,256,256]{2,1,0:T(8,128)(2,1)}, u32[]{:S(2)}) copy-start(bf16[4,256,256]{2,1,0:T(8,128)(2,1)} %copy-done.1) | copy-start | bytes 1572868
  42.1 5.0 %copy-start.5 = (bf16[4,256,256]{2,1,0:T(8,128)(2,1)S(1)}, bf16[4,256,256]{2,1,0:T(8,128)(2,1)}, u32[]{:S(2)}) copy-start(bf16[4,256,256]{2,1,0:T(8,128)(2,1)} %copy-done.4) | copy-start | bytes 1572868
  42.1 5.0 %copy-start.7 = (bf16[4,256,256]{2,1,0:T(8,128)(2,1)S(1)}, bf16[4,256,256]{2,1,0:T(8,128)(2,1)}, u32[]{:S(2)}) copy-start(bf16[4,256,256]{2,1,0:T(8,128)(2,1)} %copy-done.6) | copy-start | bytes 1572868
  86.8 13.8 %collective-permute-start.12 = (bf16[20,256,256]{2,1,0:T(8,128)(2,1)}, bf16[20,256,256]{2,1,0:T(8,128)(2,1)S(1)}, u32[]{:S(2)}, u32[]{:S(2)}) collective-permute-start(bf16[20,256,256]{2,1,0:T(8,128)(2,1)} %get-tuple-element.15.give), channel_id=1, source_target_pairs={{0,1},{1,0},{2,3},{3,2},{4,5},{5,4},{6,7},{7,6},{8,9},{9,8},{10,11... | collective-permute-start | bytes 7864328 | tf_op jit(solution)/shard_map/give/ppermute | solution.py:325
  86.9 13.7 %collective-permute-start.18 = (bf16[4,256,256]{2,1,0:T(8,128)(2,1)S(1)}, bf16[4,256,256]{2,1,0:T(8,128)(2,1)S(1)}, u32[]{:S(2)}, u32[]{:S(2)}) collective-permute-start(bf16[4,256,256]{2,1,0:T(8,128)(2,1)S(1)} %get-tuple-element.21), channel_id=1, source_target_pairs={{0,96},{1,25},{2,98},{3,27},{4,100},{5,29},{6,102},{7,31},{8,104},... | collective-permute-start | bytes 1572872 | tf_op jit(solution)/shard_map/item_relay_down/ppermute | solution.py:319
  90.1 10.5 %collective-permute-start.23 = (bf16[4,256,256]{2,1,0:T(8,128)(2,1)S(1)}, bf16[4,256,256]{2,1,0:T(8,128)(2,1)S(1)}, u32[]{:S(2)}, u32[]{:S(2)}) collective-permute-start(bf16[4,256,256]{2,1,0:T(8,128)(2,1)S(1)} %get-tuple-element.26), channel_id=1, source_target_pairs={{0,32},{1,9},{2,34},{3,11},{4,36},{5,13},{6,38},{7,15},{8,40},{9,1... | collective-permute-start | bytes 1572872 | tf_op jit(solution)/shard_map/item_relay_up/ppermute | solution.py:319
  90.1 1.7 %collective-permute-start.19 = (f32[8,256]{1,0:T(8,128)S(1)}, f32[8,256]{1,0:T(8,128)S(1)}, u32[]{:S(2)}, u32[]{:S(2)}) collective-permute-start(f32[8,256]{1,0:T(8,128)S(1)} %get-tuple-element.22), channel_id=1, source_target_pairs={{0,1},{1,0},{2,3},{3,2},{4,5},{5,4},{6,7},{7,6},{8,9},{9,8},{10,11... | collective-permute-start | bytes 24584 | tf_op jit(solution)/shard_map/totals_0/ppermute | solution.py:308
  91.8 3.7 %collective-permute-start.20 = (f32[8,256]{1,0:T(8,128)S(1)}, f32[8,256]{1,0:T(8,128)S(1)}, u32[]{:S(2)}, u32[]{:S(2)}) collective-permute-start(f32[8,256]{1,0:T(8,128)S(1)} %add.128), channel_id=1, source_target_pairs={{0,2},{1,3},{2,0},{3,1},{4,6},{5,7},{6,4},{7,5},{8,10},{9,11},{10,... | collective-permute-start | bytes 24584 | tf_op jit(solution)/shard_map/totals_1/ppermute | solution.py:308
  95.4 5.2 %collective-permute-start.21 = (f32[8,256]{1,0:T(8,128)S(1)}, f32[8,256]{1,0:T(8,128)S(1)}, u32[]{:S(2)}, u32[]{:S(2)}) collective-permute-start(f32[8,256]{1,0:T(8,128)S(1)} %add.129), channel_id=1, source_target_pairs={{0,4},{1,5},{2,6},{3,7},{4,0},{5,1},{6,2},{7,3},{8,12},{9,13},{10,... | collective-permute-start | bytes 24584 | tf_op jit(solution)/shard_map/totals_2/ppermute | solution.py:308
  101.1 21.1 %collective-permute-start.24 = (bf16[8,256,256]{2,1,0:T(8,128)(2,1)S(1)}, bf16[8,256,256]{2,1,0:T(8,128)(2,1)S(1)}, u32[]{:S(2)}, u32[]{:S(2)}) collective-permute-start(bf16[8,256,256]{2,1,0:T(8,128)(2,1)S(1)} %pad_maximum_fusion.2), channel_id=1, source_target_pairs={{0,32},{1,9},{2,34},{3,11},{4,36},{5,13},{6,38},{7,15},{8,40},{9,1... | collective-permute-start | bytes 3145736 | tf_op jit(solution)/shard_map/item_up/ppermute | solution.py:319
  102.7 19.5 %collective-permute-start.22 = (bf16[8,256,256]{2,1,0:T(8,128)(2,1)S(1)}, bf16[8,256,256]{2,1,0:T(8,128)(2,1)S(1)}, u32[]{:S(2)}, u32[]{:S(2)}) collective-permute-start(bf16[8,256,256]{2,1,0:T(8,128)(2,1)S(1)} %pad_maximum_fusion.1), channel_id=1, source_target_pairs={{0,96},{1,25},{2,98},{3,27},{4,100},{5,29},{6,102},{7,31},{8,104},... | collective-permute-start | bytes 3145736 | tf_op jit(solution)/shard_map/item_down/ppermute | solution.py:319
  105.1 12.3 %collective-permute-start.13 = (bf16[4,256,256]{2,1,0:T(8,128)(2,1)S(1)}, bf16[4,256,256]{2,1,0:T(8,128)(2,1)S(1)}, u32[]{:S(2)}, u32[]{:S(2)}) collective-permute-start(bf16[4,256,256]{2,1,0:T(8,128)(2,1)S(1)} %get-tuple-element.32), channel_id=1, source_target_pairs={{0,2},{1,7},{2,4},{3,1},{4,6},{5,3},{6,0},{7,5},{8,10},{9,15},{10,... | collective-permute-start | bytes 1572872 | tf_op jit(solution)/shard_map/user_early/ppermute | solution.py:302
  107.1 14.1 %collective-permute-start.14 = (bf16[4,256,256]{2,1,0:T(8,128)(2,1)S(1)}, bf16[4,256,256]{2,1,0:T(8,128)(2,1)S(1)}, u32[]{:S(2)}, u32[]{:S(2)}) collective-permute-start(bf16[4,256,256]{2,1,0:T(8,128)(2,1)S(1)} %get-tuple-element.31), channel_id=1, source_target_pairs={{0,2},{1,7},{2,4},{3,1},{4,6},{5,3},{6,0},{7,5},{8,10},{9,15},{10,... | collective-permute-start | bytes 1572872 | tf_op jit(solution)/shard_map/user_relay/ppermute | solution.py:302
  108.5 3.8 %collective-permute-start.25 = (f32[8,256]{1,0:T(8,128)S(1)}, f32[8,256]{1,0:T(8,128)S(1)}, u32[]{:S(2)}, u32[]{:S(2)}) collective-permute-start(f32[8,256]{1,0:T(8,128)S(1)} %get-tuple-element.40), channel_id=1, source_target_pairs={{0,8},{1,9},{2,10},{3,11},{4,12},{5,13},{6,14},{7,15},{8,0},{9,1},... | collective-permute-start | bytes 24584 | tf_op jit(solution)/shard_map/totals_3/ppermute | solution.py:308
  112.3 5.2 %collective-permute-start.26 = (f32[8,256]{1,0:T(8,128)S(1)}, f32[8,256]{1,0:T(8,128)S(1)}, u32[]{:S(2)}, u32[]{:S(2)}) collective-permute-start(f32[8,256]{1,0:T(8,128)S(1)} %add.139), channel_id=1, source_target_pairs={{0,16},{1,17},{2,18},{3,19},{4,20},{5,21},{6,22},{7,23},{8,24},{9,... | collective-permute-start | bytes 24584 | tf_op jit(solution)/shard_map/totals_4/ppermute | solution.py:308
  117.4 11.0 %collective-permute-start.30 = (f32[8,256]{1,0:T(8,128)S(1)}, f32[8,256]{1,0:T(8,128)S(1)}, u32[]{:S(2)}, u32[]{:S(2)}) collective-permute-start(f32[8,256]{1,0:T(8,128)S(1)} %get-tuple-element.30), channel_id=1, source_target_pairs={{0,32},{1,33},{2,34},{3,35},{4,36},{5,37},{6,38},{7,39},{8,40},{9,... | collective-permute-start | bytes 24584 | tf_op jit(solution)/shard_map/totals_5/ppermute | solution.py:308
  121.4 12.4 %collective-permute-start.15 = (bf16[4,256,256]{2,1,0:T(8,128)(2,1)S(1)}, bf16[4,256,256]{2,1,0:T(8,128)(2,1)S(1)}, u32[]{:S(2)}, u32[]{:S(2)}) collective-permute-start(bf16[4,256,256]{2,1,0:T(8,128)(2,1)S(1)} %add_convert_fusion), channel_id=1, source_target_pairs={{0,2},{1,7},{2,4},{3,1},{4,6},{5,3},{6,0},{7,5},{8,10},{9,15},{10,... | collective-permute-start | bytes 1572872 | tf_op jit(solution)/shard_map/user_late/ppermute | solution.py:302
  122.9 14.0 %copy-start = (bf16[20,256,256]{2,1,0:T(8,128)(2,1)S(1)}, bf16[20,256,256]{2,1,0:T(8,128)(2,1)}, u32[]{:S(2)}) copy-start(bf16[20,256,256]{2,1,0:T(8,128)(2,1)} %get-tuple-element.15.give) | copy-start | bytes 7864324
  123.0 13.0 %collective-permute-start.29 = (bf16[2,256,256]{2,1,0:T(8,128)(2,1)S(1)}, bf16[2,256,256]{2,1,0:T(8,128)(2,1)S(1)}, u32[]{:S(2)}, u32[]{:S(2)}) collective-permute-start(bf16[2,256,256]{2,1,0:T(8,128)(2,1)S(1)} %bitcast.49), channel_id=1, source_target_pairs={{0,8},{1,33},{2,10},{3,35},{4,12},{5,37},{6,14},{7,39},{8,16},{9,4... | collective-permute-start | bytes 786440 | tf_op jit(solution)/shard_map/item_back/ppermute | solution.py:313
  124.0 12.0 %collective-permute-start.27 = (bf16[2,256,256]{2,1,0:T(8,128)(2,1)S(1)}, bf16[2,256,256]{2,1,0:T(8,128)(2,1)S(1)}, u32[]{:S(2)}, u32[]{:S(2)}) collective-permute-start(bf16[2,256,256]{2,1,0:T(8,128)(2,1)S(1)} %bitcast.48), channel_id=1, source_target_pairs={{0,24},{1,97},{2,26},{3,99},{4,28},{5,101},{6,30},{7,103},{8,0},{9... | collective-permute-start | bytes 786440 | tf_op jit(solution)/shard_map/item_back/ppermute | solution.py:313
  126.3 9.7 %collective-permute-start.28 = (bf16[2,256,256]{2,1,0:T(8,128)(2,1)S(1)}, bf16[2,256,256]{2,1,0:T(8,128)(2,1)S(1)}, u32[]{:S(2)}, u32[]{:S(2)}) collective-permute-start(bf16[2,256,256]{2,1,0:T(8,128)(2,1)S(1)} %bitcast.47), channel_id=1, source_target_pairs={{0,16},{1,65},{2,18},{3,67},{4,20},{5,69},{6,22},{7,71},{8,24},{9,... | collective-permute-start | bytes 786440 | tf_op jit(solution)/shard_map/item_back/ppermute | solution.py:313
  128.4 5.3 %collective-permute-start.31 = (f32[8,256]{1,0:T(8,128)S(1)}, f32[8,256]{1,0:T(8,128)S(1)}, u32[]{:S(2)}, u32[]{:S(2)}) collective-permute-start(f32[8,256]{1,0:T(8,128)S(1)} %add.146), channel_id=1, source_target_pairs={{0,64},{1,65},{2,66},{3,67},{4,68},{5,69},{6,70},{7,71},{8,72},{9,... | collective-permute-start | bytes 24584 | tf_op jit(solution)/shard_map/totals_6/ppermute | solution.py:308
  133.7 3.2 %collective-permute-start.16 = (bf16[4,256,256]{2,1,0:T(8,128)(2,1)S(1)}, bf16[4,256,256]{2,1,0:T(8,128)(2,1)S(1)}, u32[]{:S(2)}, u32[]{:S(2)}) collective-permute-start(bf16[4,256,256]{2,1,0:T(8,128)(2,1)S(1)} %collective-permute-done.13.early), channel_id=1, source_target_pairs={{0,1},{1,0},{2,3},{3,2},{4,5},{5,4},{6,7},{7,6},{8,9},{9,8},{10,11... | collective-permute-start | bytes 1572872 | tf_op jit(solution)/shard_map/early_over/ppermute | solution.py:325
  133.8 3.1 %collective-permute-start.17 = (bf16[4,256,256]{2,1,0:T(8,128)(2,1)S(1)}, bf16[4,256,256]{2,1,0:T(8,128)(2,1)S(1)}, u32[]{:S(2)}, u32[]{:S(2)}) collective-permute-start(bf16[4,256,256]{2,1,0:T(8,128)(2,1)S(1)} %collective-permute-done.15.late), channel_id=1, source_target_pairs={{0,1},{1,0},{2,3},{3,2},{4,5},{5,4},{6,7},{7,6},{8,9},{9,8},{10,11... | collective-permute-start | bytes 1572872 | tf_op jit(solution)/shard_map/late_over/ppermute | solution.py:325

commit v4 on v3

--- a/solution.py
+++ b/solution.py
@@ -74,27 +74,26 @@
 ):
     core = place[3]
     blocks, half, width = keep_2.shape
-    mine = pl.multiple_of(core * half, half)
-    other = pl.multiple_of((1 - core) * half, half)
     near = jnp.where(core == 0, 1, RING - 1)
     far = RING - near
-    body_rows = blocks * half
-    copies = []
+    rows = blocks * half
     h = line_a.shape[0]
     n = 2 * h
+    mine, other = core * rows, (1 - core) * rows
+    first, rest = [], []
     for k, (piece, at) in enumerate([
             (line_a, 0), (line_b, h), (up_a, n), (up_b, n + h), (down_b, 3 * n), (down_a, 3 * n + h),
             (up_2, 2 * n), (down_2, 2 * n + h)]):
-        copies.append(pltpu.make_async_copy(piece, items.at[pl.ds(at, piece.shape[0])], in_sem.at[k]))
-    moves = [(own, 0, 0, 0), (own, body_rows, 0, half), (ring, 0, near, 0), (ring, body_rows, near, half),
-             (over, body_rows + 16, far, 0), (over, 2 * body_rows + 16, far, half), (ring_2, 0, 2, mine),
-             (over, 0, 2, other)]
-    for k, (packet, first, d, at) in enumerate(moves):
-        for b in range(blocks):
-            copies.append(pltpu.make_async_copy(
-                packet.at[pl.ds(first + b * half, half), :],
-                users.at[d * blocks + b, pl.ds(at, half), :], in_sem.at[8 + k * blocks + b]))
-    for c in copies:
+        first.append(pltpu.make_async_copy(piece, items.at[pl.ds(at, piece.shape[0])], in_sem.at[k]))
+    moves = [(own, mine, 0, 0), (own, other, 0, half), (ring_2, 0, 2, 0), (over, 0, 2, half),
+             (ring, mine, near, 0), (ring, other, near, half),
+             (over, rows + 16 + mine, far, 0), (over, rows + 16 + other, far, half)]
+    for k, (packet, start, d, at) in enumerate(moves):
+        c = pltpu.make_async_copy(
+            packet.at[pl.ds(pl.multiple_of(start, 16), rows), :].reshape(blocks, half, width),
+            users.at[pl.ds(d * blocks, blocks), pl.ds(at, half), :], in_sem.at[8 + k])
+        (first if k < 2 else rest).append(c)
+    for c in first + rest:
         c.start()
 
     uacc[...] = jnp.zeros_like(uacc)
@@ -102,13 +101,12 @@
     row = lax.broadcasted_iota(jnp.int32, (128, 128), 0)
     col = lax.broadcasted_iota(jnp.int32, (128, 128), 1)
     eye[...] = (row == col).astype(F32)
-    for c in copies:
+    for c in first:
         c.wait()
 
     slope, shift, gain = scalars[0], scalars[1], scalars[2]
 
-    def tile(u, it, slope_j, shift_j, label_j):
-        inner = lax.dot_general(u, it, NT, preferred_element_type=F32)
+    def tile(inner, slope_j, shift_j, label_j):
         y = inner * slope_j + shift_j
         w = pl.reciprocal(1.0 + jnp.exp2(y), approx=True)
         less = 1.0 - w
@@ -140,76 +138,95 @@
         slope_j = jnp.where(live, slope, 0.0)
         shift_j = jnp.where(live, shift, 1e30)
         it = items[ii]
-        um = users[ui, pl.ds(mine, half), :]
-        uo = users[ui, pl.ds(other, half), :]
-        sm, a0, l0, w0 = tile(um, it, slope_j, shift_j, label_j)
-        so, a1, l1, w1 = tile(uo, it, slope_j, shift_j, None)
-        uacc[ui, pl.ds(mine, half), :] += lax.dot_general(sm, it, NN, preferred_element_type=F32)
-        uacc[ui, pl.ds(other, half), :] += lax.dot_general(so, it, NN, preferred_element_type=F32)
-        iacc[ii] += (lax.dot_general(sm, um, TN, preferred_element_type=F32)
-                     + lax.dot_general(so, uo, TN, preferred_element_type=F32))
+        u = users[ui]
+        inner = lax.dot_general(u, it, NT, preferred_element_type=F32)
+        sm, a0, l0, w0 = tile(inner[:half], slope_j, shift_j, label_j)
+        so, a1, l1, w1 = tile(inner[half:], slope_j, shift_j, None)
+        scaled = jnp.concatenate([sm, so], axis=0)
+        uacc[ui] += lax.dot_general(scaled, it, NN, preferred_element_type=F32)
+        iacc[ii] += lax.dot_general(scaled, u, TN, preferred_element_type=F32)
         return soft_acc + (a0 + a1), log_acc + (l0 + l1), w_acc + (w0 + w1)
 
-    turn = 4
-
-    def some_jobs(g, carry):
-        for k in range(turn):
-            carry = one_job(turn * g + k, carry)
-        return carry
-
-    zero = jnp.zeros((8, 256), F32)
-    soft_acc, log_acc, w_acc = lax.fori_loop(0, jobs.shape[0] // turn, some_jobs, (zero, zero, zero))
-
-    out = []
-
-    def send(src, dst):
-        c = pltpu.make_async_copy(src, dst, out_sem.at[len(out)])
-        c.start()
-        out.append(c)
-
-    def rows_of(d, at):
-        return uacc.at[pl.ds(d * blocks, blocks), pl.ds(at, half), :]
-
-    def lower(d, at, slot):
+    sends = [
+        (ugive, give),
+        (iacc.at[pl.ds(n, h)], item_down), (iacc.at[pl.ds(3 * n + h, h)], item_up), (iacc.at[pl.ds(0, n)], item_keep),
+        (uacc.at[pl.ds(2 * blocks, blocks), pl.ds(0, half), :], keep_2),
+        (uacc.at[pl.ds(far * blocks, blocks), pl.ds(half, half), :], keep_early),
+        (uacc.at[pl.ds(far * blocks, blocks), pl.ds(0, half), :], keep_late),
+        (igive.at[pl.ds(0, h)], item_relay_down), (igive.at[pl.ds(h, h)], item_relay_up),
+        (igive.at[pl.ds(2 * h, h)], item_down_low), (igive.at[pl.ds(3 * h, h)], item_up_low),
+    ]
+    out = [pltpu.make_async_copy(src, dst, out_sem.at[k]) for k, (src, dst) in enumerate(sends)]
+
+    def lower(d, at, to):
         def one(b, none):
-            ugive[slot * blocks + b] = uacc[d * blocks + b, pl.ds(at, half), :].astype(BF)
+            ugive[to(b)] = uacc[d * blocks + b, pl.ds(at, half), :].astype(BF)
             return none
         lax.fori_loop(0, blocks, one, 0)
 
-    def item_lower(first, count, at, dst):
+    def item_lower(at, to):
         def one(b, none):
-            igive[at + b] = iacc[first + b].astype(BF)
+            igive[to + b] = iacc[at + b].astype(BF)
             return none
-        lax.fori_loop(0, count, one, 0)
-        send(igive.at[pl.ds(at, count)], dst)
-
-    item_lower(2 * n, h, 0, item_relay_down)
-    item_lower(2 * n + h, h, h, item_relay_up)
-    lower(2, other, 0)
-    lower(near, mine, 1)
-    lower(near, other, 2)
-
-    def own_lower(b, none):
-        for k in range(2):
-            ugive[3 * blocks + 2 * b + k] = uacc[b, k * half: (k + 1) * half, :].astype(BF)
-        return none
-
-    lax.fori_loop(0, blocks, own_lower, 0)
-    send(ugive, give)
-    send(iacc.at[pl.ds(n, h)], item_down)
-    send(iacc.at[pl.ds(3 * n + h, h)], item_up)
-    item_lower(n + h, h, 2 * h, item_down_low)
-    item_lower(3 * n, h, 3 * h, item_up_low)
-    send(iacc.at[pl.ds(0, n)], item_keep)
-    send(rows_of(2, mine), keep_2)
-    send(rows_of(far, other), keep_early)
-    send(rows_of(far, mine), keep_late)
-
-    def scale_sum(b, acc):
-        prod = uacc[b] * users[b].astype(F32)
-        return acc + prod.reshape(64, 8, 256).sum(0)
-
-    scale_acc = lax.fori_loop(0, RING * blocks, scale_sum, zero)
+        lax.fori_loop(0, h, one, 0)
+
+    turn = 8
+    a_phase = 16 // turn
+
+    def phase(p, carry):
+        d = jnp.where(p == 0, 0, jnp.where(p == 1, 2, jnp.where(p == 2, near, far)))
+
+        @pl.when(p == 1)
+        def _():
+            for c in rest:
+                c.wait()
+
+        def some_jobs(g, carry):
+            for k in range(turn):
+                carry = one_job(d * 16 + turn * g + k, carry)
+            return carry
+
+        soft_acc, log_acc, w_acc, scale_acc = carry
+        soft_acc, log_acc, w_acc = lax.fori_loop(0, a_phase, some_jobs, (soft_acc, log_acc, w_acc))
+
+        @pl.when(p == 0)
+        def _():
+            lower(0, 0, lambda b: 3 * blocks + 2 * b + core)
+            lower(0, half, lambda b: 3 * blocks + 2 * b + 1 - core)
+
+        @pl.when(p == 1)
+        def _():
+            lower(2, half, lambda b: b)
+            out[4].start()
+
+        @pl.when(p == 2)
+        def _():
+            lower(near, 0, lambda b: blocks + b)
+            lower(near, half, lambda b: 2 * blocks + b)
+            out[0].start()
+
+        @pl.when(p == 3)
+        def _():
+            item_lower(2 * n, 0)
+            out[7].start()
+            item_lower(2 * n + h, h)
+            out[8].start()
+            for k in (1, 2, 3, 5, 6):
+                out[k].start()
+            item_lower(n + h, 2 * h)
+            out[9].start()
+            item_lower(3 * n, 3 * h)
+            out[10].start()
+
+        def scale_sum(b, acc):
+            prod = uacc[d * blocks + b] * users[d * blocks + b].astype(F32)
+            return acc + prod.reshape(64, 8, 256).sum(0)
+
+        return soft_acc, log_acc, w_acc, lax.fori_loop(0, blocks, scale_sum, scale_acc)
+
+    zero = jnp.zeros((8, 256), F32)
+    soft_acc, log_acc, w_acc, scale_acc = lax.fori_loop(0, RING, phase, (zero, zero, zero, zero))
+
     total = [(soft_acc + log_acc) * (-1.0 / LOG2E), scale_acc * scalars[3], w_acc]
     lane = lax.broadcasted_iota(jnp.int32, (8, 256), 1)
     packed = jnp.zeros((8, 256), F32)
@@ -246,7 +263,7 @@
             pltpu.VMEM((5 * blocks, half, width), BF),
             pltpu.VMEM((2 * n, half, width), BF),
             pltpu.VMEM((128, 128), F32),
-            pltpu.SemaphoreType.DMA((48,)),
+            pltpu.SemaphoreType.DMA((16,)),
             pltpu.SemaphoreType.DMA((16,)),
         ],
         compiler_params=pltpu.CompilerParams(vmem_limit_bytes=36 * 2**20),

time: 141 us -> 133 us (0.943)
  Pallas kernels: 43.8 us -> 36.2 us
    pallas_call x1, Pallas kernels: 39.6 us -> 32 us  [score(): pl.pallas_call(score_kernel, in_specs=[smem, smem, smem] + [any_] * len(p...]
  transfers between devices with their start and end apart: 32 -> 32, of which waited for: 15 -> 15; matrix products, arithmetic and copies ran while one was open for 3% -> 4% of each run, Pallas kernels for 1% -> 1%
where the time goes in v4:
time: 133 us; the launch traced here: 132 us
  starting transfers between devices  45.5 us (34%)
  Pallas kernels  36.2 us (27%)
  waiting for transfers between devices  35 us (26%)
  other arithmetic  7.21 us (5%)
  local copies, waits for them, and re-layouts  4.42 us (3%)
  between operations  3.59 us (3%)
    pallas_call x1, Pallas kernels, score(): pl.pallas_call(score_kernel, in_specs=[smem, smem, smem] + [any_] * len(p...  32 us
    ppermute x10, starting transfers between devices, along_second(): lax.ppermute(a, AXES, [(device(x, y, z, c), device(x + (0 if c else d), y...  15.9 us
    ppermute x7, waiting for transfers between devices, swap(): return lax.ppermute(a, AXES, [(i, i ^ bit) for i in range(128)])  13.7 us
    ppermute x5, waiting for transfers between devices, along_z(): lax.ppermute(a, AXES, [(device(x, y, z, c), device(x, y, z + (-1 if c els...  13.2 us
    ppermute x6, starting transfers between devices, along_first(): lax.ppermute(a, AXES, [(device(x, y, z, c), device(x + (d if c else 0), y...  11.3 us
    ppermute x7, starting transfers between devices, swap(): return lax.ppermute(a, AXES, [(i, i ^ bit) for i in range(128)])  11.1 us
    ppermute x5, starting transfers between devices, along_z(): lax.ppermute(a, AXES, [(device(x, y, z, c), device(x, y, z + (-1 if c els...  6.29 us
    ppermute x10, waiting for transfers between devices, along_second(): lax.ppermute(a, AXES, [(device(x, y, z, c), device(x + (0 if c else d), y...  5.27 us
  transfers between devices with their start and end apart: 32, of which 15 were waited for; matrix products, arithmetic and copies ran while one was open for 4% of the time, Pallas kernels for 1%

profile of v4, /device:TPU:0, one launch (start us, length us, event | category | flops | bytes accessed | tf_op | source)
XLA Modules:
  0.0 131.9 jit_solution(1355658798246431521)
XLA Ops:
  1.3 0.7 copy.11
  2.0 1.7 %convert.13 = bf16[4,512,256]{2,1,0:T(8,128)(2,1)S(1)} convert(f32[4,512,256]{2,1,0:T(8,128)} %param.6) | non-fusion elementwise | flops 524288 | bytes 3145728 | tf_op jit(solution)/shard_map/convert.6
  3.8 2.1 %collective-permute-start = (bf16[2064,256]{1,0:T(8,128)(2,1)S(1)}, bf16[2064,256]{1,0:T(8,128)(2,1)S(1)}, u32[]{:S(2)}, u32[]{:S(2)}) collective-permute-start(bf16[2064,256]{1,0:T(8,128)(2,1)S(1)} %fusion.1.own), channel_id=1, source_target_pairs={{0,2},{1,7},{2,4},{3,1},{4,6},{5,3},{6,0},{7,5},{8,10},{9,15},{10,... | collective-permute-start | bytes 3170312 | tf_op jit(solution)/shard_map/users_ring/ppermute | solution.py:319
  5.9 1.6 %collective-permute-start.2 = (bf16[2,256,256]{2,1,0:T(8,128)(2,1)S(1)}, bf16[2,256,256]{2,1,0:T(8,128)(2,1)S(1)}, u32[]{:S(2)}, u32[]{:S(2)}) collective-permute-start(bf16[2,256,256]{2,1,0:T(8,128)(2,1)S(1)} %convert_element_type.82), channel_id=1, source_target_pairs={{0,8},{1,33},{2,10},{3,35},{4,12},{5,37},{6,14},{7,39},{8,16},{9,4... | collective-permute-start | bytes 786440 | tf_op jit(solution)/shard_map/items_line/ppermute | solution.py:330
  7.6 2.9 %collective-permute-start.4 = (bf16[2,256,256]{2,1,0:T(8,128)(2,1)S(1)}, bf16[2,256,256]{2,1,0:T(8,128)(2,1)S(1)}, u32[]{:S(2)}, u32[]{:S(2)}) collective-permute-start(bf16[2,256,256]{2,1,0:T(8,128)(2,1)S(1)} %convert_element_type.82), channel_id=1, source_target_pairs={{0,16},{1,65},{2,18},{3,67},{4,20},{5,69},{6,22},{7,71},{8,24},{9,... | collective-permute-start | bytes 786440 | tf_op jit(solution)/shard_map/items_line/ppermute | solution.py:330
  10.5 1.3 %collective-permute-start.5 = (bf16[2,256,256]{2,1,0:T(8,128)(2,1)S(1)}, bf16[2,256,256]{2,1,0:T(8,128)(2,1)}, u32[]{:S(2)}, u32[]{:S(2)}) collective-permute-start(bf16[2,256,256]{2,1,0:T(8,128)(2,1)S(1)} %convert_element_type.82), channel_id=1, source_target_pairs={{0,24},{1,97},{2,26},{3,99},{4,28},{5,101},{6,30},{7,103},{8,0},{9... | collective-permute-start | bytes 786440 | tf_op jit(solution)/shard_map/items_line/ppermute | solution.py:330
  11.8 1.8 %collective-permute-done.2 = bf16[2,256,256]{2,1,0:T(8,128)(2,1)S(1)} collective-permute-done((bf16[2,256,256]{2,1,0:T(8,128)(2,1)S(1)}, bf16[2,256,256]{2,1,0:T(8,128)(2,1)S(1)}, u32[]{:S(2)}, u32[]{:S(2)}) %collective-permute-start.2) | collective-permute-done | bytes 262176 | tf_op jit(solution)/shard_map/items_line/ppermute | solution.py:330
  13.7 2.8 %collective-permute-start.8 = (bf16[4,256,256]{2,1,0:T(8,128)(2,1)S(1)}, bf16[4,256,256]{2,1,0:T(8,128)(2,1)S(1)}, u32[]{:S(2)}, u32[]{:S(2)}) collective-permute-start(bf16[4,256,256]{2,1,0:T(8,128)(2,1)S(1)} %pad_maximum_fusion.4.line_a), channel_id=1, source_target_pairs={{0,96},{1,25},{2,98},{3,27},{4,100},{5,29},{6,102},{7,31},{8,104},... | collective-permute-start | bytes 1572872 | tf_op jit(solution)/shard_map/items_down_b/ppermute | solution.py:336
  16.5 1.2 collective-permute-done.4
  17.7 3.2 %collective-permute-done.ring = bf16[2064,256]{1,0:T(8,128)(2,1)S(1)} collective-permute-done((bf16[2064,256]{1,0:T(8,128)(2,1)S(1)}, bf16[2064,256]{1,0:T(8,128)(2,1)S(1)}, u32[]{:S(2)}, u32[]{:S(2)}) %collective-permute-start) | collective-permute-done | bytes 1056800 | tf_op jit(solution)/shard_map/users_ring/ppermute | solution.py:319
  21.1 1.0 constant_dynamic-update-slice_fusion.line_b
  22.1 1.9 %collective-permute-start.7 = (bf16[4,256,256]{2,1,0:T(8,128)(2,1)S(1)}, bf16[4,256,256]{2,1,0:T(8,128)(2,1)S(1)}, u32[]{:S(2)}, u32[]{:S(2)}) collective-permute-start(bf16[4,256,256]{2,1,0:T(8,128)(2,1)S(1)} %constant_dynamic-update-slice_fusion.line_b), channel_id=1, source_target_pairs={{0,32},{1,9},{2,34},{3,11},{4,36},{5,13},{6,38},{7,15},{8,40},{9,1... | collective-permute-start | bytes 1572872 | tf_op jit(solution)/shard_map/items_up_b/ppermute | solution.py:336
  24.0 1.4 %collective-permute-start.6 = (bf16[4,256,256]{2,1,0:T(8,128)(2,1)S(1)}, bf16[4,256,256]{2,1,0:T(8,128)(2,1)}, u32[]{:S(2)}, u32[]{:S(2)}) collective-permute-start(bf16[4,256,256]{2,1,0:T(8,128)(2,1)S(1)} %constant_dynamic-update-slice_fusion.line_b), channel_id=1, source_target_pairs={{0,96},{1,25},{2,98},{3,27},{4,100},{5,29},{6,102},{7,31},{8,104},... | collective-permute-start | bytes 1572872 | tf_op jit(solution)/shard_map/items_down_a/ppermute | solution.py:336
  25.4 6.2 %collective-permute-done.1.ring_2 = bf16[1040,256]{1,0:T(8,128)(2,1)S(1)} collective-permute-done((bf16[1040,256]{1,0:T(8,128)(2,1)S(1)}, bf16[1040,256]{1,0:T(8,128)(2,1)S(1)}, u32[]{:S(2)}, u32[]{:S(2)}) %collective-permute-start.1) | collective-permute-done | bytes 532512 | tf_op jit(solution)/shard_map/users_ring_2/ppermute | solution.py:319
  31.6 0.9 collective-permute-done.7.rest_0_.up_b
  32.5 0.8 collective-permute-done.6.down_a
  33.3 0.7 fusion.8
  34.0 0.8 copy-done.1
  34.8 1.2 pad_maximum_fusion
  36.1 0.3 collective-permute-start.9
  36.3 1.3 collective-permute-start.10
  37.7 1.9 %collective-permute-start.11 = (bf16[4,256,256]{2,1,0:T(8,128)(2,1)}, bf16[4,256,256]{2,1,0:T(8,128)(2,1)}, u32[]{:S(2)}, u32[]{:S(2)}) collective-permute-start(bf16[4,256,256]{2,1,0:T(8,128)(2,1)} %collective-permute-done.6.down_a), channel_id=1, source_target_pairs={{0,96},{1,25},{2,98},{3,27},{4,100},{5,29},{6,102},{7,31},{8,104},... | collective-permute-start | bytes 1572872 | tf_op jit(solution)/shard_map/items_down_2/ppermute | solution.py:336
  40.9 0.1 pad_add_fusion.place
  41.0 0.1 pad_maximum_fusion.5.scalars
  41.1 1.0 copy-done.2
  42.1 1.5 %shard_map.85.jobs = s32[64,128]{1,0:T(8,128)S(1)} custom-call(s32[4]{0:T(128)S(1)} %pad_add_fusion.place, bf16[2064,256]{1,0:T(8,128)(2,1)S(1)} %fusion.1.own, bf16[2064,256]{1,0:T(8,128)(2,1)S(1)} %collective-permute-done.ring, bf16[1040,256]{1,0:T(8,128)(2,1)S(1)} %collective-permute-done.1.ring_2, bf16[3104,256]{1,0:T(8,128)(2,1)} %collective-permute-done.9.over, ...), custom_call_target="tpu_custom_call" | custom-call | flops 1000000 | bytes 1048576 | tf_op jit(solution)/shard_map/pallas_call | solution.py:58
  43.6 3.5 %collective-permute-done.10.up_2 = bf16[4,256,256]{2,1,0:T(8,128)(2,1)} collective-permute-done((bf16[4,256,256]{2,1,0:T(8,128)(2,1)}, bf16[4,256,256]{2,1,0:T(8,128)(2,1)}, u32[]{:S(2)}, u32[]{:S(2)}) %collective-permute-start.10) | collective-permute-done | bytes 524320 | tf_op jit(solution)/shard_map/items_up_2/ppermute | solution.py:336
  47.1 0.1 collective-permute-done.11.down_2
  47.2 32.0 %shard_map.86 = (f32[4,256,256]{2,1,0:T(8,128)S(1)}, f32[4,256,256]{2,1,0:T(8,128)S(1)}, f32[4,256,256]{2,1,0:T(8,128)S(1)}, bf16[20,256,256]{2,1,0:T(8,128)(2,1...) custom-call(s32[4]{0:T(128)S(1)} %pad_add_fusion.place, ...), custom_call_target="tpu_custom_call" | custom-call | flops 12999999488 | bytes 20971520 | tf_op jit(solution)/shard_map/pallas_call | solution.py:250
  79.2 0.1 collective-permute-start.12
  79.3 3.2 %collective-permute-start.18 = (bf16[4,256,256]{2,1,0:T(8,128)(2,1)S(1)}, bf16[4,256,256]{2,1,0:T(8,128)(2,1)S(1)}, u32[]{:S(2)}, u32[]{:S(2)}) collective-permute-start(bf16[4,256,256]{2,1,0:T(8,128)(2,1)S(1)} %get-tuple-element.21), channel_id=1, source_target_pairs={{0,96},{1,25},{2,98},{3,27},{4,100},{5,29},{6,102},{7,31},{8,104},... | collective-permute-start | bytes 1572872 | tf_op jit(solution)/shard_map/item_relay_down/ppermute | solution.py:336
  82.5 1.7 %collective-permute-done.19 = f32[8,256]{1,0:T(8,128)S(1)} collective-permute-done((f32[8,256]{1,0:T(8,128)S(1)}, f32[8,256]{1,0:T(8,128)S(1)}, u32[]{:S(2)}, u32[]{:S(2)}) %collective-permute-start.19) | collective-permute-done | bytes 8224 | tf_op jit(solution)/shard_map/totals_0/ppermute | solution.py:325
  84.2 2.0 %collective-permute-start.20 = (f32[8,256]{1,0:T(8,128)S(1)}, f32[8,256]{1,0:T(8,128)S(1)}, u32[]{:S(2)}, u32[]{:S(2)}) collective-permute-start(f32[8,256]{1,0:T(8,128)S(1)} %add.128), channel_id=1, source_target_pairs={{0,2},{1,3},{2,0},{3,1},{4,6},{5,7},{6,4},{7,5},{8,10},{9,11},{10,... | collective-permute-start | bytes 24584 | tf_op jit(solution)/shard_map/totals_1/ppermute | solution.py:325
  86.1 1.7 %collective-permute-done.20 = f32[8,256]{1,0:T(8,128)S(1)} collective-permute-done((f32[8,256]{1,0:T(8,128)S(1)}, f32[8,256]{1,0:T(8,128)S(1)}, u32[]{:S(2)}, u32[]{:S(2)}) %collective-permute-start.20) | collective-permute-done | bytes 8224 | tf_op jit(solution)/shard_map/totals_1/ppermute | solution.py:325
  87.8 3.3 %collective-permute-start.21 = (f32[8,256]{1,0:T(8,128)S(1)}, f32[8,256]{1,0:T(8,128)S(1)}, u32[]{:S(2)}, u32[]{:S(2)}) collective-permute-start(f32[8,256]{1,0:T(8,128)S(1)} %add.129), channel_id=1, source_target_pairs={{0,4},{1,5},{2,6},{3,7},{4,0},{5,1},{6,2},{7,3},{8,12},{9,13},{10,... | collective-permute-start | bytes 24584 | tf_op jit(solution)/shard_map/totals_2/ppermute | solution.py:325
  91.1 1.8 %collective-permute-done.21 = f32[8,256]{1,0:T(8,128)S(1)} collective-permute-done((f32[8,256]{1,0:T(8,128)S(1)}, f32[8,256]{1,0:T(8,128)S(1)}, u32[]{:S(2)}, u32[]{:S(2)}) %collective-permute-start.21) | collective-permute-done | bytes 8224 | tf_op jit(solution)/shard_map/totals_2/ppermute | solution.py:325
  93.1 0.3 fusion.2
  93.4 0.1 pad_maximum_fusion.2
  93.5 1.3 %collective-permute-start.24 = (bf16[8,256,256]{2,1,0:T(8,128)(2,1)S(1)}, bf16[8,256,256]{2,1,0:T(8,128)(2,1)S(1)}, u32[]{:S(2)}, u32[]{:S(2)}) collective-permute-start(bf16[8,256,256]{2,1,0:T(8,128)(2,1)S(1)} %pad_maximum_fusion.2), channel_id=1, source_target_pairs={{0,32},{1,9},{2,34},{3,11},{4,36},{5,13},{6,38},{7,15},{8,40},{9,1... | collective-permute-start | bytes 3145736 | tf_op jit(solution)/shard_map/item_up/ppermute | solution.py:336
  94.9 0.1 pad_maximum_fusion.1
  95.0 2.0 %collective-permute-start.22 = (bf16[8,256,256]{2,1,0:T(8,128)(2,1)S(1)}, bf16[8,256,256]{2,1,0:T(8,128)(2,1)S(1)}, u32[]{:S(2)}, u32[]{:S(2)}) collective-permute-start(bf16[8,256,256]{2,1,0:T(8,128)(2,1)S(1)} %pad_maximum_fusion.1), channel_id=1, source_target_pairs={{0,96},{1,25},{2,98},{3,27},{4,100},{5,29},{6,102},{7,31},{8,104},... | collective-permute-start | bytes 3145736 | tf_op jit(solution)/shard_map/item_down/ppermute | solution.py:336
  97.0 0.4 add_convert_fusion.1
  97.4 2.0 %collective-permute-start.13 = (bf16[4,256,256]{2,1,0:T(8,128)(2,1)S(1)}, bf16[4,256,256]{2,1,0:T(8,128)(2,1)S(1)}, u32[]{:S(2)}, u32[]{:S(2)}) collective-permute-start(bf16[4,256,256]{2,1,0:T(8,128)(2,1)S(1)} %get-tuple-element.32), channel_id=1, source_target_pairs={{0,2},{1,7},{2,4},{3,1},{4,6},{5,3},{6,0},{7,5},{8,10},{9,15},{10,... | collective-permute-start | bytes 1572872 | tf_op jit(solution)/shard_map/user_early/ppermute | solution.py:319
  99.4 1.3 collective-permute-start.14
  100.7 1.2 collective-permute-start.25
  101.9 2.6 %collective-permute-done.25 = f32[8,256]{1,0:T(8,128)S(1)} collective-permute-done((f32[8,256]{1,0:T(8,128)S(1)}, f32[8,256]{1,0:T(8,128)S(1)}, u32[]{:S(2)}, u32[]{:S(2)}) %collective-permute-start.25) | collective-permute-done | bytes 8224 | tf_op jit(solution)/shard_map/totals_3/ppermute | solution.py:325
  104.5 3.3 %collective-permute-start.26 = (f32[8,256]{1,0:T(8,128)S(1)}, f32[8,256]{1,0:T(8,128)S(1)}, u32[]{:S(2)}, u32[]{:S(2)}) collective-permute-start(f32[8,256]{1,0:T(8,128)S(1)} %add.139), channel_id=1, source_target_pairs={{0,16},{1,17},{2,18},{3,19},{4,20},{5,21},{6,22},{7,23},{8,24},{9,... | collective-permute-start | bytes 24584 | tf_op jit(solution)/shard_map/totals_4/ppermute | solution.py:325
  107.8 1.9 %collective-permute-done.26 = f32[8,256]{1,0:T(8,128)S(1)} collective-permute-done((f32[8,256]{1,0:T(8,128)S(1)}, f32[8,256]{1,0:T(8,128)S(1)}, u32[]{:S(2)}, u32[]{:S(2)}) %collective-permute-start.26) | collective-permute-done | bytes 8224 | tf_op jit(solution)/shard_map/totals_4/ppermute | solution.py:325
  109.7 3.8 %collective-permute-done.14 = bf16[4,256,256]{2,1,0:T(8,128)(2,1)S(1)} collective-permute-done((bf16[4,256,256]{2,1,0:T(8,128)(2,1)S(1)}, bf16[4,256,256]{2,1,0:T(8,128)(2,1)S(1)}, u32[]{:S(2)}, u32[]{:S(2)}) %collective-permute-start.14) | collective-permute-done | bytes 524320 | tf_op jit(solution)/shard_map/user_relay/ppermute | solution.py:319
  113.4 0.2 add_convert_fusion
  113.7 0.8 collective-permute-start.15
  114.5 0.4 convert_add_fusion
  115.0 0.2 fusion.11
  115.2 1.0 collective-permute-start.29
  116.2 2.3 %collective-permute-start.27 = (bf16[2,256,256]{2,1,0:T(8,128)(2,1)S(1)}, bf16[2,256,256]{2,1,0:T(8,128)(2,1)S(1)}, u32[]{:S(2)}, u32[]{:S(2)}) collective-permute-start(bf16[2,256,256]{2,1,0:T(8,128)(2,1)S(1)} %bitcast.48), channel_id=1, source_target_pairs={{0,24},{1,97},{2,26},{3,99},{4,28},{5,101},{6,30},{7,103},{8,0},{9... | collective-permute-start | bytes 786440 | tf_op jit(solution)/shard_map/item_back/ppermute | solution.py:330
  118.5 2.1 %collective-permute-start.28 = (bf16[2,256,256]{2,1,0:T(8,128)(2,1)S(1)}, bf16[2,256,256]{2,1,0:T(8,128)(2,1)S(1)}, u32[]{:S(2)}, u32[]{:S(2)}) collective-permute-start(bf16[2,256,256]{2,1,0:T(8,128)(2,1)S(1)} %bitcast.47), channel_id=1, source_target_pairs={{0,16},{1,65},{2,18},{3,67},{4,20},{5,69},{6,22},{7,71},{8,24},{9,... | collective-permute-start | bytes 786440 | tf_op jit(solution)/shard_map/item_back/ppermute | solution.py:330
  120.6 1.3 %collective-permute-start.31 = (f32[8,256]{1,0:T(8,128)S(1)}, f32[8,256]{1,0:T(8,128)S(1)}, u32[]{:S(2)}, u32[]{:S(2)}) collective-permute-start(f32[8,256]{1,0:T(8,128)S(1)} %add.146), channel_id=1, source_target_pairs={{0,64},{1,65},{2,66},{3,67},{4,68},{5,69},{6,70},{7,71},{8,72},{9,... | collective-permute-start | bytes 24584 | tf_op jit(solution)/shard_map/totals_6/ppermute | solution.py:325
  122.0 4.0 %collective-permute-done.31 = f32[8,256]{1,0:T(8,128)S(1)} collective-permute-done((f32[8,256]{1,0:T(8,128)S(1)}, f32[8,256]{1,0:T(8,128)S(1)}, u32[]{:S(2)}, u32[]{:S(2)}) %collective-permute-start.31) | collective-permute-done | bytes 8224 | tf_op jit(solution)/shard_map/totals_6/ppermute | solution.py:325
  125.9 0.1 collective-permute-start.16
  126.1 0.4 collective-permute-start.17
  126.4 0.6 slice.111
  127.7 0.5 fusion.10
  128.3 0.9 fusion.5
  129.2 2.8 %shard_map.87 = f32[4,512,256]{2,1,0:T(8,128)} custom-call(s32[4]{0:T(128)S(1)} %pad_add_fusion.place, bf16[20,256,256]{2,1,0:T(8,128)(2,1)S(1)} %copy-done, bf16[20,256,256]{2,1,0:T(8,128)(2,1)S(1)} %collective-permute-done.12.given, bf16[4,256,256]{2,1,0:T(8,128)(2,1)S(1)} %collective-permute-done.13.early, ...), custom_call_target="tpu_custom_call" | custom-call | flops 2000000 | bytes 6291456 | tf_op jit(solution)/shard_map/pallas_call | solution.py:288
  (59 shorter events, 0.7 us)
Async XLA Ops:
  3.7 2.3 %copy-start.8 = (f32[2,256,256]{2,1,0:T(8,128)S(1)}, f32[2,256,256]{2,1,0:T(8,128)}, u32[]{:S(2)}) copy-start(f32[2,256,256]{2,1,0:T(8,128)} %param.7) | copy-start | bytes 1572868
  3.8 17.1 %collective-permute-start = (bf16[2064,256]{1,0:T(8,128)(2,1)S(1)}, bf16[2064,256]{1,0:T(8,128)(2,1)S(1)}, u32[]{:S(2)}, u32[]{:S(2)}) collective-permute-start(bf16[2064,256]{1,0:T(8,128)(2,1)S(1)} %fusion.1.own), channel_id=1, source_target_pairs={{0,2},{1,7},{2,4},{3,1},{4,6},{5,3},{6,0},{7,5},{8,10},{9,15},{10,... | collective-permute-start | bytes 3170312 | tf_op jit(solution)/shard_map/users_ring/ppermute | solution.py:319
  5.9 7.7 %collective-permute-start.2 = (bf16[2,256,256]{2,1,0:T(8,128)(2,1)S(1)}, bf16[2,256,256]{2,1,0:T(8,128)(2,1)S(1)}, u32[]{:S(2)}, u32[]{:S(2)}) collective-permute-start(bf16[2,256,256]{2,1,0:T(8,128)(2,1)S(1)} %convert_element_type.82), channel_id=1, source_target_pairs={{0,8},{1,33},{2,10},{3,35},{4,12},{5,37},{6,14},{7,39},{8,16},{9,4... | collective-permute-start | bytes 786440 | tf_op jit(solution)/shard_map/items_line/ppermute | solution.py:330
  7.6 10.1 %collective-permute-start.4 = (bf16[2,256,256]{2,1,0:T(8,128)(2,1)S(1)}, bf16[2,256,256]{2,1,0:T(8,128)(2,1)S(1)}, u32[]{:S(2)}, u32[]{:S(2)}) collective-permute-start(bf16[2,256,256]{2,1,0:T(8,128)(2,1)S(1)} %convert_element_type.82), channel_id=1, source_target_pairs={{0,16},{1,65},{2,18},{3,67},{4,20},{5,69},{6,22},{7,71},{8,24},{9,... | collective-permute-start | bytes 786440 | tf_op jit(solution)/shard_map/items_line/ppermute | solution.py:330
  10.5 10.6 %collective-permute-start.5 = (bf16[2,256,256]{2,1,0:T(8,128)(2,1)S(1)}, bf16[2,256,256]{2,1,0:T(8,128)(2,1)}, u32[]{:S(2)}, u32[]{:S(2)}) collective-permute-start(bf16[2,256,256]{2,1,0:T(8,128)(2,1)S(1)} %convert_element_type.82), channel_id=1, source_target_pairs={{0,24},{1,97},{2,26},{3,99},{4,28},{5,101},{6,30},{7,103},{8,0},{9... | collective-permute-start | bytes 786440 | tf_op jit(solution)/shard_map/items_line/ppermute | solution.py:330
  13.6 17.9 %copy-start.4 = (bf16[4,256,256]{2,1,0:T(8,128)(2,1)}, bf16[4,256,256]{2,1,0:T(8,128)(2,1)S(1)}, u32[]{:S(2)}) copy-start(bf16[4,256,256]{2,1,0:T(8,128)(2,1)S(1)} %pad_maximum_fusion.4.line_a) | copy-start | bytes 1572868
  13.7 17.9 %collective-permute-start.8 = (bf16[4,256,256]{2,1,0:T(8,128)(2,1)S(1)}, bf16[4,256,256]{2,1,0:T(8,128)(2,1)S(1)}, u32[]{:S(2)}, u32[]{:S(2)}) collective-permute-start(bf16[4,256,256]{2,1,0:T(8,128)(2,1)S(1)} %pad_maximum_fusion.4.line_a), channel_id=1, source_target_pairs={{0,96},{1,25},{2,98},{3,27},{4,100},{5,29},{6,102},{7,31},{8,104},... | collective-permute-start | bytes 1572872 | tf_op jit(solution)/shard_map/items_down_b/ppermute | solution.py:336
  16.5 15.1 %collective-permute-start.3 = (bf16[4,256,256]{2,1,0:T(8,128)(2,1)S(1)}, bf16[4,256,256]{2,1,0:T(8,128)(2,1)}, u32[]{:S(2)}, u32[]{:S(2)}) collective-permute-start(bf16[4,256,256]{2,1,0:T(8,128)(2,1)S(1)} %pad_maximum_fusion.4.line_a), channel_id=1, source_target_pairs={{0,32},{1,9},{2,34},{3,11},{4,36},{5,13},{6,38},{7,15},{8,40},{9,1... | collective-permute-start | bytes 1572872 | tf_op jit(solution)/shard_map/items_up_a/ppermute | solution.py:336
  21.0 10.5 %collective-permute-start.1 = (bf16[1040,256]{1,0:T(8,128)(2,1)S(1)}, bf16[1040,256]{1,0:T(8,128)(2,1)S(1)}, u32[]{:S(2)}, u32[]{:S(2)}) collective-permute-start(bf16[1040,256]{1,0:T(8,128)(2,1)S(1)} %pad_maximum_fusion.3), channel_id=1, source_target_pairs={{0,2},{1,7},{2,4},{3,1},{4,6},{5,3},{6,0},{7,5},{8,10},{9,15},{10,... | collective-permute-start | bytes 1597448 | tf_op jit(solution)/shard_map/users_ring_2/ppermute | solution.py:319
  22.1 10.5 %copy-start.6 = (bf16[4,256,256]{2,1,0:T(8,128)(2,1)}, bf16[4,256,256]{2,1,0:T(8,128)(2,1)S(1)}, u32[]{:S(2)}) copy-start(bf16[4,256,256]{2,1,0:T(8,128)(2,1)S(1)} %constant_dynamic-update-slice_fusion.line_b) | copy-start | bytes 1572868
  22.1 10.5 %collective-permute-start.7 = (bf16[4,256,256]{2,1,0:T(8,128)(2,1)S(1)}, bf16[4,256,256]{2,1,0:T(8,128)(2,1)S(1)}, u32[]{:S(2)}, u32[]{:S(2)}) collective-permute-start(bf16[4,256,256]{2,1,0:T(8,128)(2,1)S(1)} %constant_dynamic-update-slice_fusion.line_b), channel_id=1, source_target_pairs={{0,32},{1,9},{2,34},{3,11},{4,36},{5,13},{6,38},{7,15},{8,40},{9,1... | collective-permute-start | bytes 1572872 | tf_op jit(solution)/shard_map/items_up_b/ppermute | solution.py:336
  24.0 9.3 %collective-permute-start.6 = (bf16[4,256,256]{2,1,0:T(8,128)(2,1)S(1)}, bf16[4,256,256]{2,1,0:T(8,128)(2,1)}, u32[]{:S(2)}, u32[]{:S(2)}) collective-permute-start(bf16[4,256,256]{2,1,0:T(8,128)(2,1)S(1)} %constant_dynamic-update-slice_fusion.line_b), channel_id=1, source_target_pairs={{0,96},{1,25},{2,98},{3,27},{4,100},{5,29},{6,102},{7,31},{8,104},... | collective-permute-start | bytes 1572872 | tf_op jit(solution)/shard_map/items_down_a/ppermute | solution.py:336
  34.0 0.8 copy-start.1
  36.1 5.0 %collective-permute-start.9 = (bf16[3104,256]{1,0:T(8,128)(2,1)}, bf16[3104,256]{1,0:T(8,128)(2,1)}, u32[]{:S(2)}, u32[]{:S(2)}) collective-permute-start(bf16[3104,256]{1,0:T(8,128)(2,1)} %pad_maximum_fusion), channel_id=1, source_target_pairs={{0,1},{1,0},{2,3},{3,2},{4,5},{5,4},{6,7},{7,6},{8,9},{9,8},{10,11... | collective-permute-start | bytes 4767752 | tf_op jit(solution)/shard_map/users_over/ppermute | solution.py:342
  36.3 10.7 %collective-permute-start.10 = (bf16[4,256,256]{2,1,0:T(8,128)(2,1)}, bf16[4,256,256]{2,1,0:T(8,128)(2,1)}, u32[]{:S(2)}, u32[]{:S(2)}) collective-permute-start(bf16[4,256,256]{2,1,0:T(8,128)(2,1)} %collective-permute-done.3.up_a), channel_id=1, source_target_pairs={{0,32},{1,9},{2,34},{3,11},{4,36},{5,13},{6,38},{7,15},{8,40},{9,1... | collective-permute-start | bytes 1572872 | tf_op jit(solution)/shard_map/items_up_2/ppermute | solution.py:336
  37.7 9.5 %collective-permute-start.11 = (bf16[4,256,256]{2,1,0:T(8,128)(2,1)}, bf16[4,256,256]{2,1,0:T(8,128)(2,1)}, u32[]{:S(2)}, u32[]{:S(2)}) collective-permute-start(bf16[4,256,256]{2,1,0:T(8,128)(2,1)} %collective-permute-done.6.down_a), channel_id=1, source_target_pairs={{0,96},{1,25},{2,98},{3,27},{4,100},{5,29},{6,102},{7,31},{8,104},... | collective-permute-start | bytes 1572872 | tf_op jit(solution)/shard_map/items_down_2/ppermute | solution.py:336
  41.1 1.0 copy-start.2
  42.1 5.0 %copy-start.3 = (bf16[4,256,256]{2,1,0:T(8,128)(2,1)S(1)}, bf16[4,256,256]{2,1,0:T(8,128)(2,1)}, u32[]{:S(2)}) copy-start(bf16[4,256,256]{2,1,0:T(8,128)(2,1)} %copy-done.1) | copy-start | bytes 1572868
  42.1 5.0 %copy-start.5 = (bf16[4,256,256]{2,1,0:T(8,128)(2,1)S(1)}, bf16[4,256,256]{2,1,0:T(8,128)(2,1)}, u32[]{:S(2)}) copy-start(bf16[4,256,256]{2,1,0:T(8,128)(2,1)} %copy-done.4) | copy-start | bytes 1572868
  42.1 5.0 %copy-start.7 = (bf16[4,256,256]{2,1,0:T(8,128)(2,1)S(1)}, bf16[4,256,256]{2,1,0:T(8,128)(2,1)}, u32[]{:S(2)}) copy-start(bf16[4,256,256]{2,1,0:T(8,128)(2,1)} %copy-done.6) | copy-start | bytes 1572868
  79.2 13.8 %collective-permute-start.12 = (bf16[20,256,256]{2,1,0:T(8,128)(2,1)}, bf16[20,256,256]{2,1,0:T(8,128)(2,1)S(1)}, u32[]{:S(2)}, u32[]{:S(2)}) collective-permute-start(bf16[20,256,256]{2,1,0:T(8,128)(2,1)} %get-tuple-element.15.give), channel_id=1, source_target_pairs={{0,1},{1,0},{2,3},{3,2},{4,5},{5,4},{6,7},{7,6},{8,9},{9,8},{10,11... | collective-permute-start | bytes 7864328 | tf_op jit(solution)/shard_map/give/ppermute | solution.py:342
  79.3 13.7 %collective-permute-start.18 = (bf16[4,256,256]{2,1,0:T(8,128)(2,1)S(1)}, bf16[4,256,256]{2,1,0:T(8,128)(2,1)S(1)}, u32[]{:S(2)}, u32[]{:S(2)}) collective-permute-start(bf16[4,256,256]{2,1,0:T(8,128)(2,1)S(1)} %get-tuple-element.21), channel_id=1, source_target_pairs={{0,96},{1,25},{2,98},{3,27},{4,100},{5,29},{6,102},{7,31},{8,104},... | collective-permute-start | bytes 1572872 | tf_op jit(solution)/shard_map/item_relay_down/ppermute | solution.py:336
  82.5 10.6 %collective-permute-start.23 = (bf16[4,256,256]{2,1,0:T(8,128)(2,1)S(1)}, bf16[4,256,256]{2,1,0:T(8,128)(2,1)S(1)}, u32[]{:S(2)}, u32[]{:S(2)}) collective-permute-start(bf16[4,256,256]{2,1,0:T(8,128)(2,1)S(1)} %get-tuple-element.26), channel_id=1, source_target_pairs={{0,32},{1,9},{2,34},{3,11},{4,36},{5,13},{6,38},{7,15},{8,40},{9,1... | collective-permute-start | bytes 1572872 | tf_op jit(solution)/shard_map/item_relay_up/ppermute | solution.py:336
  82.5 1.7 %collective-permute-start.19 = (f32[8,256]{1,0:T(8,128)S(1)}, f32[8,256]{1,0:T(8,128)S(1)}, u32[]{:S(2)}, u32[]{:S(2)}) collective-permute-start(f32[8,256]{1,0:T(8,128)S(1)} %get-tuple-element.22), channel_id=1, source_target_pairs={{0,1},{1,0},{2,3},{3,2},{4,5},{5,4},{6,7},{7,6},{8,9},{9,8},{10,11... | collective-permute-start | bytes 24584 | tf_op jit(solution)/shard_map/totals_0/ppermute | solution.py:325
  84.2 3.7 %collective-permute-start.20 = (f32[8,256]{1,0:T(8,128)S(1)}, f32[8,256]{1,0:T(8,128)S(1)}, u32[]{:S(2)}, u32[]{:S(2)}) collective-permute-start(f32[8,256]{1,0:T(8,128)S(1)} %add.128), channel_id=1, source_target_pairs={{0,2},{1,3},{2,0},{3,1},{4,6},{5,7},{6,4},{7,5},{8,10},{9,11},{10,... | collective-permute-start | bytes 24584 | tf_op jit(solution)/shard_map/totals_1/ppermute | solution.py:325
  87.8 5.2 %collective-permute-start.21 = (f32[8,256]{1,0:T(8,128)S(1)}, f32[8,256]{1,0:T(8,128)S(1)}, u32[]{:S(2)}, u32[]{:S(2)}) collective-permute-start(f32[8,256]{1,0:T(8,128)S(1)} %add.129), channel_id=1, source_target_pairs={{0,4},{1,5},{2,6},{3,7},{4,0},{5,1},{6,2},{7,3},{8,12},{9,13},{10,... | collective-permute-start | bytes 24584 | tf_op jit(solution)/shard_map/totals_2/ppermute | solution.py:325
  93.5 21.0 %collective-permute-start.24 = (bf16[8,256,256]{2,1,0:T(8,128)(2,1)S(1)}, bf16[8,256,256]{2,1,0:T(8,128)(2,1)S(1)}, u32[]{:S(2)}, u32[]{:S(2)}) collective-permute-start(bf16[8,256,256]{2,1,0:T(8,128)(2,1)S(1)} %pad_maximum_fusion.2), channel_id=1, source_target_pairs={{0,32},{1,9},{2,34},{3,11},{4,36},{5,13},{6,38},{7,15},{8,40},{9,1... | collective-permute-start | bytes 3145736 | tf_op jit(solution)/shard_map/item_up/ppermute | solution.py:336
  95.0 19.5 %collective-permute-start.22 = (bf16[8,256,256]{2,1,0:T(8,128)(2,1)S(1)}, bf16[8,256,256]{2,1,0:T(8,128)(2,1)S(1)}, u32[]{:S(2)}, u32[]{:S(2)}) collective-permute-start(bf16[8,256,256]{2,1,0:T(8,128)(2,1)S(1)} %pad_maximum_fusion.1), channel_id=1, source_target_pairs={{0,96},{1,25},{2,98},{3,27},{4,100},{5,29},{6,102},{7,31},{8,104},... | collective-permute-start | bytes 3145736 | tf_op jit(solution)/shard_map/item_down/ppermute | solution.py:336
  97.4 12.3 %collective-permute-start.13 = (bf16[4,256,256]{2,1,0:T(8,128)(2,1)S(1)}, bf16[4,256,256]{2,1,0:T(8,128)(2,1)S(1)}, u32[]{:S(2)}, u32[]{:S(2)}) collective-permute-start(bf16[4,256,256]{2,1,0:T(8,128)(2,1)S(1)} %get-tuple-element.32), channel_id=1, source_target_pairs={{0,2},{1,7},{2,4},{3,1},{4,6},{5,3},{6,0},{7,5},{8,10},{9,15},{10,... | collective-permute-start | bytes 1572872 | tf_op jit(solution)/shard_map/user_early/ppermute | solution.py:319
  99.4 14.1 %collective-permute-start.14 = (bf16[4,256,256]{2,1,0:T(8,128)(2,1)S(1)}, bf16[4,256,256]{2,1,0:T(8,128)(2,1)S(1)}, u32[]{:S(2)}, u32[]{:S(2)}) collective-permute-start(bf16[4,256,256]{2,1,0:T(8,128)(2,1)S(1)} %get-tuple-element.31), channel_id=1, source_target_pairs={{0,2},{1,7},{2,4},{3,1},{4,6},{5,3},{6,0},{7,5},{8,10},{9,15},{10,... | collective-permute-start | bytes 1572872 | tf_op jit(solution)/shard_map/user_relay/ppermute | solution.py:319
  100.7 3.8 %collective-permute-start.25 = (f32[8,256]{1,0:T(8,128)S(1)}, f32[8,256]{1,0:T(8,128)S(1)}, u32[]{:S(2)}, u32[]{:S(2)}) collective-permute-start(f32[8,256]{1,0:T(8,128)S(1)} %get-tuple-element.40), channel_id=1, source_target_pairs={{0,8},{1,9},{2,10},{3,11},{4,12},{5,13},{6,14},{7,15},{8,0},{9,1},... | collective-permute-start | bytes 24584 | tf_op jit(solution)/shard_map/totals_3/ppermute | solution.py:325
  104.5 5.2 %collective-permute-start.26 = (f32[8,256]{1,0:T(8,128)S(1)}, f32[8,256]{1,0:T(8,128)S(1)}, u32[]{:S(2)}, u32[]{:S(2)}) collective-permute-start(f32[8,256]{1,0:T(8,128)S(1)} %add.139), channel_id=1, source_target_pairs={{0,16},{1,17},{2,18},{3,19},{4,20},{5,21},{6,22},{7,23},{8,24},{9,... | collective-permute-start | bytes 24584 | tf_op jit(solution)/shard_map/totals_4/ppermute | solution.py:325
  109.7 11.0 %collective-permute-start.30 = (f32[8,256]{1,0:T(8,128)S(1)}, f32[8,256]{1,0:T(8,128)S(1)}, u32[]{:S(2)}, u32[]{:S(2)}) collective-permute-start(f32[8,256]{1,0:T(8,128)S(1)} %get-tuple-element.30), channel_id=1, source_target_pairs={{0,32},{1,33},{2,34},{3,35},{4,36},{5,37},{6,38},{7,39},{8,40},{9,... | collective-permute-start | bytes 24584 | tf_op jit(solution)/shard_map/totals_5/ppermute | solution.py:325
  113.7 12.4 %collective-permute-start.15 = (bf16[4,256,256]{2,1,0:T(8,128)(2,1)S(1)}, bf16[4,256,256]{2,1,0:T(8,128)(2,1)S(1)}, u32[]{:S(2)}, u32[]{:S(2)}) collective-permute-start(bf16[4,256,256]{2,1,0:T(8,128)(2,1)S(1)} %add_convert_fusion), channel_id=1, source_target_pairs={{0,2},{1,7},{2,4},{3,1},{4,6},{5,3},{6,0},{7,5},{8,10},{9,15},{10,... | collective-permute-start | bytes 1572872 | tf_op jit(solution)/shard_map/user_late/ppermute | solution.py:319
  115.2 14.0 %copy-start = (bf16[20,256,256]{2,1,0:T(8,128)(2,1)S(1)}, bf16[20,256,256]{2,1,0:T(8,128)(2,1)}, u32[]{:S(2)}) copy-start(bf16[20,256,256]{2,1,0:T(8,128)(2,1)} %get-tuple-element.15.give) | copy-start | bytes 7864324
  115.2 13.0 %collective-permute-start.29 = (bf16[2,256,256]{2,1,0:T(8,128)(2,1)S(1)}, bf16[2,256,256]{2,1,0:T(8,128)(2,1)S(1)}, u32[]{:S(2)}, u32[]{:S(2)}) collective-permute-start(bf16[2,256,256]{2,1,0:T(8,128)(2,1)S(1)} %bitcast.49), channel_id=1, source_target_pairs={{0,8},{1,33},{2,10},{3,35},{4,12},{5,37},{6,14},{7,39},{8,16},{9,4... | collective-permute-start | bytes 786440 | tf_op jit(solution)/shard_map/item_back/ppermute | solution.py:330
  116.2 12.0 %collective-permute-start.27 = (bf16[2,256,256]{2,1,0:T(8,128)(2,1)S(1)}, bf16[2,256,256]{2,1,0:T(8,128)(2,1)S(1)}, u32[]{:S(2)}, u32[]{:S(2)}) collective-permute-start(bf16[2,256,256]{2,1,0:T(8,128)(2,1)S(1)} %bitcast.48), channel_id=1, source_target_pairs={{0,24},{1,97},{2,26},{3,99},{4,28},{5,101},{6,30},{7,103},{8,0},{9... | collective-permute-start | bytes 786440 | tf_op jit(solution)/shard_map/item_back/ppermute | solution.py:330
  118.5 9.7 %collective-permute-start.28 = (bf16[2,256,256]{2,1,0:T(8,128)(2,1)S(1)}, bf16[2,256,256]{2,1,0:T(8,128)(2,1)S(1)}, u32[]{:S(2)}, u32[]{:S(2)}) collective-permute-start(bf16[2,256,256]{2,1,0:T(8,128)(2,1)S(1)} %bitcast.47), channel_id=1, source_target_pairs={{0,16},{1,65},{2,18},{3,67},{4,20},{5,69},{6,22},{7,71},{8,24},{9,... | collective-permute-start | bytes 786440 | tf_op jit(solution)/shard_map/item_back/ppermute | solution.py:330
  120.6 5.3 %collective-permute-start.31 = (f32[8,256]{1,0:T(8,128)S(1)}, f32[8,256]{1,0:T(8,128)S(1)}, u32[]{:S(2)}, u32[]{:S(2)}) collective-permute-start(f32[8,256]{1,0:T(8,128)S(1)} %add.146), channel_id=1, source_target_pairs={{0,64},{1,65},{2,66},{3,67},{4,68},{5,69},{6,70},{7,71},{8,72},{9,... | collective-permute-start | bytes 24584 | tf_op jit(solution)/shard_map/totals_6/ppermute | solution.py:325
  125.9 3.2 %collective-permute-start.16 = (bf16[4,256,256]{2,1,0:T(8,128)(2,1)S(1)}, bf16[4,256,256]{2,1,0:T(8,128)(2,1)S(1)}, u32[]{:S(2)}, u32[]{:S(2)}) collective-permute-start(bf16[4,256,256]{2,1,0:T(8,128)(2,1)S(1)} %collective-permute-done.13.early), channel_id=1, source_target_pairs={{0,1},{1,0},{2,3},{3,2},{4,5},{5,4},{6,7},{7,6},{8,9},{9,8},{10,11... | collective-permute-start | bytes 1572872 | tf_op jit(solution)/shard_map/early_over/ppermute | solution.py:342
  126.1 3.1 %collective-permute-start.17 = (bf16[4,256,256]{2,1,0:T(8,128)(2,1)S(1)}, bf16[4,256,256]{2,1,0:T(8,128)(2,1)S(1)}, u32[]{:S(2)}, u32[]{:S(2)}) collective-permute-start(bf16[4,256,256]{2,1,0:T(8,128)(2,1)S(1)} %collective-permute-done.15.late), channel_id=1, source_target_pairs={{0,1},{1,0},{2,3},{3,2},{4,5},{5,4},{6,7},{7,6},{8,9},{9,8},{10,11... | collective-permute-start | bytes 1572872 | tf_op jit(solution)/shard_map/late_over/ppermute | solution.py:342

commit v5 on v4

--- a/solution.py
+++ b/solution.py
@@ -170,7 +170,7 @@
             return none
         lax.fori_loop(0, h, one, 0)
 
-    turn = 8
+    turn = 16
     a_phase = 16 // turn
 
     def phase(p, carry):
@@ -207,12 +207,12 @@
 
         @pl.when(p == 3)
         def _():
+            for k in (1, 2, 3, 5, 6):
+                out[k].start()
             item_lower(2 * n, 0)
             out[7].start()
             item_lower(2 * n + h, h)
             out[8].start()
-            for k in (1, 2, 3, 5, 6):
-                out[k].start()
             item_lower(n + h, 2 * h)
             out[9].start()
             item_lower(3 * n, 3 * h)

time: 133 us -> 133 us (level)
  no operation moved by 1% of the time
where the time goes in v5:
time: 133 us; the launch traced here: 131 us
  starting transfers between devices  45.7 us (34%)
  Pallas kernels  35.4 us (27%)
  waiting for transfers between devices  34.9 us (26%)
  other arithmetic  7.21 us (5%)
  local copies, waits for them, and re-layouts  4.42 us (3%)
  between operations  3.59 us (3%)
    pallas_call x1, Pallas kernels, score(): pl.pallas_call(score_kernel, in_specs=[smem, smem, smem] + [any_] * len(p...  31.2 us
    ppermute x10, starting transfers between devices, along_second(): lax.ppermute(a, AXES, [(device(x, y, z, c), device(x + (0 if c else d), y...  15.9 us
    ppermute x7, waiting for transfers between devices, swap(): return lax.ppermute(a, AXES, [(i, i ^ bit) for i in range(128)])  13.5 us
    ppermute x5, waiting for transfers between devices, along_z(): lax.ppermute(a, AXES, [(device(x, y, z, c), device(x, y, z + (-1 if c els...  13.2 us
    ppermute x6, starting transfers between devices, along_first(): lax.ppermute(a, AXES, [(device(x, y, z, c), device(x + (d if c else 0), y...  11.3 us
    ppermute x7, starting transfers between devices, swap(): return lax.ppermute(a, AXES, [(i, i ^ bit) for i in range(128)])  11.1 us
    ppermute x5, starting transfers between devices, along_z(): lax.ppermute(a, AXES, [(device(x, y, z, c), device(x, y, z + (-1 if c els...  6.51 us
    ppermute x10, waiting for transfers between devices, along_second(): lax.ppermute(a, AXES, [(device(x, y, z, c), device(x + (0 if c else d), y...  5.27 us
  transfers between devices with their start and end apart: 32, of which 15 were waited for; matrix products, arithmetic and copies ran while one was open for 4% of the time, Pallas kernels for 1%

profile of v5, /device:TPU:0, one launch (start us, length us, event | category | flops | bytes accessed | tf_op | source)
XLA Modules:
  0.0 131.2 jit_solution(9872095659926052138)
XLA Ops:
  1.3 0.7 copy.11
  2.0 1.7 %convert.13 = bf16[4,512,256]{2,1,0:T(8,128)(2,1)S(1)} convert(f32[4,512,256]{2,1,0:T(8,128)} %param.6) | non-fusion elementwise | flops 524288 | bytes 3145728 | tf_op jit(solution)/shard_map/convert.6
  3.8 2.1 %collective-permute-start = (bf16[2064,256]{1,0:T(8,128)(2,1)S(1)}, bf16[2064,256]{1,0:T(8,128)(2,1)S(1)}, u32[]{:S(2)}, u32[]{:S(2)}) collective-permute-start(bf16[2064,256]{1,0:T(8,128)(2,1)S(1)} %fusion.1.own), channel_id=1, source_target_pairs={{0,2},{1,7},{2,4},{3,1},{4,6},{5,3},{6,0},{7,5},{8,10},{9,15},{10,... | collective-permute-start | bytes 3170312 | tf_op jit(solution)/shard_map/users_ring/ppermute | solution.py:319
  5.9 1.6 %collective-permute-start.2 = (bf16[2,256,256]{2,1,0:T(8,128)(2,1)S(1)}, bf16[2,256,256]{2,1,0:T(8,128)(2,1)S(1)}, u32[]{:S(2)}, u32[]{:S(2)}) collective-permute-start(bf16[2,256,256]{2,1,0:T(8,128)(2,1)S(1)} %convert_element_type.82), channel_id=1, source_target_pairs={{0,8},{1,33},{2,10},{3,35},{4,12},{5,37},{6,14},{7,39},{8,16},{9,4... | collective-permute-start | bytes 786440 | tf_op jit(solution)/shard_map/items_line/ppermute | solution.py:330
  7.6 2.9 %collective-permute-start.4 = (bf16[2,256,256]{2,1,0:T(8,128)(2,1)S(1)}, bf16[2,256,256]{2,1,0:T(8,128)(2,1)S(1)}, u32[]{:S(2)}, u32[]{:S(2)}) collective-permute-start(bf16[2,256,256]{2,1,0:T(8,128)(2,1)S(1)} %convert_element_type.82), channel_id=1, source_target_pairs={{0,16},{1,65},{2,18},{3,67},{4,20},{5,69},{6,22},{7,71},{8,24},{9,... | collective-permute-start | bytes 786440 | tf_op jit(solution)/shard_map/items_line/ppermute | solution.py:330
  10.5 1.3 %collective-permute-start.5 = (bf16[2,256,256]{2,1,0:T(8,128)(2,1)S(1)}, bf16[2,256,256]{2,1,0:T(8,128)(2,1)}, u32[]{:S(2)}, u32[]{:S(2)}) collective-permute-start(bf16[2,256,256]{2,1,0:T(8,128)(2,1)S(1)} %convert_element_type.82), channel_id=1, source_target_pairs={{0,24},{1,97},{2,26},{3,99},{4,28},{5,101},{6,30},{7,103},{8,0},{9... | collective-permute-start | bytes 786440 | tf_op jit(solution)/shard_map/items_line/ppermute | solution.py:330
  11.8 1.8 %collective-permute-done.2 = bf16[2,256,256]{2,1,0:T(8,128)(2,1)S(1)} collective-permute-done((bf16[2,256,256]{2,1,0:T(8,128)(2,1)S(1)}, bf16[2,256,256]{2,1,0:T(8,128)(2,1)S(1)}, u32[]{:S(2)}, u32[]{:S(2)}) %collective-permute-start.2) | collective-permute-done | bytes 262176 | tf_op jit(solution)/shard_map/items_line/ppermute | solution.py:330
  13.7 2.8 %collective-permute-start.8 = (bf16[4,256,256]{2,1,0:T(8,128)(2,1)S(1)}, bf16[4,256,256]{2,1,0:T(8,128)(2,1)S(1)}, u32[]{:S(2)}, u32[]{:S(2)}) collective-permute-start(bf16[4,256,256]{2,1,0:T(8,128)(2,1)S(1)} %pad_maximum_fusion.4.line_a), channel_id=1, source_target_pairs={{0,96},{1,25},{2,98},{3,27},{4,100},{5,29},{6,102},{7,31},{8,104},... | collective-permute-start | bytes 1572872 | tf_op jit(solution)/shard_map/items_down_b/ppermute | solution.py:336
  16.5 1.2 collective-permute-done.4
  17.7 3.2 %collective-permute-done.ring = bf16[2064,256]{1,0:T(8,128)(2,1)S(1)} collective-permute-done((bf16[2064,256]{1,0:T(8,128)(2,1)S(1)}, bf16[2064,256]{1,0:T(8,128)(2,1)S(1)}, u32[]{:S(2)}, u32[]{:S(2)}) %collective-permute-start) | collective-permute-done | bytes 1056800 | tf_op jit(solution)/shard_map/users_ring/ppermute | solution.py:319
  21.0 0.1 collective-permute-start.1
  21.1 1.0 constant_dynamic-update-slice_fusion.line_b
  22.1 1.9 %collective-permute-start.7 = (bf16[4,256,256]{2,1,0:T(8,128)(2,1)S(1)}, bf16[4,256,256]{2,1,0:T(8,128)(2,1)S(1)}, u32[]{:S(2)}, u32[]{:S(2)}) collective-permute-start(bf16[4,256,256]{2,1,0:T(8,128)(2,1)S(1)} %constant_dynamic-update-slice_fusion.line_b), channel_id=1, source_target_pairs={{0,32},{1,9},{2,34},{3,11},{4,36},{5,13},{6,38},{7,15},{8,40},{9,1... | collective-permute-start | bytes 1572872 | tf_op jit(solution)/shard_map/items_up_b/ppermute | solution.py:336
  24.0 1.4 %collective-permute-start.6 = (bf16[4,256,256]{2,1,0:T(8,128)(2,1)S(1)}, bf16[4,256,256]{2,1,0:T(8,128)(2,1)}, u32[]{:S(2)}, u32[]{:S(2)}) collective-permute-start(bf16[4,256,256]{2,1,0:T(8,128)(2,1)S(1)} %constant_dynamic-update-slice_fusion.line_b), channel_id=1, source_target_pairs={{0,96},{1,25},{2,98},{3,27},{4,100},{5,29},{6,102},{7,31},{8,104},... | collective-permute-start | bytes 1572872 | tf_op jit(solution)/shard_map/items_down_a/ppermute | solution.py:336
  25.4 6.2 %collective-permute-done.1.ring_2 = bf16[1040,256]{1,0:T(8,128)(2,1)S(1)} collective-permute-done((bf16[1040,256]{1,0:T(8,128)(2,1)S(1)}, bf16[1040,256]{1,0:T(8,128)(2,1)S(1)}, u32[]{:S(2)}, u32[]{:S(2)}) %collective-permute-start.1) | collective-permute-done | bytes 532512 | tf_op jit(solution)/shard_map/users_ring_2/ppermute | solution.py:319
  31.6 0.9 collective-permute-done.7.rest_0_.up_b
  32.5 0.8 collective-permute-done.6.down_a
  33.3 0.7 fusion.8
  34.0 0.8 copy-done.1
  34.8 1.2 pad_maximum_fusion
  36.1 0.3 collective-permute-start.9
  36.3 1.3 %collective-permute-start.10 = (bf16[4,256,256]{2,1,0:T(8,128)(2,1)}, bf16[4,256,256]{2,1,0:T(8,128)(2,1)}, u32[]{:S(2)}, u32[]{:S(2)}) collective-permute-start(bf16[4,256,256]{2,1,0:T(8,128)(2,1)} %collective-permute-done.3.up_a), channel_id=1, source_target_pairs={{0,32},{1,9},{2,34},{3,11},{4,36},{5,13},{6,38},{7,15},{8,40},{9,1... | collective-permute-start | bytes 1572872 | tf_op jit(solution)/shard_map/items_up_2/ppermute | solution.py:336
  37.7 1.9 %collective-permute-start.11 = (bf16[4,256,256]{2,1,0:T(8,128)(2,1)}, bf16[4,256,256]{2,1,0:T(8,128)(2,1)}, u32[]{:S(2)}, u32[]{:S(2)}) collective-permute-start(bf16[4,256,256]{2,1,0:T(8,128)(2,1)} %collective-permute-done.6.down_a), channel_id=1, source_target_pairs={{0,96},{1,25},{2,98},{3,27},{4,100},{5,29},{6,102},{7,31},{8,104},... | collective-permute-start | bytes 1572872 | tf_op jit(solution)/shard_map/items_down_2/ppermute | solution.py:336
  40.9 0.1 pad_add_fusion.place
  41.0 0.1 pad_maximum_fusion.5.scalars
  41.1 1.0 copy-done.2
  42.1 1.5 %shard_map.85.jobs = s32[64,128]{1,0:T(8,128)S(1)} custom-call(s32[4]{0:T(128)S(1)} %pad_add_fusion.place, bf16[2064,256]{1,0:T(8,128)(2,1)S(1)} %fusion.1.own, bf16[2064,256]{1,0:T(8,128)(2,1)S(1)} %collective-permute-done.ring, bf16[1040,256]{1,0:T(8,128)(2,1)S(1)} %collective-permute-done.1.ring_2, bf16[3104,256]{1,0:T(8,128)(2,1)} %collective-permute-done.9.over, ...), custom_call_target="tpu_custom_call" | custom-call | flops 1000000 | bytes 1048576 | tf_op jit(solution)/shard_map/pallas_call | solution.py:58
  43.6 3.5 %collective-permute-done.10.up_2 = bf16[4,256,256]{2,1,0:T(8,128)(2,1)} collective-permute-done((bf16[4,256,256]{2,1,0:T(8,128)(2,1)}, bf16[4,256,256]{2,1,0:T(8,128)(2,1)}, u32[]{:S(2)}, u32[]{:S(2)}) %collective-permute-start.10) | collective-permute-done | bytes 524320 | tf_op jit(solution)/shard_map/items_up_2/ppermute | solution.py:336
  47.1 0.1 collective-permute-done.11.down_2
  47.2 31.2 %shard_map.86 = (f32[4,256,256]{2,1,0:T(8,128)S(1)}, f32[4,256,256]{2,1,0:T(8,128)S(1)}, f32[4,256,256]{2,1,0:T(8,128)S(1)}, bf16[20,256,256]{2,1,0:T(8,128)(2,1...) custom-call(s32[4]{0:T(128)S(1)} %pad_add_fusion.place, ...), custom_call_target="tpu_custom_call" | custom-call | flops 12999999488 | bytes 20971520 | tf_op jit(solution)/shard_map/pallas_call | solution.py:250
  78.4 0.1 collective-permute-start.12
  78.5 3.2 %collective-permute-start.18 = (bf16[4,256,256]{2,1,0:T(8,128)(2,1)S(1)}, bf16[4,256,256]{2,1,0:T(8,128)(2,1)S(1)}, u32[]{:S(2)}, u32[]{:S(2)}) collective-permute-start(bf16[4,256,256]{2,1,0:T(8,128)(2,1)S(1)} %get-tuple-element.21), channel_id=1, source_target_pairs={{0,96},{1,25},{2,98},{3,27},{4,100},{5,29},{6,102},{7,31},{8,104},... | collective-permute-start | bytes 1572872 | tf_op jit(solution)/shard_map/item_relay_down/ppermute | solution.py:336
  81.7 1.7 %collective-permute-done.19 = f32[8,256]{1,0:T(8,128)S(1)} collective-permute-done((f32[8,256]{1,0:T(8,128)S(1)}, f32[8,256]{1,0:T(8,128)S(1)}, u32[]{:S(2)}, u32[]{:S(2)}) %collective-permute-start.19) | collective-permute-done | bytes 8224 | tf_op jit(solution)/shard_map/totals_0/ppermute | solution.py:325
  83.4 2.0 %collective-permute-start.20 = (f32[8,256]{1,0:T(8,128)S(1)}, f32[8,256]{1,0:T(8,128)S(1)}, u32[]{:S(2)}, u32[]{:S(2)}) collective-permute-start(f32[8,256]{1,0:T(8,128)S(1)} %add.128), channel_id=1, source_target_pairs={{0,2},{1,3},{2,0},{3,1},{4,6},{5,7},{6,4},{7,5},{8,10},{9,11},{10,... | collective-permute-start | bytes 24584 | tf_op jit(solution)/shard_map/totals_1/ppermute | solution.py:325
  85.3 1.7 %collective-permute-done.20 = f32[8,256]{1,0:T(8,128)S(1)} collective-permute-done((f32[8,256]{1,0:T(8,128)S(1)}, f32[8,256]{1,0:T(8,128)S(1)}, u32[]{:S(2)}, u32[]{:S(2)}) %collective-permute-start.20) | collective-permute-done | bytes 8224 | tf_op jit(solution)/shard_map/totals_1/ppermute | solution.py:325
  87.0 3.3 %collective-permute-start.21 = (f32[8,256]{1,0:T(8,128)S(1)}, f32[8,256]{1,0:T(8,128)S(1)}, u32[]{:S(2)}, u32[]{:S(2)}) collective-permute-start(f32[8,256]{1,0:T(8,128)S(1)} %add.129), channel_id=1, source_target_pairs={{0,4},{1,5},{2,6},{3,7},{4,0},{5,1},{6,2},{7,3},{8,12},{9,13},{10,... | collective-permute-start | bytes 24584 | tf_op jit(solution)/shard_map/totals_2/ppermute | solution.py:325
  90.4 1.8 %collective-permute-done.21 = f32[8,256]{1,0:T(8,128)S(1)} collective-permute-done((f32[8,256]{1,0:T(8,128)S(1)}, f32[8,256]{1,0:T(8,128)S(1)}, u32[]{:S(2)}, u32[]{:S(2)}) %collective-permute-start.21) | collective-permute-done | bytes 8224 | tf_op jit(solution)/shard_map/totals_2/ppermute | solution.py:325
  92.3 0.3 fusion.2
  92.6 0.1 pad_maximum_fusion.2
  92.7 1.3 %collective-permute-start.24 = (bf16[8,256,256]{2,1,0:T(8,128)(2,1)S(1)}, bf16[8,256,256]{2,1,0:T(8,128)(2,1)S(1)}, u32[]{:S(2)}, u32[]{:S(2)}) collective-permute-start(bf16[8,256,256]{2,1,0:T(8,128)(2,1)S(1)} %pad_maximum_fusion.2), channel_id=1, source_target_pairs={{0,32},{1,9},{2,34},{3,11},{4,36},{5,13},{6,38},{7,15},{8,40},{9,1... | collective-permute-start | bytes 3145736 | tf_op jit(solution)/shard_map/item_up/ppermute | solution.py:336
  94.1 0.1 pad_maximum_fusion.1
  94.2 2.0 %collective-permute-start.22 = (bf16[8,256,256]{2,1,0:T(8,128)(2,1)S(1)}, bf16[8,256,256]{2,1,0:T(8,128)(2,1)S(1)}, u32[]{:S(2)}, u32[]{:S(2)}) collective-permute-start(bf16[8,256,256]{2,1,0:T(8,128)(2,1)S(1)} %pad_maximum_fusion.1), channel_id=1, source_target_pairs={{0,96},{1,25},{2,98},{3,27},{4,100},{5,29},{6,102},{7,31},{8,104},... | collective-permute-start | bytes 3145736 | tf_op jit(solution)/shard_map/item_down/ppermute | solution.py:336
  96.2 0.4 add_convert_fusion.1
  96.6 2.2 %collective-permute-start.13 = (bf16[4,256,256]{2,1,0:T(8,128)(2,1)S(1)}, bf16[4,256,256]{2,1,0:T(8,128)(2,1)S(1)}, u32[]{:S(2)}, u32[]{:S(2)}) collective-permute-start(bf16[4,256,256]{2,1,0:T(8,128)(2,1)S(1)} %get-tuple-element.32), channel_id=1, source_target_pairs={{0,2},{1,7},{2,4},{3,1},{4,6},{5,3},{6,0},{7,5},{8,10},{9,15},{10,... | collective-permute-start | bytes 1572872 | tf_op jit(solution)/shard_map/user_early/ppermute | solution.py:319
  98.8 1.3 collective-permute-start.14
  100.1 1.2 collective-permute-start.25
  101.4 2.6 %collective-permute-done.25 = f32[8,256]{1,0:T(8,128)S(1)} collective-permute-done((f32[8,256]{1,0:T(8,128)S(1)}, f32[8,256]{1,0:T(8,128)S(1)}, u32[]{:S(2)}, u32[]{:S(2)}) %collective-permute-start.25) | collective-permute-done | bytes 8224 | tf_op jit(solution)/shard_map/totals_3/ppermute | solution.py:325
  103.9 3.3 %collective-permute-start.26 = (f32[8,256]{1,0:T(8,128)S(1)}, f32[8,256]{1,0:T(8,128)S(1)}, u32[]{:S(2)}, u32[]{:S(2)}) collective-permute-start(f32[8,256]{1,0:T(8,128)S(1)} %add.139), channel_id=1, source_target_pairs={{0,16},{1,17},{2,18},{3,19},{4,20},{5,21},{6,22},{7,23},{8,24},{9,... | collective-permute-start | bytes 24584 | tf_op jit(solution)/shard_map/totals_4/ppermute | solution.py:325
  107.2 1.9 %collective-permute-done.26 = f32[8,256]{1,0:T(8,128)S(1)} collective-permute-done((f32[8,256]{1,0:T(8,128)S(1)}, f32[8,256]{1,0:T(8,128)S(1)}, u32[]{:S(2)}, u32[]{:S(2)}) %collective-permute-start.26) | collective-permute-done | bytes 8224 | tf_op jit(solution)/shard_map/totals_4/ppermute | solution.py:325
  109.1 3.8 %collective-permute-done.14 = bf16[4,256,256]{2,1,0:T(8,128)(2,1)S(1)} collective-permute-done((bf16[4,256,256]{2,1,0:T(8,128)(2,1)S(1)}, bf16[4,256,256]{2,1,0:T(8,128)(2,1)S(1)}, u32[]{:S(2)}, u32[]{:S(2)}) %collective-permute-start.14) | collective-permute-done | bytes 524320 | tf_op jit(solution)/shard_map/user_relay/ppermute | solution.py:319
  112.9 0.2 add_convert_fusion
  113.1 0.8 collective-permute-start.15
  113.9 0.4 convert_add_fusion
  114.4 0.2 fusion.11
  114.7 1.0 collective-permute-start.29
  115.7 2.3 %collective-permute-start.27 = (bf16[2,256,256]{2,1,0:T(8,128)(2,1)S(1)}, bf16[2,256,256]{2,1,0:T(8,128)(2,1)S(1)}, u32[]{:S(2)}, u32[]{:S(2)}) collective-permute-start(bf16[2,256,256]{2,1,0:T(8,128)(2,1)S(1)} %bitcast.48), channel_id=1, source_target_pairs={{0,24},{1,97},{2,26},{3,99},{4,28},{5,101},{6,30},{7,103},{8,0},{9... | collective-permute-start | bytes 786440 | tf_op jit(solution)/shard_map/item_back/ppermute | solution.py:330
  118.0 2.1 %collective-permute-start.28 = (bf16[2,256,256]{2,1,0:T(8,128)(2,1)S(1)}, bf16[2,256,256]{2,1,0:T(8,128)(2,1)S(1)}, u32[]{:S(2)}, u32[]{:S(2)}) collective-permute-start(bf16[2,256,256]{2,1,0:T(8,128)(2,1)S(1)} %bitcast.47), channel_id=1, source_target_pairs={{0,16},{1,65},{2,18},{3,67},{4,20},{5,69},{6,22},{7,71},{8,24},{9,... | collective-permute-start | bytes 786440 | tf_op jit(solution)/shard_map/item_back/ppermute | solution.py:330
  120.1 1.3 %collective-permute-start.31 = (f32[8,256]{1,0:T(8,128)S(1)}, f32[8,256]{1,0:T(8,128)S(1)}, u32[]{:S(2)}, u32[]{:S(2)}) collective-permute-start(f32[8,256]{1,0:T(8,128)S(1)} %add.146), channel_id=1, source_target_pairs={{0,64},{1,65},{2,66},{3,67},{4,68},{5,69},{6,70},{7,71},{8,72},{9,... | collective-permute-start | bytes 24584 | tf_op jit(solution)/shard_map/totals_6/ppermute | solution.py:325
  121.4 3.8 %collective-permute-done.31 = f32[8,256]{1,0:T(8,128)S(1)} collective-permute-done((f32[8,256]{1,0:T(8,128)S(1)}, f32[8,256]{1,0:T(8,128)S(1)}, u32[]{:S(2)}, u32[]{:S(2)}) %collective-permute-start.31) | collective-permute-done | bytes 8224 | tf_op jit(solution)/shard_map/totals_6/ppermute | solution.py:325
  125.2 0.5 collective-permute-start.17
  125.7 0.6 slice.111
  127.0 0.5 fusion.10
  127.6 0.9 fusion.5
  128.5 2.8 %shard_map.87 = f32[4,512,256]{2,1,0:T(8,128)} custom-call(s32[4]{0:T(128)S(1)} %pad_add_fusion.place, bf16[20,256,256]{2,1,0:T(8,128)(2,1)S(1)} %copy-done, bf16[20,256,256]{2,1,0:T(8,128)(2,1)S(1)} %collective-permute-done.12.given, bf16[4,256,256]{2,1,0:T(8,128)(2,1)S(1)} %collective-permute-done.13.early, ...), custom_call_target="tpu_custom_call" | custom-call | flops 2000000 | bytes 6291456 | tf_op jit(solution)/shard_map/pallas_call | solution.py:288
  (59 shorter events, 0.6 us)
Async XLA Ops:
  3.7 2.3 %copy-start.8 = (f32[2,256,256]{2,1,0:T(8,128)S(1)}, f32[2,256,256]{2,1,0:T(8,128)}, u32[]{:S(2)}) copy-start(f32[2,256,256]{2,1,0:T(8,128)} %param.7) | copy-start | bytes 1572868
  3.8 17.1 %collective-permute-start = (bf16[2064,256]{1,0:T(8,128)(2,1)S(1)}, bf16[2064,256]{1,0:T(8,128)(2,1)S(1)}, u32[]{:S(2)}, u32[]{:S(2)}) collective-permute-start(bf16[2064,256]{1,0:T(8,128)(2,1)S(1)} %fusion.1.own), channel_id=1, source_target_pairs={{0,2},{1,7},{2,4},{3,1},{4,6},{5,3},{6,0},{7,5},{8,10},{9,15},{10,... | collective-permute-start | bytes 3170312 | tf_op jit(solution)/shard_map/users_ring/ppermute | solution.py:319
  5.9 7.7 %collective-permute-start.2 = (bf16[2,256,256]{2,1,0:T(8,128)(2,1)S(1)}, bf16[2,256,256]{2,1,0:T(8,128)(2,1)S(1)}, u32[]{:S(2)}, u32[]{:S(2)}) collective-permute-start(bf16[2,256,256]{2,1,0:T(8,128)(2,1)S(1)} %convert_element_type.82), channel_id=1, source_target_pairs={{0,8},{1,33},{2,10},{3,35},{4,12},{5,37},{6,14},{7,39},{8,16},{9,4... | collective-permute-start | bytes 786440 | tf_op jit(solution)/shard_map/items_line/ppermute | solution.py:330
  7.6 10.1 %collective-permute-start.4 = (bf16[2,256,256]{2,1,0:T(8,128)(2,1)S(1)}, bf16[2,256,256]{2,1,0:T(8,128)(2,1)S(1)}, u32[]{:S(2)}, u32[]{:S(2)}) collective-permute-start(bf16[2,256,256]{2,1,0:T(8,128)(2,1)S(1)} %convert_element_type.82), channel_id=1, source_target_pairs={{0,16},{1,65},{2,18},{3,67},{4,20},{5,69},{6,22},{7,71},{8,24},{9,... | collective-permute-start | bytes 786440 | tf_op jit(solution)/shard_map/items_line/ppermute | solution.py:330
  10.5 10.6 %collective-permute-start.5 = (bf16[2,256,256]{2,1,0:T(8,128)(2,1)S(1)}, bf16[2,256,256]{2,1,0:T(8,128)(2,1)}, u32[]{:S(2)}, u32[]{:S(2)}) collective-permute-start(bf16[2,256,256]{2,1,0:T(8,128)(2,1)S(1)} %convert_element_type.82), channel_id=1, source_target_pairs={{0,24},{1,97},{2,26},{3,99},{4,28},{5,101},{6,30},{7,103},{8,0},{9... | collective-permute-start | bytes 786440 | tf_op jit(solution)/shard_map/items_line/ppermute | solution.py:330
  13.6 17.9 %copy-start.4 = (bf16[4,256,256]{2,1,0:T(8,128)(2,1)}, bf16[4,256,256]{2,1,0:T(8,128)(2,1)S(1)}, u32[]{:S(2)}) copy-start(bf16[4,256,256]{2,1,0:T(8,128)(2,1)S(1)} %pad_maximum_fusion.4.line_a) | copy-start | bytes 1572868
  13.7 17.9 %collective-permute-start.8 = (bf16[4,256,256]{2,1,0:T(8,128)(2,1)S(1)}, bf16[4,256,256]{2,1,0:T(8,128)(2,1)S(1)}, u32[]{:S(2)}, u32[]{:S(2)}) collective-permute-start(bf16[4,256,256]{2,1,0:T(8,128)(2,1)S(1)} %pad_maximum_fusion.4.line_a), channel_id=1, source_target_pairs={{0,96},{1,25},{2,98},{3,27},{4,100},{5,29},{6,102},{7,31},{8,104},... | collective-permute-start | bytes 1572872 | tf_op jit(solution)/shard_map/items_down_b/ppermute | solution.py:336
  16.5 15.1 %collective-permute-start.3 = (bf16[4,256,256]{2,1,0:T(8,128)(2,1)S(1)}, bf16[4,256,256]{2,1,0:T(8,128)(2,1)}, u32[]{:S(2)}, u32[]{:S(2)}) collective-permute-start(bf16[4,256,256]{2,1,0:T(8,128)(2,1)S(1)} %pad_maximum_fusion.4.line_a), channel_id=1, source_target_pairs={{0,32},{1,9},{2,34},{3,11},{4,36},{5,13},{6,38},{7,15},{8,40},{9,1... | collective-permute-start | bytes 1572872 | tf_op jit(solution)/shard_map/items_up_a/ppermute | solution.py:336
  21.0 10.5 %collective-permute-start.1 = (bf16[1040,256]{1,0:T(8,128)(2,1)S(1)}, bf16[1040,256]{1,0:T(8,128)(2,1)S(1)}, u32[]{:S(2)}, u32[]{:S(2)}) collective-permute-start(bf16[1040,256]{1,0:T(8,128)(2,1)S(1)} %pad_maximum_fusion.3), channel_id=1, source_target_pairs={{0,2},{1,7},{2,4},{3,1},{4,6},{5,3},{6,0},{7,5},{8,10},{9,15},{10,... | collective-permute-start | bytes 1597448 | tf_op jit(solution)/shard_map/users_ring_2/ppermute | solution.py:319
  22.1 10.5 %copy-start.6 = (bf16[4,256,256]{2,1,0:T(8,128)(2,1)}, bf16[4,256,256]{2,1,0:T(8,128)(2,1)S(1)}, u32[]{:S(2)}) copy-start(bf16[4,256,256]{2,1,0:T(8,128)(2,1)S(1)} %constant_dynamic-update-slice_fusion.line_b) | copy-start | bytes 1572868
  22.1 10.5 %collective-permute-start.7 = (bf16[4,256,256]{2,1,0:T(8,128)(2,1)S(1)}, bf16[4,256,256]{2,1,0:T(8,128)(2,1)S(1)}, u32[]{:S(2)}, u32[]{:S(2)}) collective-permute-start(bf16[4,256,256]{2,1,0:T(8,128)(2,1)S(1)} %constant_dynamic-update-slice_fusion.line_b), channel_id=1, source_target_pairs={{0,32},{1,9},{2,34},{3,11},{4,36},{5,13},{6,38},{7,15},{8,40},{9,1... | collective-permute-start | bytes 1572872 | tf_op jit(solution)/shard_map/items_up_b/ppermute | solution.py:336
  24.0 9.3 %collective-permute-start.6 = (bf16[4,256,256]{2,1,0:T(8,128)(2,1)S(1)}, bf16[4,256,256]{2,1,0:T(8,128)(2,1)}, u32[]{:S(2)}, u32[]{:S(2)}) collective-permute-start(bf16[4,256,256]{2,1,0:T(8,128)(2,1)S(1)} %constant_dynamic-update-slice_fusion.line_b), channel_id=1, source_target_pairs={{0,96},{1,25},{2,98},{3,27},{4,100},{5,29},{6,102},{7,31},{8,104},... | collective-permute-start | bytes 1572872 | tf_op jit(solution)/shard_map/items_down_a/ppermute | solution.py:336
  34.0 0.8 copy-start.1
  36.1 5.0 %collective-permute-start.9 = (bf16[3104,256]{1,0:T(8,128)(2,1)}, bf16[3104,256]{1,0:T(8,128)(2,1)}, u32[]{:S(2)}, u32[]{:S(2)}) collective-permute-start(bf16[3104,256]{1,0:T(8,128)(2,1)} %pad_maximum_fusion), channel_id=1, source_target_pairs={{0,1},{1,0},{2,3},{3,2},{4,5},{5,4},{6,7},{7,6},{8,9},{9,8},{10,11... | collective-permute-start | bytes 4767752 | tf_op jit(solution)/shard_map/users_over/ppermute | solution.py:342
  36.3 10.7 %collective-permute-start.10 = (bf16[4,256,256]{2,1,0:T(8,128)(2,1)}, bf16[4,256,256]{2,1,0:T(8,128)(2,1)}, u32[]{:S(2)}, u32[]{:S(2)}) collective-permute-start(bf16[4,256,256]{2,1,0:T(8,128)(2,1)} %collective-permute-done.3.up_a), channel_id=1, source_target_pairs={{0,32},{1,9},{2,34},{3,11},{4,36},{5,13},{6,38},{7,15},{8,40},{9,1... | collective-permute-start | bytes 1572872 | tf_op jit(solution)/shard_map/items_up_2/ppermute | solution.py:336
  37.7 9.5 %collective-permute-start.11 = (bf16[4,256,256]{2,1,0:T(8,128)(2,1)}, bf16[4,256,256]{2,1,0:T(8,128)(2,1)}, u32[]{:S(2)}, u32[]{:S(2)}) collective-permute-start(bf16[4,256,256]{2,1,0:T(8,128)(2,1)} %collective-permute-done.6.down_a), channel_id=1, source_target_pairs={{0,96},{1,25},{2,98},{3,27},{4,100},{5,29},{6,102},{7,31},{8,104},... | collective-permute-start | bytes 1572872 | tf_op jit(solution)/shard_map/items_down_2/ppermute | solution.py:336
  41.1 1.0 copy-start.2
  42.1 5.0 %copy-start.3 = (bf16[4,256,256]{2,1,0:T(8,128)(2,1)S(1)}, bf16[4,256,256]{2,1,0:T(8,128)(2,1)}, u32[]{:S(2)}) copy-start(bf16[4,256,256]{2,1,0:T(8,128)(2,1)} %copy-done.1) | copy-start | bytes 1572868
  42.1 5.0 %copy-start.5 = (bf16[4,256,256]{2,1,0:T(8,128)(2,1)S(1)}, bf16[4,256,256]{2,1,0:T(8,128)(2,1)}, u32[]{:S(2)}) copy-start(bf16[4,256,256]{2,1,0:T(8,128)(2,1)} %copy-done.4) | copy-start | bytes 1572868
  42.1 5.0 %copy-start.7 = (bf16[4,256,256]{2,1,0:T(8,128)(2,1)S(1)}, bf16[4,256,256]{2,1,0:T(8,128)(2,1)}, u32[]{:S(2)}) copy-start(bf16[4,256,256]{2,1,0:T(8,128)(2,1)} %copy-done.6) | copy-start | bytes 1572868
  78.4 13.8 %collective-permute-start.12 = (bf16[20,256,256]{2,1,0:T(8,128)(2,1)}, bf16[20,256,256]{2,1,0:T(8,128)(2,1)S(1)}, u32[]{:S(2)}, u32[]{:S(2)}) collective-permute-start(bf16[20,256,256]{2,1,0:T(8,128)(2,1)} %get-tuple-element.15.give), channel_id=1, source_target_pairs={{0,1},{1,0},{2,3},{3,2},{4,5},{5,4},{6,7},{7,6},{8,9},{9,8},{10,11... | collective-permute-start | bytes 7864328 | tf_op jit(solution)/shard_map/give/ppermute | solution.py:342
  78.5 13.7 %collective-permute-start.18 = (bf16[4,256,256]{2,1,0:T(8,128)(2,1)S(1)}, bf16[4,256,256]{2,1,0:T(8,128)(2,1)S(1)}, u32[]{:S(2)}, u32[]{:S(2)}) collective-permute-start(bf16[4,256,256]{2,1,0:T(8,128)(2,1)S(1)} %get-tuple-element.21), channel_id=1, source_target_pairs={{0,96},{1,25},{2,98},{3,27},{4,100},{5,29},{6,102},{7,31},{8,104},... | collective-permute-start | bytes 1572872 | tf_op jit(solution)/shard_map/item_relay_down/ppermute | solution.py:336
  81.7 10.5 %collective-permute-start.23 = (bf16[4,256,256]{2,1,0:T(8,128)(2,1)S(1)}, bf16[4,256,256]{2,1,0:T(8,128)(2,1)S(1)}, u32[]{:S(2)}, u32[]{:S(2)}) collective-permute-start(bf16[4,256,256]{2,1,0:T(8,128)(2,1)S(1)} %get-tuple-element.26), channel_id=1, source_target_pairs={{0,32},{1,9},{2,34},{3,11},{4,36},{5,13},{6,38},{7,15},{8,40},{9,1... | collective-permute-start | bytes 1572872 | tf_op jit(solution)/shard_map/item_relay_up/ppermute | solution.py:336
  81.7 1.7 %collective-permute-start.19 = (f32[8,256]{1,0:T(8,128)S(1)}, f32[8,256]{1,0:T(8,128)S(1)}, u32[]{:S(2)}, u32[]{:S(2)}) collective-permute-start(f32[8,256]{1,0:T(8,128)S(1)} %get-tuple-element.22), channel_id=1, source_target_pairs={{0,1},{1,0},{2,3},{3,2},{4,5},{5,4},{6,7},{7,6},{8,9},{9,8},{10,11... | collective-permute-start | bytes 24584 | tf_op jit(solution)/shard_map/totals_0/ppermute | solution.py:325
  83.4 3.7 %collective-permute-start.20 = (f32[8,256]{1,0:T(8,128)S(1)}, f32[8,256]{1,0:T(8,128)S(1)}, u32[]{:S(2)}, u32[]{:S(2)}) collective-permute-start(f32[8,256]{1,0:T(8,128)S(1)} %add.128), channel_id=1, source_target_pairs={{0,2},{1,3},{2,0},{3,1},{4,6},{5,7},{6,4},{7,5},{8,10},{9,11},{10,... | collective-permute-start | bytes 24584 | tf_op jit(solution)/shard_map/totals_1/ppermute | solution.py:325
  87.0 5.2 %collective-permute-start.21 = (f32[8,256]{1,0:T(8,128)S(1)}, f32[8,256]{1,0:T(8,128)S(1)}, u32[]{:S(2)}, u32[]{:S(2)}) collective-permute-start(f32[8,256]{1,0:T(8,128)S(1)} %add.129), channel_id=1, source_target_pairs={{0,4},{1,5},{2,6},{3,7},{4,0},{5,1},{6,2},{7,3},{8,12},{9,13},{10,... | collective-permute-start | bytes 24584 | tf_op jit(solution)/shard_map/totals_2/ppermute | solution.py:325
  92.7 21.2 %collective-permute-start.24 = (bf16[8,256,256]{2,1,0:T(8,128)(2,1)S(1)}, bf16[8,256,256]{2,1,0:T(8,128)(2,1)S(1)}, u32[]{:S(2)}, u32[]{:S(2)}) collective-permute-start(bf16[8,256,256]{2,1,0:T(8,128)(2,1)S(1)} %pad_maximum_fusion.2), channel_id=1, source_target_pairs={{0,32},{1,9},{2,34},{3,11},{4,36},{5,13},{6,38},{7,15},{8,40},{9,1... | collective-permute-start | bytes 3145736 | tf_op jit(solution)/shard_map/item_up/ppermute | solution.py:336
  94.2 19.8 %collective-permute-start.22 = (bf16[8,256,256]{2,1,0:T(8,128)(2,1)S(1)}, bf16[8,256,256]{2,1,0:T(8,128)(2,1)S(1)}, u32[]{:S(2)}, u32[]{:S(2)}) collective-permute-start(bf16[8,256,256]{2,1,0:T(8,128)(2,1)S(1)} %pad_maximum_fusion.1), channel_id=1, source_target_pairs={{0,96},{1,25},{2,98},{3,27},{4,100},{5,29},{6,102},{7,31},{8,104},... | collective-permute-start | bytes 3145736 | tf_op jit(solution)/shard_map/item_down/ppermute | solution.py:336
  96.6 12.5 %collective-permute-start.13 = (bf16[4,256,256]{2,1,0:T(8,128)(2,1)S(1)}, bf16[4,256,256]{2,1,0:T(8,128)(2,1)S(1)}, u32[]{:S(2)}, u32[]{:S(2)}) collective-permute-start(bf16[4,256,256]{2,1,0:T(8,128)(2,1)S(1)} %get-tuple-element.32), channel_id=1, source_target_pairs={{0,2},{1,7},{2,4},{3,1},{4,6},{5,3},{6,0},{7,5},{8,10},{9,15},{10,... | collective-permute-start | bytes 1572872 | tf_op jit(solution)/shard_map/user_early/ppermute | solution.py:319
  98.8 14.1 %collective-permute-start.14 = (bf16[4,256,256]{2,1,0:T(8,128)(2,1)S(1)}, bf16[4,256,256]{2,1,0:T(8,128)(2,1)S(1)}, u32[]{:S(2)}, u32[]{:S(2)}) collective-permute-start(bf16[4,256,256]{2,1,0:T(8,128)(2,1)S(1)} %get-tuple-element.31), channel_id=1, source_target_pairs={{0,2},{1,7},{2,4},{3,1},{4,6},{5,3},{6,0},{7,5},{8,10},{9,15},{10,... | collective-permute-start | bytes 1572872 | tf_op jit(solution)/shard_map/user_relay/ppermute | solution.py:319
  100.1 3.8 %collective-permute-start.25 = (f32[8,256]{1,0:T(8,128)S(1)}, f32[8,256]{1,0:T(8,128)S(1)}, u32[]{:S(2)}, u32[]{:S(2)}) collective-permute-start(f32[8,256]{1,0:T(8,128)S(1)} %get-tuple-element.40), channel_id=1, source_target_pairs={{0,8},{1,9},{2,10},{3,11},{4,12},{5,13},{6,14},{7,15},{8,0},{9,1},... | collective-permute-start | bytes 24584 | tf_op jit(solution)/shard_map/totals_3/ppermute | solution.py:325
  103.9 5.2 %collective-permute-start.26 = (f32[8,256]{1,0:T(8,128)S(1)}, f32[8,256]{1,0:T(8,128)S(1)}, u32[]{:S(2)}, u32[]{:S(2)}) collective-permute-start(f32[8,256]{1,0:T(8,128)S(1)} %add.139), channel_id=1, source_target_pairs={{0,16},{1,17},{2,18},{3,19},{4,20},{5,21},{6,22},{7,23},{8,24},{9,... | collective-permute-start | bytes 24584 | tf_op jit(solution)/shard_map/totals_4/ppermute | solution.py:325
  109.1 11.0 %collective-permute-start.30 = (f32[8,256]{1,0:T(8,128)S(1)}, f32[8,256]{1,0:T(8,128)S(1)}, u32[]{:S(2)}, u32[]{:S(2)}) collective-permute-start(f32[8,256]{1,0:T(8,128)S(1)} %get-tuple-element.30), channel_id=1, source_target_pairs={{0,32},{1,33},{2,34},{3,35},{4,36},{5,37},{6,38},{7,39},{8,40},{9,... | collective-permute-start | bytes 24584 | tf_op jit(solution)/shard_map/totals_5/ppermute | solution.py:325
  113.1 12.1 %collective-permute-start.15 = (bf16[4,256,256]{2,1,0:T(8,128)(2,1)S(1)}, bf16[4,256,256]{2,1,0:T(8,128)(2,1)S(1)}, u32[]{:S(2)}, u32[]{:S(2)}) collective-permute-start(bf16[4,256,256]{2,1,0:T(8,128)(2,1)S(1)} %add_convert_fusion), channel_id=1, source_target_pairs={{0,2},{1,7},{2,4},{3,1},{4,6},{5,3},{6,0},{7,5},{8,10},{9,15},{10,... | collective-permute-start | bytes 1572872 | tf_op jit(solution)/shard_map/user_late/ppermute | solution.py:319
  114.6 13.9 %copy-start = (bf16[20,256,256]{2,1,0:T(8,128)(2,1)S(1)}, bf16[20,256,256]{2,1,0:T(8,128)(2,1)}, u32[]{:S(2)}) copy-start(bf16[20,256,256]{2,1,0:T(8,128)(2,1)} %get-tuple-element.15.give) | copy-start | bytes 7864324
  114.7 12.9 %collective-permute-start.29 = (bf16[2,256,256]{2,1,0:T(8,128)(2,1)S(1)}, bf16[2,256,256]{2,1,0:T(8,128)(2,1)S(1)}, u32[]{:S(2)}, u32[]{:S(2)}) collective-permute-start(bf16[2,256,256]{2,1,0:T(8,128)(2,1)S(1)} %bitcast.49), channel_id=1, source_target_pairs={{0,8},{1,33},{2,10},{3,35},{4,12},{5,37},{6,14},{7,39},{8,16},{9,4... | collective-permute-start | bytes 786440 | tf_op jit(solution)/shard_map/item_back/ppermute | solution.py:330
  115.7 11.9 %collective-permute-start.27 = (bf16[2,256,256]{2,1,0:T(8,128)(2,1)S(1)}, bf16[2,256,256]{2,1,0:T(8,128)(2,1)S(1)}, u32[]{:S(2)}, u32[]{:S(2)}) collective-permute-start(bf16[2,256,256]{2,1,0:T(8,128)(2,1)S(1)} %bitcast.48), channel_id=1, source_target_pairs={{0,24},{1,97},{2,26},{3,99},{4,28},{5,101},{6,30},{7,103},{8,0},{9... | collective-permute-start | bytes 786440 | tf_op jit(solution)/shard_map/item_back/ppermute | solution.py:330
  118.0 9.6 %collective-permute-start.28 = (bf16[2,256,256]{2,1,0:T(8,128)(2,1)S(1)}, bf16[2,256,256]{2,1,0:T(8,128)(2,1)S(1)}, u32[]{:S(2)}, u32[]{:S(2)}) collective-permute-start(bf16[2,256,256]{2,1,0:T(8,128)(2,1)S(1)} %bitcast.47), channel_id=1, source_target_pairs={{0,16},{1,65},{2,18},{3,67},{4,20},{5,69},{6,22},{7,71},{8,24},{9,... | collective-permute-start | bytes 786440 | tf_op jit(solution)/shard_map/item_back/ppermute | solution.py:330
  120.1 5.2 %collective-permute-start.31 = (f32[8,256]{1,0:T(8,128)S(1)}, f32[8,256]{1,0:T(8,128)S(1)}, u32[]{:S(2)}, u32[]{:S(2)}) collective-permute-start(f32[8,256]{1,0:T(8,128)S(1)} %add.146), channel_id=1, source_target_pairs={{0,64},{1,65},{2,66},{3,67},{4,68},{5,69},{6,70},{7,71},{8,72},{9,... | collective-permute-start | bytes 24584 | tf_op jit(solution)/shard_map/totals_6/ppermute | solution.py:325
  125.2 3.2 %collective-permute-start.16 = (bf16[4,256,256]{2,1,0:T(8,128)(2,1)S(1)}, bf16[4,256,256]{2,1,0:T(8,128)(2,1)S(1)}, u32[]{:S(2)}, u32[]{:S(2)}) collective-permute-start(bf16[4,256,256]{2,1,0:T(8,128)(2,1)S(1)} %collective-permute-done.13.early), channel_id=1, source_target_pairs={{0,1},{1,0},{2,3},{3,2},{4,5},{5,4},{6,7},{7,6},{8,9},{9,8},{10,11... | collective-permute-start | bytes 1572872 | tf_op jit(solution)/shard_map/early_over/ppermute | solution.py:342
  125.2 3.2 %collective-permute-start.17 = (bf16[4,256,256]{2,1,0:T(8,128)(2,1)S(1)}, bf16[4,256,256]{2,1,0:T(8,128)(2,1)S(1)}, u32[]{:S(2)}, u32[]{:S(2)}) collective-permute-start(bf16[4,256,256]{2,1,0:T(8,128)(2,1)S(1)} %collective-permute-done.15.late), channel_id=1, source_target_pairs={{0,1},{1,0},{2,3},{3,2},{4,5},{5,4},{6,7},{7,6},{8,9},{9,8},{10,11... | collective-permute-start | bytes 1572872 | tf_op jit(solution)/shard_map/late_over/ppermute | solution.py:342
